TPU v7x, 32 devices: a whole 2x2x4 slice. The times are simulated.
32 devices in a mesh: snap: 2 (over x), blk: 16 (over z, y, core).
Axes of the slice: x: 2, y: 2, z: 4, core: 2. Of those that a mesh axis runs over, the one named last changes fastest.
Arguments:
- coeffs: bfloat16 [2, 3072, 12544], P(None, ('snap', 'blk')), parts along dimension 1, may hold values from -6 to 6
- k_plus_g: float32 [6, 12544], P('snap'), parts along dimension 0, may hold values from -2 to 2
- pairs: int32 [32, 2], P(('snap', 'blk')), parts along dimension 0, may hold values from 0 to 1, as said below
- levels: int32 [3072], P(('snap', 'blk')), parts along dimension 0, may hold values from 0 to 16
Outputs:
- velocity: float32 [3, 2, 3072, 480], P(None, None, ('snap', 'blk')), parts along dimension 2
There are 2 independent parts, one for each index of `snap`. A program takes and returns all parts, laid end to end along the dimension named above; each array names one. Nothing has to cross between parts.
Inputs may be any that keep to these rules, and one draw needn't show every extreme that they name: In each row of pairs the ones come first; pairs[i, d-1] is 0 where i + d >= 16; row 0 holds 2 ones.
All inputs are finite; a program needn't handle non-finite values.
Results may differ from a plain program's by a relative error of at most 0.0029.
Values may be sent and summed in bfloat16 or wider, within the bound.
No kernel may reach another device: no remote copies, remote signals or barrier semaphores. Data moves between devices by JAX's collectives and lax.ppermute only.
A program may use at most 64 MiB of HBM per device.

v0:
```python
import math

import jax
import jax.numpy as jnp
from jax import lax
from jax.sharding import PartitionSpec as P

REACH = 2
OCC_STEPS = 16
SPAN = 5


def shifted(block, axis, distance):
    devices = range(lax.axis_size(axis))
    route = [(i - distance, i) for i in devices if i - distance in devices]
    return lax.ppermute(block, axis, route)


def pair_tile(weighted, partner):
    prod = jnp.einsum("acnp,dmp->acdnm", weighted, partner, preferred_element_type=jnp.float32)
    return jnp.stack([prod[:, 0, 0] + prod[:, 1, 1], prod[:, 0, 1] - prod[:, 1, 0]], axis=1)


def mirror(tile):
    return jnp.stack([-jnp.swapaxes(tile[:, 0], 1, 2), jnp.swapaxes(tile[:, 1], 1, 2)], axis=1)


def shards(coeffs, k_plus_g, pairs, levels):
    plane = coeffs.shape[2]
    scale = 1.0 / math.sqrt(plane)
    occup = levels.astype(jnp.float32) / OCC_STEPS
    occ_wire = occup.astype(jnp.bfloat16)
    weighted = (k_plus_g[:, None, None, :] * coeffs[None]).astype(jnp.bfloat16)

    def settle(left_weighted, right_block, occ_left, occ_right, flag):
        weights = (occ_left[:, None] - occ_right[None, :]) * (flag * scale)
        return pair_tile(left_weighted, right_block) * weights

    slots = [None] * SPAN
    slots[REACH] = settle(weighted, coeffs, occup, occup, jnp.float32(1.0))
    moving = (coeffs, occ_wire)
    for step in range(1, REACH + 1):
        moving = shifted((moving[0], moving[1]), "blk", -1)
        slots[REACH + step] = settle(
            weighted,
            moving[0],
            occup,
            moving[1].astype(jnp.float32),
            pairs[0, step - 1].astype(jnp.float32),
        )
    for step in range(1, REACH + 1):
        arrived = shifted(slots[REACH + step], "blk", step)
        slots[REACH - step] = mirror(arrived)
    stacked = jnp.stack(slots, axis=3)
    return stacked.reshape(3, 2, occup.shape[0], SPAN * occup.shape[0])


def solution(mesh):
    in_specs = (
        P(None, ("snap", "blk"), None),
        P("snap", None),
        P(("snap", "blk"), None),
        P(("snap", "blk")),
    )
    out_specs = P(None, None, ("snap", "blk"), None)
    return jax.shard_map(shards, mesh=mesh, in_specs=in_specs, out_specs=out_specs, check_vma=False)
```

profile of v0, /device:TPU:0, one launch (start us, length us, event | category | flops | bytes accessed | tf_op | source)
XLA Modules:
  0.0 158.4 jit_solution(13948620120202407646)
XLA Ops:
  0.0 1.3 collective-permute-start
  1.3 9.0 %collective-permute-done = bf16[2,96,12544]{2,1,0:T(8,128)(2,1)} collective-permute-done((bf16[2,96,12544]{2,1,0:T(8,128)(2,1)}, bf16[2,96,12544]{2,1,0:T(8,128)(2,1)}, u32[]{:S(2)}, u32[]{:S(2)}) %collective-permute-start) | collective-permute-done | bytes 4816928 | tf_op jit(solution)/shard_map/ppermute | solution.py:16
  10.3 1.3 collective-permute-start.1
  11.6 0.7 convert_multiply_fusion
  12.2 0.0 copy-start.1
  12.2 0.0 copy-start
  12.2 1.4 collective-permute-start.2
  13.7 6.7 %convert_element_type.27 = f32[2,96,12544]{2,1,0:T(8,128)} convert(bf16[2,96,12544]{2,1,0:T(8,128)(2,1)} %param.4) | non-fusion elementwise | flops 2408448 | bytes 14450688 | tf_op jit(solution)/shard_map/convert_element_type | solution.py:33
  20.4 0.0 copy-done.1
  20.4 0.6 fusion.43
  21.0 0.0 copy-done
  21.0 9.0 %fusion.18 = f32[3,2,2,96,96]{4,3,0,2,1:T(8,128)S(1)} fusion(bf16[2,96,12544]{2,1,0:T(8,128)(2,1)} %param.4, f32[2,96,12544]{2,1,0:T(8,128)} %convert_element_type.27, f32[3,12544]{1,0:T(4,128)S(1)} %copy-done), kind=kOutput, calls=%fused_computation.14 | convolution fusion | flops 2788982784 | bytes 15043584 | tf_op jit(solution)/shard_map/acnp,dmp->acdnm/dot_general | solution.py:20
  31.4 36.1 %collective-permute-done.2 = bf16[96]{0:T(256)(128)(2,1)S(1)} collective-permute-done((bf16[96]{0:T(256)(128)(2,1)S(1)}, bf16[96]{0:T(256)(128)(2,1)S(1)}, u32[]{:S(2)}, u32[]{:S(2)}) %collective-permute-start.2) | collective-permute-done | bytes 224 | tf_op jit(solution)/shard_map/ppermute | solution.py:16
  67.5 1.3 collective-permute-start.3
  68.8 48.6 %collective-permute-done.3 = bf16[96]{0:T(256)(128)(2,1)S(1)} collective-permute-done((bf16[96]{0:T(256)(128)(2,1)S(1)}, bf16[96]{0:T(256)(128)(2,1)S(1)}, u32[]{:S(2)}, u32[]{:S(2)}) %collective-permute-start.3) | collective-permute-done | bytes 224 | tf_op jit(solution)/shard_map/ppermute | solution.py:16
  117.5 0.1 subtract_multiply_fusion
  117.5 0.1 copy.15
  117.6 9.0 %fusion.13 = f32[3,2,2,96,96]{4,3,0,2,1:T(8,128)S(1)} fusion(bf16[2,96,12544]{2,1,0:T(8,128)(2,1)} %collective-permute-done, f32[2,96,12544]{2,1,0:T(8,128)} %convert_element_type.27, f32[3,12544]{1,0:T(4,128)S(1)} %copy-done), kind=kOutput, calls=%fused_computation.13 | convolution fusion | flops 2788982784 | bytes 15043584 | tf_op jit(solution)/shard_map/acnp,dmp->acdnm/dot_general | solution.py:20
  126.7 4.3 %collective-permute-start.5 = (f32[3,2,96,96]{3,2,0,1:T(8,128)S(1)}, f32[3,2,96,96]{3,2,0,1:T(8,128)S(1)}, u32[]{:S(2)}, u32[]{:S(2)}) collective-permute-start(f32[3,2,96,96]{3,2,0,1:T(8,128)S(1)} %maximum_multiply_fusion.1), channel_id=1, source_target_pairs={{0,1},{1,2},{2,3},{3,4},{4,5},{5,6},{6,7},{7,8},{8,9},{9,10},{10,1... | collective-permute-start | bytes 663560 | tf_op jit(solution)/shard_map/ppermute | solution.py:16
  131.0 0.0 collective-permute-done.1
  131.0 12.3 %fusion.23 = f32[3,2,2,96,96]{4,3,2,1,0:T(8,128)S(1)} fusion(bf16[2,96,12544]{2,1,0:T(8,128)(2,1)} %collective-permute-done.1, f32[2,96,12544]{2,1,0:T(8,128)} %convert_element_type.27, f32[3,12544]{1,0:T(4,128)S(1)} %copy-done), kind=kOutput, calls=%fused_computation.15 | convolution fusion | flops 2788982784 | bytes 15043584 | tf_op jit(solution)/shard_map/acnp,dmp->acdnm/dot_general | solution.py:20
  143.4 0.1 copy.29
  143.5 0.1 copy.30
  143.6 0.1 copy.14
  143.8 6.0 %collective-permute-start.4 = (f32[3,2,96,96]{2,3,0,1:T(8,128)S(1)}, f32[3,2,96,96]{2,3,0,1:T(8,128)S(1)}, u32[]{:S(2)}, u32[]{:S(2)}) collective-permute-start(f32[3,2,96,96]{2,3,0,1:T(8,128)S(1)} %maximum_multiply_fusion), channel_id=1, source_target_pairs={{0,2},{1,3},{2,4},{3,5},{4,6},{5,7},{6,8},{7,9},{8,10},{9,11},{10,... | collective-permute-start | bytes 663560 | tf_op jit(solution)/shard_map/ppermute | solution.py:16
  149.8 0.0 collective-permute-done.5
  149.9 0.1 copy.19
  150.1 0.1 copy.18
  150.2 6.1 %collective-permute-done.4 = f32[3,2,96,96]{2,3,0,1:T(8,128)S(1)} collective-permute-done((f32[3,2,96,96]{2,3,0,1:T(8,128)S(1)}, f32[3,2,96,96]{2,3,0,1:T(8,128)S(1)}, u32[]{:S(2)}, u32[]{:S(2)}) %collective-permute-start.4) | collective-permute-done | bytes 221216 | tf_op jit(solution)/shard_map/ppermute | solution.py:16
  156.5 0.4 copy.20
  157.0 1.5 copy.21
  (16 shorter events, 0.4 us)
Async XLA Ops:
  0.0 10.3 %collective-permute-start = (bf16[2,96,12544]{2,1,0:T(8,128)(2,1)}, bf16[2,96,12544]{2,1,0:T(8,128)(2,1)}, u32[]{:S(2)}, u32[]{:S(2)}) collective-permute-start(bf16[2,96,12544]{2,1,0:T(8,128)(2,1)} %param.4), channel_id=1, source_target_pairs={{1,0},{2,1},{3,2},{4,3},{5,4},{6,5},{7,6},{8,7},{9,8},{10,9},{11,1... | collective-permute-start | bytes 14450696 | tf_op jit(solution)/shard_map/ppermute | solution.py:16
  10.3 120.7 %collective-permute-start.1 = (bf16[2,96,12544]{2,1,0:T(8,128)(2,1)}, bf16[2,96,12544]{2,1,0:T(8,128)(2,1)}, u32[]{:S(2)}, u32[]{:S(2)}) collective-permute-start(bf16[2,96,12544]{2,1,0:T(8,128)(2,1)} %collective-permute-done), channel_id=1, source_target_pairs={{1,0},{2,1},{3,2},{4,3},{5,4},{6,5},{7,6},{8,7},{9,8},{10,9},{11,1... | collective-permute-start | bytes 14450696 | tf_op jit(solution)/shard_map/ppermute | solution.py:16
  12.2 8.1 %copy-start.1 = (s32[1,2]{1,0:T(1,128)S(1)}, s32[1,2]{1,0:T(1,128)}, u32[]{:S(2)}) copy-start(s32[1,2]{1,0:T(1,128)} %param.6) | copy-start | bytes 28
  12.2 8.8 %copy-start = (f32[3,12544]{1,0:T(4,128)S(1)}, f32[3,12544]{1,0:T(4,128)}, u32[]{:S(2)}) copy-start(f32[3,12544]{1,0:T(4,128)} %param.5) | copy-start | bytes 451588
  12.2 55.3 %collective-permute-start.2 = (bf16[96]{0:T(256)(128)(2,1)S(1)}, bf16[96]{0:T(256)(128)(2,1)S(1)}, u32[]{:S(2)}, u32[]{:S(2)}) collective-permute-start(bf16[96]{0:T(256)(128)(2,1)S(1)} %get-tuple-element.27), channel_id=1, source_target_pairs={{1,0},{2,1},{3,2},{4,3},{5,4},{6,5},{7,6},{8,7},{9,8},{10,9},{11,1... | collective-permute-start | bytes 584 | tf_op jit(solution)/shard_map/ppermute | solution.py:16
  67.5 49.9 %collective-permute-start.3 = (bf16[96]{0:T(256)(128)(2,1)S(1)}, bf16[96]{0:T(256)(128)(2,1)S(1)}, u32[]{:S(2)}, u32[]{:S(2)}) collective-permute-start(bf16[96]{0:T(256)(128)(2,1)S(1)} %collective-permute-done.2), channel_id=1, source_target_pairs={{1,0},{2,1},{3,2},{4,3},{5,4},{6,5},{7,6},{8,7},{9,8},{10,9},{11,1... | collective-permute-start | bytes 584 | tf_op jit(solution)/shard_map/ppermute | solution.py:16
  126.7 23.1 %collective-permute-start.5 = (f32[3,2,96,96]{3,2,0,1:T(8,128)S(1)}, f32[3,2,96,96]{3,2,0,1:T(8,128)S(1)}, u32[]{:S(2)}, u32[]{:S(2)}) collective-permute-start(f32[3,2,96,96]{3,2,0,1:T(8,128)S(1)} %maximum_multiply_fusion.1), channel_id=1, source_target_pairs={{0,1},{1,2},{2,3},{3,4},{4,5},{5,6},{6,7},{7,8},{8,9},{9,10},{10,1... | collective-permute-start | bytes 663560 | tf_op jit(solution)/shard_map/ppermute | solution.py:16
  143.8 12.5 %collective-permute-start.4 = (f32[3,2,96,96]{2,3,0,1:T(8,128)S(1)}, f32[3,2,96,96]{2,3,0,1:T(8,128)S(1)}, u32[]{:S(2)}, u32[]{:S(2)}) collective-permute-start(f32[3,2,96,96]{2,3,0,1:T(8,128)S(1)} %maximum_multiply_fusion), channel_id=1, source_target_pairs={{0,2},{1,3},{2,4},{3,5},{4,6},{5,7},{6,8},{7,9},{8,10},{9,11},{10,... | collective-permute-start | bytes 663560 | tf_op jit(solution)/shard_map/ppermute | solution.py:16
where the time goes:
time: 159 us; the launch traced here: 158 us
  waiting for transfers between devices  99.9 us (63%)
  matrix products  30.3 us (19%)
  starting transfers between devices  15.6 us (10%)
  other arithmetic  7.83 us (5%)
  local copies, waits for them, and re-layouts  3.26 us (2%)
    ppermute x6, waiting for transfers between devices, shifted(): return lax.ppermute(block, axis, route)  99.9 us
    dot_general x3, matrix products, pair_tile(): jnp.einsum('acnp,dmp->acdnm', weighted, partner, preferred_element_type=j...  30.3 us
    ppermute x6, starting transfers between devices, shifted(): return lax.ppermute(block, axis, route)  15.6 us
    convert_element_type x1, other arithmetic, shards(): weighted = (k_plus_g[:, None, None, :] * coeffs[None]).astype(jnp.bfloat16)  6.71 us
  transfers between devices with their start and end apart: 6, of which 4 were waited for; matrix products, arithmetic and copies ran while one was open for 25% of the time, Pallas kernels for 0%

commit v1 on v0

v1 whole, which is shorter than its diff:
```python
import functools
import math

import jax
import jax.numpy as jnp
from jax import lax
from jax.experimental import pallas as pl
from jax.experimental.pallas import tpu as pltpu
from jax.sharding import PartitionSpec as P

REACH = 2
OCC_STEPS = 16
SPAN = 5
LANES = 128
SECOND = (28, 14, 7)
PIECE = 7
F32 = jnp.float32
BF16 = jnp.bfloat16
VMEM_BYTES = 62 * 2**20


def product(k, low, high):
    wide = low.astype(F32)
    rows = jnp.concatenate([(k[a][None, :] * wide[c]).astype(BF16) for c in range(2) for a in range(3)], axis=0)
    cols = jnp.concatenate([high[0], high[1]], axis=0)
    return lax.dot_general(rows, cols, (((1,), (1,)), ((), ())), preferred_element_type=F32)


def combine(acc):
    rows, bands = acc.shape[0] // 2, acc.shape[1] // 2
    up, down = acc[:rows], acc[rows:]
    return jnp.concatenate([up[:, :bands] + down[:, bands:], up[:, bands:] - down[:, :bands]], axis=1)


def weights_of(low, high, offset, scale):
    bands = low.shape[1]
    low, high = low.astype(F32), high.astype(F32)
    flag = low[1, 0:1, bands + offset - 1 : bands + offset] if offset else 1.0
    weights = (low[0][:, :bands] - high[1][:, :bands]) * (flag * scale)
    weights = jnp.concatenate([weights] * 3, axis=0)
    return jnp.concatenate([weights, weights], axis=1)


def pack(tile):
    rows = tile.shape[0]
    rest = tile[:, LANES:]
    return jnp.concatenate([tile[:, :LANES], jnp.concatenate([rest[: rows // 2], rest[rows // 2 :]], axis=1)], axis=0)


def unpack(packed):
    rows = packed.shape[0] * 2 // 3
    rest = packed[rows:]
    width = LANES // 2
    return jnp.concatenate([packed[:rows], jnp.concatenate([rest[:, :width], rest[:, width:]], axis=0)], axis=1)


def roles(kind, info):
    early, side, core = info[0], info[1], info[2]
    if kind == "diag":
        return 1, 0, (0,)
    if kind == "near":
        return 1, core, (1 - core,)
    if kind == "early":
        return early, side, (1 - side, 1 - side, side)
    return 1 - early, side, (1 - side, side, side)


OFFSETS = {"diag": (0,), "near": (1,), "early": (2, 1, 2), "late": (2, 1, 2)}


def pair_body(kind, has_start, steps, step, begin, ends, scale, info, k_ref, x_ref, *refs):
    offsets = OFFSETS[kind]
    count = len(offsets)
    active, half, others = roles(kind, info)
    q_refs, refs = refs[:count], refs[count:]
    if ends:
        facts_x, facts_q, refs = refs[0], refs[1 : 1 + count], refs[1 + count :]
    if has_start:
        start, refs = refs[0], refs[1:]
    outs, acc = refs[:-1], refs[-1]
    at = pl.program_id(0)

    def each(run):
        for i in range(count):
            if offsets[i] == 0:
                run(i, x_ref, x_ref, *([facts_x] * 2 if ends else [None] * 2))
                continue
            facts = (facts_q[i], facts_x) if ends else (None, None)
            pl.when(others[i] == 1)(lambda: run(i, q_refs[i], x_ref, facts[0], facts[1]))
            pl.when(others[i] == 0)(lambda: run(i, x_ref, q_refs[i], facts[1], facts[0]))

    @pl.when(active == 1)
    def _():
        first = half * (k_ref.shape[1] // 2 // LANES) + begin + at * step
        k = k_ref[:, pl.ds(pl.multiple_of(first * LANES, LANES), step * LANES)]

        def add(i, low, high, facts_low, facts_high):
            part = product(k, low[...], high[...])

            @pl.when(at == 0)
            def _():
                acc[i] = part

            @pl.when(at > 0)
            def _():
                acc[i] += part

        each(add)

        @pl.when(at == steps - 1)
        def _():
            if not ends:
                for i in range(count):
                    tile = combine(acc[i])
                    outs[0][i] = tile + start[i] if has_start else tile
                return

            def end(i, low, high, facts_low, facts_high):
                tile = combine(acc[i])
                if has_start:
                    tile = tile + start[i]
                tile = tile * weights_of(facts_low[...], facts_high[...], offsets[i], scale)
                if i == 0:
                    outs[0][...] = tile
                if len(outs) > 1:
                    outs[1][i] = pack(tile).astype(BF16)

            each(end)

    if not isinstance(active, int):
        @pl.when((active == 0) & (at == 0))
        def _():
            for out in outs:
                out[...] = jnp.zeros_like(out)


def pair_sums(kind, info, k, x, partners, begin, start, steps, step, facts):
    width = step * LANES
    bands = x[0].shape[1]
    count = len(partners)
    ends = facts is not None
    shape = (count, 3 * bands, 2 * bands)

    def block(at):
        return pl.BlockSpec((2, bands, width), lambda j, info: (0, 0, at + j * roles(kind, info)[0]))

    whole = lambda shape: pl.BlockSpec(shape, lambda j, info: (0,) * len(shape))
    in_specs = [whole(k.shape), block(x[1])] + [block(at) for _, at in partners]
    operands = [k, x[0]] + [q for q, _ in partners]
    if ends:
        in_specs += [pl.BlockSpec((2, bands, LANES), lambda j, info, at=at: (0, 0, at)) for _, at in facts]
        operands += [array for array, _ in facts]
    if start is not None:
        in_specs.append(whole(shape))
        operands.append(start)
    if ends:
        out_shape = [jax.ShapeDtypeStruct(shape[1:], F32)]
        if kind != "diag":
            out_shape.append(jax.ShapeDtypeStruct((count, 9 * bands // 2, LANES), BF16))
    else:
        out_shape = [jax.ShapeDtypeStruct(shape, F32)]
    return pl.pallas_call(
        functools.partial(pair_body, kind, start is not None, steps, step, begin, ends, 1.0 / math.sqrt(k.shape[1])),
        grid_spec=pltpu.PrefetchScalarGridSpec(
            num_scalar_prefetch=1,
            grid=(steps,),
            in_specs=in_specs,
            out_specs=[whole(s.shape) for s in out_shape],
            scratch_shapes=[pltpu.VMEM((count, 6 * bands, 2 * bands), F32)],
        ),
        out_shape=out_shape,
        compiler_params=pltpu.CompilerParams(vmem_limit_bytes=VMEM_BYTES),
        cost_estimate=pl.CostEstimate(flops=1000, bytes_accessed=1000, transcendentals=0),
        name=kind,
    )(info, *operands)


def halves_body(which, cuts, with_facts, info, levels, pairs, coeffs, *refs):
    outs, held, sems = refs[: len(cuts)], refs[-2], refs[-1]
    bands = coeffs.shape[1]
    half = coeffs.shape[2] // 2
    count = half // (PIECE * LANES)
    base = half * (info[2] if which == 0 else 1 - info[2])
    span = lambda start, size: pl.ds(start * LANES, size * LANES)
    loads = []
    for i in range(count):
        source = pl.ds(pl.multiple_of(base + i * PIECE * LANES, LANES), PIECE * LANES)
        loads.append(pltpu.make_async_copy(coeffs.at[:, :, source], held.at[:, :, span(i * PIECE, PIECE)], sems.at[0, i]))
        loads[-1].start()
    occup = levels[...].astype(F32) / OCC_STEPS
    spread = jnp.broadcast_to(occup, (bands, bands))
    lane = lax.broadcasted_iota(jnp.int32, (bands, LANES - bands), 1)
    flags = jnp.zeros((bands, LANES - bands), F32)
    for d in range(REACH):
        flags = jnp.where(lane == d, pairs[0, d].astype(F32), flags)
    last = span(count * PIECE, 1)
    held[0, :, last] = jnp.concatenate([spread.T, jnp.zeros_like(flags)], axis=1).astype(BF16)
    held[1, :, last] = jnp.concatenate([spread, flags], axis=1).astype(BF16)
    stores = []

    def store(out, i, start, at, size):
        copy = pltpu.make_async_copy(held.at[:, :, span(start, size)], outs[out].at[:, :, span(at, size)], sems.at[1 + out, i])
        copy.start()
        stores.append(copy)

    for out, (start, size) in enumerate(cuts):
        if with_facts[out]:
            store(out, count, count * PIECE, size, 1)
    for i in range(count):
        loads[i].wait()
        for out, (start, size) in enumerate(cuts):
            if start <= i * PIECE < start + size:
                store(out, i, i * PIECE, i * PIECE - start, PIECE)
    for copy in stores:
        copy.wait()


def halves(which, cuts, with_facts, info, levels, pairs, coeffs, name):
    bands = coeffs.shape[1]
    anywhere = pl.BlockSpec(memory_space=pl.ANY)
    return pl.pallas_call(
        functools.partial(halves_body, which, cuts, with_facts),
        in_specs=[
            pl.BlockSpec(memory_space=pltpu.SMEM),
            pl.BlockSpec(memory_space=pltpu.VMEM),
            pl.BlockSpec(memory_space=pltpu.SMEM),
            anywhere,
        ],
        out_specs=[anywhere] * len(cuts),
        out_shape=[
            jax.ShapeDtypeStruct((2, bands, (size + int(more)) * LANES), BF16) for (_, size), more in zip(cuts, with_facts)
        ],
        scratch_shapes=[
            pltpu.VMEM((2, bands, coeffs.shape[2] // 2 + LANES), BF16),
            pltpu.SemaphoreType.DMA((1 + len(cuts), coeffs.shape[2] // 2 // LANES // PIECE + 1)),
        ],
        compiler_params=pltpu.CompilerParams(vmem_limit_bytes=VMEM_BYTES),
        cost_estimate=pl.CostEstimate(flops=1000, bytes_accessed=1000, transcendentals=0),
        name=name,
    )(info, levels[None, :], pairs, coeffs)


def final_body(info, diag, own, core, early, late, side, up_y, down_y, up_z, down_z, cross, out):
    bands = out.shape[2]
    first = info[0] == 1
    low = info[1] == 0
    wide = lambda ref: unpack(ref[...].astype(F32))
    received = [unpack(up_y[i].astype(F32) + down_y[i].astype(F32)) for i in range(3)]
    far = unpack(up_z[...].astype(F32) + down_z[...].astype(F32))
    mine = own[...] + unpack(core[0].astype(F32))
    near1 = jnp.where(first, mine, received[1] + unpack(side[1].astype(F32)))
    near2 = early[...] + late[...] + received[0]
    away1 = jnp.where(first, received[1] + wide(cross), mine)
    away2 = received[2] + far
    above = [jnp.where(low, near1, away1), jnp.where(low, near2, away2)]
    below = [jnp.where(low, away1, near1), jnp.where(low, away2, near2)]
    for a in range(3):
        for part in range(2):
            cut = lambda tile: tile[a * bands : (a + 1) * bands, part * bands : (part + 1) * bands]
            turn = lambda tile: -cut(tile).T if part == 0 else cut(tile).T
            out[a, part] = jnp.concatenate([turn(below[1]), turn(below[0]), cut(diag), cut(above[0]), cut(above[1])], axis=1)


def final(info, bands, *operands):
    vmem = pl.BlockSpec(memory_space=pltpu.VMEM)
    return pl.pallas_call(
        final_body,
        in_specs=[pl.BlockSpec(memory_space=pltpu.SMEM)] + [vmem] * len(operands),
        out_specs=vmem,
        out_shape=jax.ShapeDtypeStruct((3, 2, bands, SPAN * bands), F32),
        compiler_params=pltpu.CompilerParams(vmem_limit_bytes=VMEM_BYTES),
        name="final",
    )(info, *operands)


def routes(groups):
    quads = range(groups // 4)
    at = lambda q, side, core: 4 * q + 2 * side + core
    early = lambda q, side: at(q, side, side)
    late = lambda q, side: at(q, side, 1 - side)
    away = lambda q, side: q + 1 - 2 * side
    both = [(q, side) for q in quads for side in (0, 1)]
    other = [(at(q, s, c), at(q, s, 1 - c)) for q, s in both for c in (0, 1)]
    y_early = [(late(q, 1 - s), early(q, s)) for q, s in both]
    y_late = [(early(q, 1 - s), late(q, s)) for q, s in both]
    ok = [(q, s) for q, s in both if 0 <= away(q, s) < groups // 4]
    z_early = [(early(away(q, s), s), early(q, s)) for q, s in ok]
    z_late = [(late(away(q, s), s), late(q, s)) for q, s in ok]
    forward = [(early(q, s), late(q, s)) for q, s in both]
    turn = lambda route: [(b, a) for a, b in route]
    cross = [(late(q, s), early(away(q, s), s)) for q, s in ok]
    return dict(
        other=other, y_early=y_early, y_late=y_late, z_early=z_early, z_late=z_late, forward=forward,
        tile_y_early=turn(y_early), tile_y_late=turn(y_late), tile_z_early=turn(z_early), tile_z_late=turn(z_late), cross=cross,
    )


def after(value, *first):
    return lax.optimization_barrier((value, *first))[0]


def shards(coeffs, k_plus_g, pairs, levels):
    groups = lax.axis_size("blk")
    me = lax.axis_index("blk")
    bands, plane = coeffs.shape[1:]
    tiles = plane // 2 // LANES
    core = me % 2
    side = (me // 2) % 2
    info = jnp.stack([(core == side).astype(jnp.int32), side, core])
    way = routes(groups)
    send = lambda value, name: lax.ppermute(value, "blk", way[name])

    (first,) = halves(0, [(0, tiles)], [True], info, levels, pairs, coeffs, "first")
    y_first, z_first = send(first, "y_early"), send(first, "z_early")
    begins = [sum(SECOND[:i]) for i in range(len(SECOND))]
    swap, *second = halves(
        1, [(0, tiles)] + list(zip(begins, SECOND)), [True, True] + [False] * (len(SECOND) - 1), info, levels, pairs,
        after(coeffs, first), "second",
    )
    swapped = send(swap, "other")

    here, facts_y, facts_core, facts_z = (first, tiles), (y_first, tiles), (swapped, tiles), (z_first, tiles)
    (diag,) = pair_sums("diag", info, k_plus_g, (after(coeffs, swap), 0), [(coeffs, 0)], 0, None, 7, 14, [here, here])
    own, own_packed = pair_sums(
        "near", info, k_plus_g, (swapped, 0), [(after(first, diag), 0)], 0, None, 7, 7, [facts_core, here]
    )
    tile_core = send(own_packed, "other")

    y_second, z_second = [], []

    def send_second(block, *first):
        block = after(block, *first)
        y_second.append(send(block, "y_late"))
        z_second.append(send(block, "z_late"))

    send_second(second[0], own)
    forward = send(after(z_first, own), "forward")
    send_second(second[1], own, y_first, z_first)
    early_tile, early_tiles = pair_sums(
        "early", info, k_plus_g, (y_first, 0), [(after(first, own), 0), (swapped, 0), (z_first, 0)], 0, None, 7, 7,
        [facts_y, here, facts_core, facts_z],
    )
    tile_y_early = send(early_tiles, "tile_y_early")
    tile_side = send(early_tiles, "forward")
    tile_z_early = send(early_tiles[2], "tile_z_early")
    send_second(second[2], early_tiles, y_second[0], z_second[0])

    sums = None
    for i, (begin, size) in enumerate(zip(begins, SECOND)):
        step = 14 if size % 14 == 0 else 7
        ends = i == len(SECOND) - 1
        out = pair_sums(
            "late", info, k_plus_g, (y_second[i], 0), [(after(second[i], early_tiles), 0), (forward, begin // step), (z_second[i], 0)],
            begin, sums, size // step, step,
            [(y_second[0], SECOND[0]), here, (forward, tiles), (z_second[0], SECOND[0])] if ends else None,
        )
        sums = out[0]
    late_tile, late_tiles = out
    tile_y_late = send(late_tiles, "tile_y_late")
    tile_z_late = send(late_tiles[2], "tile_z_late")
    cross = send(late_tiles[1], "cross")
    return final(
        info, bands, diag, own, tile_core, early_tile, late_tile, tile_side, tile_y_early, tile_y_late, tile_z_early, tile_z_late, cross
    )


def solution(mesh):
    in_specs = (
        P(None, ("snap", "blk"), None),
        P("snap", None),
        P(("snap", "blk"), None),
        P(("snap", "blk")),
    )
    out_specs = P(None, None, ("snap", "blk"), None)
    return jax.shard_map(shards, mesh=mesh, in_specs=in_specs, out_specs=out_specs, check_vma=False)
```

time: 159 us -> 109 us (0.69)
  waiting for transfers between devices: 99.9 us -> 19.8 us
  Pallas kernels: 0 us -> 57.2 us
  matrix products: 30.3 us -> 0 us
  starting transfers between devices: 15.6 us -> 27.2 us
  other arithmetic: 7.83 us -> 0.65 us
    ppermute x6 -> x17, waiting for transfers between devices: 99.9 us -> 19.8 us  [shards(): send = lambda value, name: lax.ppermute(value, 'blk', way[name])]
    pallas_call x0 -> x9, Pallas kernels: none -> 57.2 us  [the longest x6 45.4 us: pair_sums(): pl.pallas_call(functools.partial(pair_body, kind, start is not None, step...]
    dot_general x3 -> x0, matrix products: 30.3 us -> none  [pair_tile(): jnp.einsum('acnp,dmp->acdnm', weighted, partner, preferred_element_type=j...]
    ppermute x6 -> x17, starting transfers between devices: 15.6 us -> 27.2 us  [shards(): send = lambda value, name: lax.ppermute(value, 'blk', way[name])]
    convert_element_type x3 -> x0, other arithmetic: 6.72 us -> none  [the longest x1 6.71 us: shards(): weighted = (k_plus_g[:, None, None, :] * coeffs[None]).astype(jnp.bfloat16)]
    squeeze x0 -> x2, local copies, waits for them, and re-layouts: none -> 1.87 us  [the longest x1 0.97 us: shards(): cross = send(late_tiles[1], 'cross')]
  transfers between devices with their start and end apart: 6 -> 17, of which waited for: 4 -> 2; matrix products, arithmetic and copies ran while one was open for 25% -> 2% of each run, Pallas kernels for 0% -> 42%
where the time goes in v1:
time: 109 us; the launch traced here: 108 us
  Pallas kernels  57.2 us (52%)
  starting transfers between devices  27.2 us (25%)
  waiting for transfers between devices  19.8 us (18%)
  local copies, waits for them, and re-layouts  2.6 us (2%)
    pallas_call x6, Pallas kernels, pair_sums(): pl.pallas_call(functools.partial(pair_body, kind, start is not None, step...  45.4 us
    ppermute x17, starting transfers between devices, shards(): send = lambda value, name: lax.ppermute(value, 'blk', way[name])  27.2 us
    ppermute x17, waiting for transfers between devices, shards(): send = lambda value, name: lax.ppermute(value, 'blk', way[name])  19.8 us
    pallas_call x2, Pallas kernels, halves(): pl.pallas_call(functools.partial(halves_body, which, cuts, with_facts), i...  7.8 us
    pallas_call x1, Pallas kernels, final(): pl.pallas_call(final_body, in_specs=[pl.BlockSpec(memory_space=pltpu.SMEM...  4 us
  transfers between devices with their start and end apart: 17, of which 2 were waited for; matrix products, arithmetic and copies ran while one was open for 2% of the time, Pallas kernels for 42%

profile of v1, /device:TPU:0, one launch (start us, length us, event | category | flops | bytes accessed | tf_op | source)
XLA Modules:
  0.0 107.7 jit_solution(11574080090783223137)
XLA Ops:
  0.0 0.7 pad_add_fusion.info
  0.7 3.4 %first.1.refs_1_.refs_2_.refs_0_.refs_4_ = bf16[2,96,6400]{2,1,0:T(8,128)(2,1)} custom-call(s32[3]{0:T(128)} %pad_add_fusion.info, s32[1,96]{1,0:T(1,128)} %bitcast.10, s32[1,2]{1,0:T(1,128)} %pairs.3, bf16[2,96,12544]{2,1,0:T(8,128)(2,1)} %refs_0_.1), custom_call_target="tpu_custom_call" | custom-call | flops 1000 | bytes 1000 | tf_op jit(solution)/shard_map/first/pallas_call | solution.py:221
  4.1 4.4 %second.1 = (bf16[2,96,6400]{2,1,0:T(8,128)(2,1)}, bf16[2,96,3712]{2,1,0:T(8,128)(2,1)}, bf16[2,96,1792]{2,1,0:T(8,128)(2,1)}, bf16[2,96,896]{2,1,0:T(8,128)(2,1)}) custom-call(s32[3]{0:T(128)} %pad_add_fusion.info, s32[1,96]{1,0:T(1,128)} %bitcast.11, s32[1,2]{1,0:T(1,128)} %pairs.3, bf16[2,96,12544]{2,1,0:T(8,128)(2,1)} %refs_0_.1), custom_call_target="tpu_custom_call" | custom-call | flops 1000 | bytes 1000 | tf_op jit(solution)/shard_map/second/pallas_call | solution.py:221
  8.5 0.5 collective-permute-start
  9.0 1.3 %collective-permute-start.3 = (bf16[2,96,6400]{2,1,0:T(8,128)(2,1)}, bf16[2,96,6400]{2,1,0:T(8,128)(2,1)}, u32[]{:S(2)}, u32[]{:S(2)}) collective-permute-start(bf16[2,96,6400]{2,1,0:T(8,128)(2,1)} %first.1.refs_1_.refs_2_.refs_0_.refs_4_), channel_id=1, source_target_pairs={{4,0},{8,4},{3,7},{12,8},{7,11},{11,15},{20,16},{24,20},{19,23},{2... | collective-permute-start | bytes 7372808 | tf_op jit(solution)/shard_map/ppermute | solution.py:311
  10.3 1.3 %collective-permute-start.2 = (bf16[2,96,6400]{2,1,0:T(8,128)(2,1)}, bf16[2,96,6400]{2,1,0:T(8,128)(2,1)}, u32[]{:S(2)}, u32[]{:S(2)}) collective-permute-start(bf16[2,96,6400]{2,1,0:T(8,128)(2,1)} %first.1.refs_1_.refs_2_.refs_0_.refs_4_), channel_id=1, source_target_pairs={{2,0},{1,3},{6,4},{5,7},{10,8},{9,11},{14,12},{13,15},{18,16},{17,... | collective-permute-start | bytes 7372808 | tf_op jit(solution)/shard_map/ppermute | solution.py:311
  11.6 10.3 %diag.1 = f32[288,192]{1,0:T(8,128)} custom-call(s32[3]{0:T(128)} %pad_add_fusion.info, f32[3,12544]{1,0:T(4,128)} %k_ref.11, bf16[2,96,12544]{2,1,0:T(8,128)(2,1)} %refs_0_.1, bf16[2,96,12544]{2,1,0:T(8,128)(2,1)} %refs_0_.1, bf16[2,96,6400]{2,1,0:T(8,128)(2,1)} %first.1.refs_1_.refs_2_.refs_0_.refs_4_, ...), custom_call_target="tpu_custom_call" | custom-call | flops 1000 | bytes 1000 | tf_op jit(solution)/shard_map/diag/pallas_call | solution.py:162
  21.8 0.0 collective-permute-done.x_ref.refs_1_.refs_5_
  21.8 8.5 %near.1 = (f32[288,192]{1,0:T(8,128)}, bf16[1,432,128]{2,1,0:T(8,128)(2,1)}) custom-call(s32[3]{0:T(128)} %pad_add_fusion.info, f32[3,12544]{1,0:T(4,128)} %k_ref.11, bf16[2,96,6400]{2,1,0:T(8,128)(2,1)} %collective-permute-done.x_ref.refs_1_.refs_5_, bf16[2,96,6400]{2,1,0:T(8,128)(2,1)} %first.1.refs_1_.refs_2_.refs_0_.refs_4_, ...), custom_call_target="tpu_custom_call" | custom-call | flops 1000 | bytes 1000 | tf_op jit(solution)/shard_map/near/pallas_call | solution.py:162
  30.3 11.4 %collective-permute-done.3.refs_2_.refs_6_ = bf16[2,96,6400]{2,1,0:T(8,128)(2,1)} collective-permute-done((bf16[2,96,6400]{2,1,0:T(8,128)(2,1)}, bf16[2,96,6400]{2,1,0:T(8,128)(2,1)}, u32[]{:S(2)}, u32[]{:S(2)}) %collective-permute-start.3) | collective-permute-done | bytes 2457632 | tf_op jit(solution)/shard_map/ppermute | solution.py:311
  41.7 2.8 %collective-permute-start.7 = (bf16[2,96,6400]{2,1,0:T(8,128)(2,1)}, bf16[2,96,6400]{2,1,0:T(8,128)(2,1)}, u32[]{:S(2)}, u32[]{:S(2)}) collective-permute-start(bf16[2,96,6400]{2,1,0:T(8,128)(2,1)} %collective-permute-done.3.refs_2_.refs_6_), channel_id=1, source_target_pairs={{0,1},{3,2},{4,5},{7,6},{8,9},{11,10},{12,13},{15,14},{16,17},{19,... | collective-permute-start | bytes 7372808 | tf_op jit(solution)/shard_map/ppermute | solution.py:311
  44.4 0.7 collective-permute-start.5
  45.2 2.4 %collective-permute-start.4 = (bf16[2,96,3712]{2,1,0:T(8,128)(2,1)}, bf16[2,96,3712]{2,1,0:T(8,128)(2,1)}, u32[]{:S(2)}, u32[]{:S(2)}) collective-permute-start(bf16[2,96,3712]{2,1,0:T(8,128)(2,1)} %get-tuple-element.44.refs_0_), channel_id=1, source_target_pairs={{3,1},{0,2},{7,5},{4,6},{11,9},{8,10},{15,13},{12,14},{19,17},{16,... | collective-permute-start | bytes 4276232 | tf_op jit(solution)/shard_map/ppermute | solution.py:311
  47.6 0.0 collective-permute-done.2.x_ref.refs_3_
  47.6 0.0 copy-start.1
  47.6 1.6 %collective-permute-start.10 = (bf16[2,96,1792]{2,1,0:T(8,128)(2,1)}, bf16[2,96,1792]{2,1,0:T(8,128)(2,1)}, u32[]{:S(2)}, u32[]{:S(2)}) collective-permute-start(bf16[2,96,1792]{2,1,0:T(8,128)(2,1)} %get-tuple-element.43.refs_0_), channel_id=1, source_target_pairs={{5,1},{9,5},{2,6},{13,9},{6,10},{10,14},{21,17},{25,21},{18,22},{2... | collective-permute-start | bytes 2064392 | tf_op jit(solution)/shard_map/ppermute | solution.py:311
  49.2 2.1 %collective-permute-start.9 = (bf16[2,96,1792]{2,1,0:T(8,128)(2,1)}, bf16[2,96,1792]{2,1,0:T(8,128)(2,1)}, u32[]{:S(2)}, u32[]{:S(2)}) collective-permute-start(bf16[2,96,1792]{2,1,0:T(8,128)(2,1)} %get-tuple-element.43.refs_0_), channel_id=1, source_target_pairs={{3,1},{0,2},{7,5},{4,6},{11,9},{8,10},{15,13},{12,14},{19,17},{16,... | collective-permute-start | bytes 2064392 | tf_op jit(solution)/shard_map/ppermute | solution.py:311
  51.4 16.1 %early.1 = (f32[288,192]{1,0:T(8,128)}, bf16[3,432,128]{2,1,0:T(8,128)(2,1)}) custom-call(s32[3]{0:T(128)} %pad_add_fusion.info, f32[3,12544]{1,0:T(4,128)} %k_ref.11, bf16[2,96,6400]{2,1,0:T(8,128)(2,1)} %collective-permute-done.2.x_ref.refs_3_, bf16[2,96,6400]{2,1,0:T(8,128)(2,1)} %first.1.refs_1_.refs_2_.refs_0_.refs_4_, ...), custom_call_target="tpu_custom_call" | custom-call | flops 1000 | bytes 1000 | tf_op jit(solution)/shard_map/early/pallas_call | solution.py:162
  67.5 0.0 collective-permute-done.5.refs_2_.refs_6_
  67.5 0.0 copy-start
  67.5 0.0 collective-permute-done.4.x_ref.refs_3_
  67.5 0.0 copy-done.1
  67.5 1.4 %collective-permute-start.8 = (bf16[2,96,896]{2,1,0:T(8,128)(2,1)S(1)}, bf16[2,96,896]{2,1,0:T(8,128)(2,1)}, u32[]{:S(2)}, u32[]{:S(2)}) collective-permute-start(bf16[2,96,896]{2,1,0:T(8,128)(2,1)S(1)} %copy-done.1), channel_id=1, source_target_pairs={{5,1},{9,5},{2,6},{13,9},{6,10},{10,14},{21,17},{25,21},{18,22},{2... | collective-permute-start | bytes 1032200 | tf_op jit(solution)/shard_map/ppermute | solution.py:311
  68.9 4.0 %collective-permute-start.6 = (bf16[2,96,896]{2,1,0:T(8,128)(2,1)S(1)}, bf16[2,96,896]{2,1,0:T(8,128)(2,1)}, u32[]{:S(2)}, u32[]{:S(2)}) collective-permute-start(bf16[2,96,896]{2,1,0:T(8,128)(2,1)S(1)} %copy-done.1), channel_id=1, source_target_pairs={{3,1},{0,2},{7,5},{4,6},{11,9},{8,10},{15,13},{12,14},{19,17},{16,... | collective-permute-start | bytes 1032200 | tf_op jit(solution)/shard_map/ppermute | solution.py:311
  72.9 0.9 slice_bitcast_fusion.2
  73.8 0.0 collective-permute-done.7.refs_1_.refs_5_
  73.8 2.0 %collective-permute-start.12 = (bf16[3,432,128]{2,1,0:T(8,128)(2,1)}, bf16[3,432,128]{2,1,0:T(8,128)(2,1)}, u32[]{:S(2)}, u32[]{:S(2)}) collective-permute-start(bf16[3,432,128]{2,1,0:T(8,128)(2,1)} %get-tuple-element.35), channel_id=1, source_target_pairs={{0,2},{3,1},{4,6},{7,5},{8,10},{11,9},{12,14},{15,13},{16,18},{19,... | collective-permute-start | bytes 995336 | tf_op jit(solution)/shard_map/ppermute | solution.py:311
  75.8 0.0 copy-done
  75.8 3.5 %late.3.refs_3_ = f32[3,288,192]{2,1,0:T(8,128)} custom-call(s32[3]{0:T(128)} %pad_add_fusion.info, f32[3,12544]{1,0:T(4,128)} %k_ref.11, bf16[2,96,3712]{2,1,0:T(8,128)(2,1)} %collective-permute-done.4.x_ref.refs_3_, bf16[2,96,3712]{2,1,0:T(8,128)(2,1)} %get-tuple-element.44.refs_0_, bf16[2,96,6400]{2,1,0:T(8,128)(2,1)} %collective-permute-done.7.refs_1_.refs_5_, ...), custom_call_target="tpu_custom_call" | custom-call | flops 1000 | bytes 1000 | tf_op jit(solution)/shard_map/late/pallas_call | solution.py:162
  79.4 0.0 copy-start.8
  79.4 0.0 collective-permute-done.10.refs_2_
  79.4 1.4 %collective-permute-start.11 = (bf16[3,432,128]{2,1,0:T(8,128)(2,1)}, bf16[3,432,128]{2,1,0:T(8,128)(2,1)S(1)}, u32[]{:S(2)}, u32[]{:S(2)}) collective-permute-start(bf16[3,432,128]{2,1,0:T(8,128)(2,1)} %get-tuple-element.35), channel_id=1, source_target_pairs={{0,1},{3,2},{4,5},{7,6},{8,9},{11,10},{12,13},{15,14},{16,17},{19,... | collective-permute-start | bytes 995336 | tf_op jit(solution)/shard_map/ppermute | solution.py:311
  80.8 0.0 collective-permute-done.9.x_ref
  80.8 2.8 %collective-permute-start.14 = (bf16[432,128]{1,0:T(8,128)(2,1)S(1)}, bf16[432,128]{1,0:T(8,128)(2,1)S(1)}, u32[]{:S(2)}, u32[]{:S(2)}) collective-permute-start(bf16[432,128]{1,0:T(8,128)(2,1)S(1)} %slice_bitcast_fusion.2), channel_id=1, source_target_pairs={{0,4},{4,8},{7,3},{8,12},{11,7},{15,11},{16,20},{20,24},{23,19},{2... | collective-permute-start | bytes 331784 | tf_op jit(solution)/shard_map/ppermute | solution.py:311
  83.7 3.7 %late.4.refs_7_ = f32[3,288,192]{2,1,0:T(8,128)} custom-call(s32[3]{0:T(128)} %pad_add_fusion.info, f32[3,12544]{1,0:T(4,128)} %k_ref.11, bf16[2,96,1792]{2,1,0:T(8,128)(2,1)} %collective-permute-done.9.x_ref, bf16[2,96,1792]{2,1,0:T(8,128)(2,1)} %get-tuple-element.43.refs_0_, bf16[2,96,6400]{2,1,0:T(8,128)(2,1)} %collective-permute-done.7.refs_1_.refs_5_, ...), custom_call_target="tpu_custom_call" | custom-call | flops 1000 | bytes 1000 | tf_op jit(solution)/shard_map/late/pallas_call | solution.py:162
  87.4 0.0 collective-permute-done.8.refs_2_
  87.4 0.0 copy-done.8
  87.4 0.1 collective-permute-start.1
  87.5 0.0 collective-permute-done.6.x_ref
  87.5 3.3 %late.5 = (f32[288,192]{1,0:T(8,128)}, bf16[3,432,128]{2,1,0:T(8,128)(2,1)}) custom-call(s32[3]{0:T(128)} %pad_add_fusion.info, f32[3,12544]{1,0:T(4,128)} %k_ref.11, bf16[2,96,896]{2,1,0:T(8,128)(2,1)} %collective-permute-done.6.x_ref, bf16[2,96,896]{2,1,0:T(8,128)(2,1)} %get-tuple-element.39.refs_0_, ...), custom_call_target="tpu_custom_call" | custom-call | flops 1000 | bytes 1000 | tf_op jit(solution)/shard_map/late/pallas_call | solution.py:162
  90.8 1.3 %collective-permute-start.13 = (bf16[3,432,128]{2,1,0:T(8,128)(2,1)}, bf16[3,432,128]{2,1,0:T(8,128)(2,1)S(1)}, u32[]{:S(2)}, u32[]{:S(2)}) collective-permute-start(bf16[3,432,128]{2,1,0:T(8,128)(2,1)} %get-tuple-element.46), channel_id=1, source_target_pairs={{1,3},{2,0},{5,7},{6,4},{9,11},{10,8},{13,15},{14,12},{17,19},{18,... | collective-permute-start | bytes 995336 | tf_op jit(solution)/shard_map/ppermute | solution.py:311
  92.1 1.0 slice_bitcast_fusion
  93.0 0.0 collective-permute-done.14.up_z
  93.1 0.0 copy-start.4
  93.1 0.7 collective-permute-start.16
  93.7 0.0 collective-permute-done.1.core
  93.8 0.0 copy-start.5
  93.8 0.7 collective-permute-start.15
  94.4 0.0 collective-permute-done.12.up_y
  94.4 0.0 collective-permute-done.11.side
  94.5 0.0 copy-start.2
  94.5 0.0 collective-permute-done.16.cross
  94.5 0.0 copy-start.6
  94.5 0.0 collective-permute-done.15.down_z
  94.5 0.0 copy-start.7
  94.5 8.4 %collective-permute-done.13.down_y = bf16[3,432,128]{2,1,0:T(8,128)(2,1)S(1)} collective-permute-done((bf16[3,432,128]{2,1,0:T(8,128)(2,1)}, bf16[3,432,128]{2,1,0:T(8,128)(2,1)S(1)}, u32[]{:S(2)}, u32[]{:S(2)}) %collective-permute-start.13) | collective-permute-done | bytes 331808 | tf_op jit(solution)/shard_map/ppermute | solution.py:311
  103.0 0.0 copy-start.3
  103.0 0.0 copy-done.4
  103.0 0.0 copy-done.5
  103.0 0.0 copy-done.2
  103.0 0.0 copy-done.6
  103.0 0.0 copy-done.7
  103.0 0.7 copy-done.3
  103.7 4.0 %final.1 = f32[3,2,96,480]{3,2,1,0:T(8,128)} custom-call(s32[3]{0:T(128)} %pad_add_fusion.info, f32[288,192]{1,0:T(8,128)} %diag.1, f32[288,192]{1,0:T(8,128)} %get-tuple-element.30.own, bf16[1,432,128]{2,1,0:T(8,128)(2,1)} %copy-done.5, f32[288,192]{1,0:T(8,128)} %get-tuple-element.33.early, f32[288,192]{1,0:T(8,128)} %get-tuple-element.45.late, ...), custom_call_target="tpu_custom_call" | custom-call | tf_op jit(solution)/shard_map/final/pallas_call | solution.py:266
Async XLA Ops:
  8.5 13.4 %collective-permute-start = (bf16[2,96,6400]{2,1,0:T(8,128)(2,1)}, bf16[2,96,6400]{2,1,0:T(8,128)(2,1)}, u32[]{:S(2)}, u32[]{:S(2)}) collective-permute-start(bf16[2,96,6400]{2,1,0:T(8,128)(2,1)} %get-tuple-element.27), channel_id=1, source_target_pairs={{0,1},{1,0},{2,3},{3,2},{4,5},{5,4},{6,7},{7,6},{8,9},{9,8},{10,11... | collective-permute-start | bytes 7372808 | tf_op jit(solution)/shard_map/ppermute | solution.py:311
  9.0 32.7 %collective-permute-start.3 = (bf16[2,96,6400]{2,1,0:T(8,128)(2,1)}, bf16[2,96,6400]{2,1,0:T(8,128)(2,1)}, u32[]{:S(2)}, u32[]{:S(2)}) collective-permute-start(bf16[2,96,6400]{2,1,0:T(8,128)(2,1)} %first.1.refs_1_.refs_2_.refs_0_.refs_4_), channel_id=1, source_target_pairs={{4,0},{8,4},{3,7},{12,8},{7,11},{11,15},{20,16},{24,20},{19,23},{2... | collective-permute-start | bytes 7372808 | tf_op jit(solution)/shard_map/ppermute | solution.py:311
  10.3 37.3 %collective-permute-start.2 = (bf16[2,96,6400]{2,1,0:T(8,128)(2,1)}, bf16[2,96,6400]{2,1,0:T(8,128)(2,1)}, u32[]{:S(2)}, u32[]{:S(2)}) collective-permute-start(bf16[2,96,6400]{2,1,0:T(8,128)(2,1)} %first.1.refs_1_.refs_2_.refs_0_.refs_4_), channel_id=1, source_target_pairs={{2,0},{1,3},{6,4},{5,7},{10,8},{9,11},{14,12},{13,15},{18,16},{17,... | collective-permute-start | bytes 7372808 | tf_op jit(solution)/shard_map/ppermute | solution.py:311
  41.7 32.1 %collective-permute-start.7 = (bf16[2,96,6400]{2,1,0:T(8,128)(2,1)}, bf16[2,96,6400]{2,1,0:T(8,128)(2,1)}, u32[]{:S(2)}, u32[]{:S(2)}) collective-permute-start(bf16[2,96,6400]{2,1,0:T(8,128)(2,1)} %collective-permute-done.3.refs_2_.refs_6_), channel_id=1, source_target_pairs={{0,1},{3,2},{4,5},{7,6},{8,9},{11,10},{12,13},{15,14},{16,17},{19,... | collective-permute-start | bytes 7372808 | tf_op jit(solution)/shard_map/ppermute | solution.py:311
  44.4 23.1 %collective-permute-start.5 = (bf16[2,96,3712]{2,1,0:T(8,128)(2,1)}, bf16[2,96,3712]{2,1,0:T(8,128)(2,1)S(1)}, u32[]{:S(2)}, u32[]{:S(2)}) collective-permute-start(bf16[2,96,3712]{2,1,0:T(8,128)(2,1)} %get-tuple-element.44.refs_0_), channel_id=1, source_target_pairs={{5,1},{9,5},{2,6},{13,9},{6,10},{10,14},{21,17},{25,21},{18,22},{2... | collective-permute-start | bytes 4276232 | tf_op jit(solution)/shard_map/ppermute | solution.py:311
  45.2 22.3 %collective-permute-start.4 = (bf16[2,96,3712]{2,1,0:T(8,128)(2,1)}, bf16[2,96,3712]{2,1,0:T(8,128)(2,1)}, u32[]{:S(2)}, u32[]{:S(2)}) collective-permute-start(bf16[2,96,3712]{2,1,0:T(8,128)(2,1)} %get-tuple-element.44.refs_0_), channel_id=1, source_target_pairs={{3,1},{0,2},{7,5},{4,6},{11,9},{8,10},{15,13},{12,14},{19,17},{16,... | collective-permute-start | bytes 4276232 | tf_op jit(solution)/shard_map/ppermute | solution.py:311
  47.6 19.9 %copy-start.1 = (bf16[2,96,896]{2,1,0:T(8,128)(2,1)S(1)}, bf16[2,96,896]{2,1,0:T(8,128)(2,1)}, u32[]{:S(2)}) copy-start(bf16[2,96,896]{2,1,0:T(8,128)(2,1)} %get-tuple-element.39.refs_0_) | copy-start | bytes 1032196
  47.6 31.8 %collective-permute-start.10 = (bf16[2,96,1792]{2,1,0:T(8,128)(2,1)}, bf16[2,96,1792]{2,1,0:T(8,128)(2,1)}, u32[]{:S(2)}, u32[]{:S(2)}) collective-permute-start(bf16[2,96,1792]{2,1,0:T(8,128)(2,1)} %get-tuple-element.43.refs_0_), channel_id=1, source_target_pairs={{5,1},{9,5},{2,6},{13,9},{6,10},{10,14},{21,17},{25,21},{18,22},{2... | collective-permute-start | bytes 2064392 | tf_op jit(solution)/shard_map/ppermute | solution.py:311
  49.2 31.6 %collective-permute-start.9 = (bf16[2,96,1792]{2,1,0:T(8,128)(2,1)}, bf16[2,96,1792]{2,1,0:T(8,128)(2,1)}, u32[]{:S(2)}, u32[]{:S(2)}) collective-permute-start(bf16[2,96,1792]{2,1,0:T(8,128)(2,1)} %get-tuple-element.43.refs_0_), channel_id=1, source_target_pairs={{3,1},{0,2},{7,5},{4,6},{11,9},{8,10},{15,13},{12,14},{19,17},{16,... | collective-permute-start | bytes 2064392 | tf_op jit(solution)/shard_map/ppermute | solution.py:311
  67.5 8.4 %copy-start = (bf16[2,96,3712]{2,1,0:T(8,128)(2,1)}, bf16[2,96,3712]{2,1,0:T(8,128)(2,1)S(1)}, u32[]{:S(2)}) copy-start(bf16[2,96,3712]{2,1,0:T(8,128)(2,1)S(1)} %collective-permute-done.5.refs_2_.refs_6_) | copy-start | bytes 4276228
  67.5 19.9 %collective-permute-start.8 = (bf16[2,96,896]{2,1,0:T(8,128)(2,1)S(1)}, bf16[2,96,896]{2,1,0:T(8,128)(2,1)}, u32[]{:S(2)}, u32[]{:S(2)}) collective-permute-start(bf16[2,96,896]{2,1,0:T(8,128)(2,1)S(1)} %copy-done.1), channel_id=1, source_target_pairs={{5,1},{9,5},{2,6},{13,9},{6,10},{10,14},{21,17},{25,21},{18,22},{2... | collective-permute-start | bytes 1032200 | tf_op jit(solution)/shard_map/ppermute | solution.py:311
  68.9 18.6 %collective-permute-start.6 = (bf16[2,96,896]{2,1,0:T(8,128)(2,1)S(1)}, bf16[2,96,896]{2,1,0:T(8,128)(2,1)}, u32[]{:S(2)}, u32[]{:S(2)}) collective-permute-start(bf16[2,96,896]{2,1,0:T(8,128)(2,1)S(1)} %copy-done.1), channel_id=1, source_target_pairs={{3,1},{0,2},{7,5},{4,6},{11,9},{8,10},{15,13},{12,14},{19,17},{16,... | collective-permute-start | bytes 1032200 | tf_op jit(solution)/shard_map/ppermute | solution.py:311
  73.8 20.6 %collective-permute-start.12 = (bf16[3,432,128]{2,1,0:T(8,128)(2,1)}, bf16[3,432,128]{2,1,0:T(8,128)(2,1)}, u32[]{:S(2)}, u32[]{:S(2)}) collective-permute-start(bf16[3,432,128]{2,1,0:T(8,128)(2,1)} %get-tuple-element.35), channel_id=1, source_target_pairs={{0,2},{3,1},{4,6},{7,5},{8,10},{11,9},{12,14},{15,13},{16,18},{19,... | collective-permute-start | bytes 995336 | tf_op jit(solution)/shard_map/ppermute | solution.py:311
  79.4 8.1 %copy-start.8 = (bf16[1,432,128]{2,1,0:T(8,128)(2,1)S(1)}, bf16[1,432,128]{2,1,0:T(8,128)(2,1)}, u32[]{:S(2)}) copy-start(bf16[1,432,128]{2,1,0:T(8,128)(2,1)} %get-tuple-element.31) | copy-start | bytes 331780
  79.4 15.1 %collective-permute-start.11 = (bf16[3,432,128]{2,1,0:T(8,128)(2,1)}, bf16[3,432,128]{2,1,0:T(8,128)(2,1)S(1)}, u32[]{:S(2)}, u32[]{:S(2)}) collective-permute-start(bf16[3,432,128]{2,1,0:T(8,128)(2,1)} %get-tuple-element.35), channel_id=1, source_target_pairs={{0,1},{3,2},{4,5},{7,6},{8,9},{11,10},{12,13},{15,14},{16,17},{19,... | collective-permute-start | bytes 995336 | tf_op jit(solution)/shard_map/ppermute | solution.py:311
  80.8 12.2 %collective-permute-start.14 = (bf16[432,128]{1,0:T(8,128)(2,1)S(1)}, bf16[432,128]{1,0:T(8,128)(2,1)S(1)}, u32[]{:S(2)}, u32[]{:S(2)}) collective-permute-start(bf16[432,128]{1,0:T(8,128)(2,1)S(1)} %slice_bitcast_fusion.2), channel_id=1, source_target_pairs={{0,4},{4,8},{7,3},{8,12},{11,7},{15,11},{16,20},{20,24},{23,19},{2... | collective-permute-start | bytes 331784 | tf_op jit(solution)/shard_map/ppermute | solution.py:311
  87.4 6.3 %collective-permute-start.1 = (bf16[1,432,128]{2,1,0:T(8,128)(2,1)S(1)}, bf16[1,432,128]{2,1,0:T(8,128)(2,1)S(1)}, u32[]{:S(2)}, u32[]{:S(2)}) collective-permute-start(bf16[1,432,128]{2,1,0:T(8,128)(2,1)S(1)} %copy-done.8), channel_id=1, source_target_pairs={{0,1},{1,0},{2,3},{3,2},{4,5},{5,4},{6,7},{7,6},{8,9},{9,8},{10,11... | collective-permute-start | bytes 331784 | tf_op jit(solution)/shard_map/ppermute | solution.py:311
  90.8 12.2 %collective-permute-start.13 = (bf16[3,432,128]{2,1,0:T(8,128)(2,1)}, bf16[3,432,128]{2,1,0:T(8,128)(2,1)S(1)}, u32[]{:S(2)}, u32[]{:S(2)}) collective-permute-start(bf16[3,432,128]{2,1,0:T(8,128)(2,1)} %get-tuple-element.46), channel_id=1, source_target_pairs={{1,3},{2,0},{5,7},{6,4},{9,11},{10,8},{13,15},{14,12},{17,19},{18,... | collective-permute-start | bytes 995336 | tf_op jit(solution)/shard_map/ppermute | solution.py:311
  93.1 9.9 %copy-start.4 = (bf16[432,128]{1,0:T(8,128)(2,1)}, bf16[432,128]{1,0:T(8,128)(2,1)S(1)}, u32[]{:S(2)}) copy-start(bf16[432,128]{1,0:T(8,128)(2,1)S(1)} %collective-permute-done.14.up_z) | copy-start | bytes 331780
  93.1 1.4 %collective-permute-start.16 = (bf16[432,128]{1,0:T(8,128)(2,1)S(1)}, bf16[432,128]{1,0:T(8,128)(2,1)S(1)}, u32[]{:S(2)}, u32[]{:S(2)}) collective-permute-start(bf16[432,128]{1,0:T(8,128)(2,1)S(1)} %get-tuple-element.47), channel_id=1, source_target_pairs={{1,4},{5,8},{6,3},{9,12},{10,7},{14,11},{17,20},{21,24},{22,19},{2... | collective-permute-start | bytes 331784 | tf_op jit(solution)/shard_map/ppermute | solution.py:311
  93.8 9.2 %copy-start.5 = (bf16[1,432,128]{2,1,0:T(8,128)(2,1)}, bf16[1,432,128]{2,1,0:T(8,128)(2,1)S(1)}, u32[]{:S(2)}) copy-start(bf16[1,432,128]{2,1,0:T(8,128)(2,1)S(1)} %collective-permute-done.1.core) | copy-start | bytes 331780
  93.8 0.7 collective-permute-start.15
  94.5 8.5 %copy-start.2 = (bf16[3,432,128]{2,1,0:T(8,128)(2,1)}, bf16[3,432,128]{2,1,0:T(8,128)(2,1)S(1)}, u32[]{:S(2)}) copy-start(bf16[3,432,128]{2,1,0:T(8,128)(2,1)S(1)} %collective-permute-done.11.side) | copy-start | bytes 995332
  94.5 8.5 %copy-start.6 = (bf16[432,128]{1,0:T(8,128)(2,1)}, bf16[432,128]{1,0:T(8,128)(2,1)S(1)}, u32[]{:S(2)}) copy-start(bf16[432,128]{1,0:T(8,128)(2,1)S(1)} %collective-permute-done.16.cross) | copy-start | bytes 331780
  94.5 8.5 %copy-start.7 = (bf16[432,128]{1,0:T(8,128)(2,1)}, bf16[432,128]{1,0:T(8,128)(2,1)S(1)}, u32[]{:S(2)}) copy-start(bf16[432,128]{1,0:T(8,128)(2,1)S(1)} %collective-permute-done.15.down_z) | copy-start | bytes 331780
  103.0 0.7 copy-start.3

commit v2 on v0

v2 whole, which is shorter than its diff:
```python
import functools
import math

import jax
import jax.numpy as jnp
from jax import lax
from jax.experimental import pallas as pl
from jax.experimental.pallas import tpu as pltpu
from jax.sharding import PartitionSpec as P

REACH = 2
OCC_STEPS = 16
SPAN = 5
LANES = 128
CHUNKS = (24, 25)
F32 = jnp.float32
BF16 = jnp.bfloat16
VMEM_BYTES = 62 * 2**20


def product(k, low, high):
    dims = (((1,), (1,)), ((), ()))
    wide = low.astype(F32)
    rows = [jnp.concatenate([(k[a][None, :] * wide[c]).astype(BF16) for a in range(3)], axis=0) for c in range(2)]
    straight = jnp.concatenate([high[0], high[1]], axis=0)
    turned = jnp.concatenate([high[1], -high[0]], axis=0)
    first = lax.dot_general(rows[0], straight, dims, preferred_element_type=F32)
    return first + lax.dot_general(rows[1], turned, dims, preferred_element_type=F32)


def weights_of(low, high, offset, scale):
    bands = low.shape[1]
    low, high = low.astype(F32), high.astype(F32)
    if isinstance(offset, int):
        flag = low[1, 0:1, bands + offset - 1 : bands + offset] if offset else 1.0
    else:
        flag = jnp.where(offset == 1, low[1, 0:1, bands : bands + 1], low[1, 0:1, bands + 1 : bands + 2])
    weights = (low[0][:, :bands] - high[1][:, :bands]) * (flag * scale)
    weights = jnp.concatenate([weights] * 3, axis=0)
    return jnp.concatenate([weights, weights], axis=1)


def pack(tile):
    rows = tile.shape[0]
    rest = tile[:, LANES:]
    return jnp.concatenate([tile[:, :LANES], jnp.concatenate([rest[: rows // 2], rest[rows // 2 :]], axis=1)], axis=0)


def unpack(packed):
    rows = packed.shape[0] * 2 // 3
    rest = packed[rows:]
    width = LANES // 2
    return jnp.concatenate([packed[:rows], jnp.concatenate([rest[:, :width], rest[:, width:]], axis=0)], axis=1)


OFFSETS = {"diag": (0,), "near": (1,), "far": (2, 1, 2)}


def roles(kind, info):
    first, side, core = info[0], info[1], info[2]
    if kind == "diag":
        return 0, (0,)
    if kind == "near":
        return core, (1 - core,)
    return side, (1 - side, jnp.where(first == 1, 1 - side, side), side)


def pick(values, i):
    out = values[0]
    for j in range(1, len(values)):
        out = jnp.where(i == j, values[j], out)
    return out


def pair_body(kind, first_tile, tiles, plans, facts_plans, has_start, scale, info, k_hbm, *refs):
    offsets = OFFSETS[kind]
    count, blocks = len(offsets), len(plans)
    half, others = roles(kind, info)
    ends = facts_plans is not None
    refs = list(refs)
    take = lambda number: [refs.pop(0) for _ in range(number)]
    sources = [take(len(plan)) for plan in plans]
    facts_sources = [take(len(plan)) for plan in facts_plans] if ends else []
    start_hbm = take(1)[0] if has_start else None
    outs = take(len(refs) - 9)
    k_held, held, facts, start, acc, sems, k_sem, facts_sems, start_sem = refs

    half_tiles = k_hbm.shape[1] // 2 // LANES
    first = half * half_tiles + first_tile
    k_copy = pltpu.make_async_copy(k_hbm.at[:, pl.ds(pl.multiple_of(first * LANES, LANES), tiles * LANES)], k_held, k_sem)

    def copies(plan, arrays, into, size, sems):
        out = []
        for n, (array, (where, at)) in enumerate(zip(arrays, plan)):
            when = None if where is None else info[0] == 1 if "first" in where else info[0] == 0 if "second" in where else None
            at += 0 if where is None else info[1] * half_tiles if "side" in where else info[2] * half_tiles if "core" in where else 0
            span = pl.ds(at * LANES if isinstance(at, int) else pl.multiple_of(at * LANES, LANES), size * LANES)
            out.append((when, pltpu.make_async_copy(array.at[:, :, span], into, sems.at[n])))
        return out

    def each(copies, run):
        for when, copy in copies:
            if when is None:
                run(copy)
            else:
                pl.when(when)(functools.partial(run, copy))

    begin = lambda copies: each(copies, lambda copy: copy.start())
    wait = lambda copies: each(copies, lambda copy: copy.wait())
    loads = [copies(plans[b], sources[b], held.at[b], tiles, sems.at[b]) for b in range(blocks)]
    later = []
    if ends:
        for b in range(blocks):
            later += copies(facts_plans[b], facts_sources[b], facts.at[b], 1, facts_sems.at[b])
    if has_start:
        later.append((None, pltpu.make_async_copy(start_hbm, start, start_sem)))
    k_copy.start()
    for load in loads[:2]:
        begin(load)
    begin(later)
    k_copy.wait()
    wait(loads[0])

    def order(i):
        if kind == "diag":
            return 0, 0
        other = pick(others, i) == 1
        return jnp.where(other, i + 1, 0), jnp.where(other, 0, i + 1)

    @pl.loop(0, count)
    def _(i):
        for j in range(1, blocks):
            @pl.when(i == j - 1)
            def _():
                wait(loads[j])
                if j == 1:
                    for load in loads[2:]:
                        begin(load)

        low, high = order(i)
        acc[i] = product(k_held[...], held[low], held[high])

    wait(later)

    @pl.loop(0, count)
    def _(i):
        tile = acc[i]
        if has_start:
            tile = tile + start[i]
        if not ends:
            outs[0][i] = tile
            return
        low, high = order(i)
        tile = tile * weights_of(facts[low], facts[high], 0 if kind == "diag" else pick(offsets, i), scale)

        @pl.when(i == 0)
        def _():
            outs[0][...] = tile

        if len(outs) > 1:
            packed = pack(tile).astype(BF16)
            outs[1][i] = packed
        for j in range(2, len(outs)):
            @pl.when(i == j - 1)
            def _():
                outs[j][...] = packed


def pair_sums(kind, info, k, blocks, begin, tiles, facts=None, start=None):
    bands = blocks[0][0][0].shape[1]
    count = len(OFFSETS[kind])
    ends = facts is not None
    shape = (count, 3 * bands, 2 * bands)
    arrays = lambda blocks: [part[0] for block in blocks for part in block]
    plans = lambda blocks: tuple(tuple((part[1], part[2]) for part in block) for block in blocks)
    operands = [k] + arrays(blocks) + arrays(facts or []) + ([] if start is None else [start])
    packed = (9 * bands // 2, LANES)
    if not ends:
        out_shape = [jax.ShapeDtypeStruct(shape, F32)]
    else:
        out_shape = [jax.ShapeDtypeStruct(shape[1:], F32)]
        if kind != "diag":
            out_shape.append(jax.ShapeDtypeStruct((count, *packed), BF16))
        if count == 3:
            out_shape += [jax.ShapeDtypeStruct(packed, BF16)] * 2
    return pl.pallas_call(
        functools.partial(
            pair_body, kind, begin, tiles, plans(blocks), plans(facts) if ends else None, start is not None, 1.0 / math.sqrt(k.shape[1])
        ),
        in_specs=[pl.BlockSpec(memory_space=pltpu.SMEM)] + [pl.BlockSpec(memory_space=pl.ANY)] * len(operands),
        out_specs=[pl.BlockSpec(memory_space=pltpu.VMEM)] * len(out_shape),
        out_shape=out_shape,
        scratch_shapes=[
            pltpu.VMEM((k.shape[0], tiles * LANES), F32),
            pltpu.VMEM((len(blocks), 2, bands, tiles * LANES), BF16),
            pltpu.VMEM((len(blocks), 2, bands, LANES), BF16),
            pltpu.VMEM(shape, F32),
            pltpu.VMEM(shape, F32),
            pltpu.SemaphoreType.DMA((len(blocks), 2)),
            pltpu.SemaphoreType.DMA,
            pltpu.SemaphoreType.DMA((len(blocks), 2)),
            pltpu.SemaphoreType.DMA,
        ],
        compiler_params=pltpu.CompilerParams(vmem_limit_bytes=VMEM_BYTES),
        cost_estimate=pl.CostEstimate(flops=1000, bytes_accessed=1000, transcendentals=0),
        name=kind,
    )(info, *operands)


def pieces_body(cuts, info, levels, pairs, coeffs, *refs):
    outs, held, sems = refs[: len(cuts)], refs[-2], refs[-1]
    bands = coeffs.shape[1]
    half = coeffs.shape[2] // 2
    tiles = half // LANES
    side, core = info[1], info[2]
    span = lambda start, size: pl.ds(pl.multiple_of(start, LANES), size * LANES)
    loads, stores, at = [], [], 1
    for n, (which, start, size, more) in enumerate(cuts):
        source = half * {"y": 1 - side, "z": side, "core": 1 - core}[which] + start * LANES
        if size == 0:
            continue
        here = held.at[:, :, span(at * LANES, size)]
        loads.append(pltpu.make_async_copy(coeffs.at[:, :, span(source, size)], here, sems.at[0, n]))
        loads[-1].start()
        stores.append(pltpu.make_async_copy(here, outs[n].at[:, :, span(0, size)], sems.at[1, n]))
        at += size
    if any(more for *_, more in cuts):
        occup = levels[...].astype(F32) / OCC_STEPS
        spread = jnp.broadcast_to(occup, (bands, bands))
        lane = lax.broadcasted_iota(jnp.int32, (bands, LANES - bands), 1)
        flags = jnp.zeros((bands, LANES - bands), F32)
        for d in range(REACH):
            flags = jnp.where(lane == d, pairs[0, d].astype(F32), flags)
        held[0, :, :LANES] = jnp.concatenate([spread.T, jnp.zeros_like(flags)], axis=1).astype(BF16)
        held[1, :, :LANES] = jnp.concatenate([spread, flags], axis=1).astype(BF16)
    facts = []
    for n, (_, _, size, more) in enumerate(cuts):
        if more:
            facts.append(pltpu.make_async_copy(held.at[:, :, span(0, 1)], outs[n].at[:, :, span(size * LANES, 1)], sems.at[2, n]))
            facts[-1].start()
    for load, store in zip(loads, stores):
        load.wait()
        store.start()
    for copy in stores + facts:
        copy.wait()


def pieces(cuts, info, levels, pairs, coeffs, name):
    bands = coeffs.shape[1]
    anywhere = pl.BlockSpec(memory_space=pl.ANY)
    return list(
        pl.pallas_call(
            functools.partial(pieces_body, cuts),
            in_specs=[
                pl.BlockSpec(memory_space=pltpu.SMEM),
                pl.BlockSpec(memory_space=pltpu.VMEM),
                pl.BlockSpec(memory_space=pltpu.SMEM),
                anywhere,
            ],
            out_specs=[anywhere] * len(cuts),
            out_shape=[jax.ShapeDtypeStruct((2, bands, (size + int(more)) * LANES), BF16) for _, _, size, more in cuts],
            scratch_shapes=[
                pltpu.VMEM((2, bands, (1 + sum(size for _, _, size, _ in cuts)) * LANES), BF16),
                pltpu.SemaphoreType.DMA((3, len(cuts))),
            ],
            compiler_params=pltpu.CompilerParams(vmem_limit_bytes=VMEM_BYTES),
            cost_estimate=pl.CostEstimate(flops=1000, bytes_accessed=1000, transcendentals=0),
            name=name,
        )(info, levels[None, :], pairs, coeffs)
    )


def final_body(info, diag, own, core, far, up_y, up_z, ring, out):
    bands = out.shape[2]
    first = info[0] == 1
    low = info[1] == 0
    wide = lambda tile: unpack(tile.astype(F32))
    received = [wide(up_y[i]) for i in range(3)]
    mine = own[...] + wide(core[0])
    near1 = jnp.where(first, mine, received[1] + wide(ring[...]))
    near2 = far[...] + received[0]
    away1 = jnp.where(first, received[1] + wide(ring[...]), mine)
    away2 = received[2] + wide(up_z[...])
    above = [jnp.where(low, near1, away1), jnp.where(low, near2, away2)]
    below = [jnp.where(low, away1, near1), jnp.where(low, away2, near2)]
    for a in range(3):
        for part in range(2):
            cut = lambda tile: tile[a * bands : (a + 1) * bands, part * bands : (part + 1) * bands]
            turn = lambda tile: -cut(tile).T if part == 0 else cut(tile).T
            out[a, part] = jnp.concatenate([turn(below[1]), turn(below[0]), cut(diag), cut(above[0]), cut(above[1])], axis=1)


def final(info, bands, *operands):
    vmem = pl.BlockSpec(memory_space=pltpu.VMEM)
    return pl.pallas_call(
        final_body,
        in_specs=[pl.BlockSpec(memory_space=pltpu.SMEM)] + [vmem] * len(operands),
        out_specs=vmem,
        out_shape=jax.ShapeDtypeStruct((3, 2, bands, SPAN * bands), F32),
        compiler_params=pltpu.CompilerParams(vmem_limit_bytes=VMEM_BYTES),
        name="final",
    )(info, *operands)


def routes(groups):
    at = lambda q, side, core: 4 * q + 2 * side + core
    first = lambda q, side: at(q, side, side)
    second = lambda q, side: at(q, side, 1 - side)
    away = lambda q, side: q + 1 - 2 * side
    both = [(q, side) for q in range(groups // 4) for side in (0, 1)]
    ok = [(q, s) for q, s in both if 0 <= away(q, s) < groups // 4]
    z = [(at(away(q, s), s, c), at(q, s, c)) for q, s in ok for c in (0, 1)]
    return dict(
        core=[(at(q, s, c), at(q, s, 1 - c)) for q, s in both for c in (0, 1)],
        y=[(at(q, s, c), at(q, 1 - s, c)) for q, s in both for c in (0, 1)],
        z=z,
        back=[(b, a) for a, b in z],
        forward=[(first(q, s), second(q, s)) for q, s in both],
        ring=[(first(q, s), second(q, s)) for q, s in both] + [(second(q, s), first(away(q, s), s)) for q, s in ok],
    )


def shards(coeffs, k_plus_g, pairs, levels):
    groups = lax.axis_size("blk")
    me = lax.axis_index("blk")
    bands, plane = coeffs.shape[1:]
    tiles = plane // 2 // LANES
    core = me % 2
    side = (me // 2) % 2
    info = jnp.stack([(core == side).astype(jnp.int32), side, core])
    way = routes(groups)
    send = lambda value, name: lax.ppermute(value, "blk", way[name])
    tie = lambda *arrays: lax.optimization_barrier(arrays)

    one, two = CHUNKS
    swapped = send(coeffs, "core")
    y_one, z_one, facts = pieces(
        [("y", 0, one, False), ("z", 0, one, False), ("y", 0, 0, True)], info, levels, pairs, coeffs, "one"
    )
    facts_core = [(send(facts, "core"), None, 0)]
    coeffs, y_one, z_one = tie(coeffs, y_one, z_one)
    got_z, got_y = [send(z_one, "z")], [send(y_one, "y")]
    y_two, z_two = pieces([("y", one, two, True), ("z", one, two, True)], info, levels, pairs, coeffs, "two")
    got_z.append(send(z_two, "z"))
    got_y.append(send(y_two, "y"))
    here = [(facts, None, 0)]

    coeffs, y_two, z_two = tie(coeffs, y_two, z_two)
    (diag,) = pair_sums("diag", info, k_plus_g, [[(coeffs, None, 0)]], 0, 2 * tiles, [here])
    diag, swapped, coeffs = tie(diag, swapped, coeffs)
    own, own_packed = pair_sums(
        "near", info, k_plus_g, [[(swapped, "core", 0)], [(coeffs, "core", 0)]], 0, tiles, [facts_core, here]
    )
    tile_own = send(own_packed, "core")
    got_y[0], got_z[0], own = tie(got_y[0], got_z[0], own)
    forward = [send(got_z[0], "forward")]
    (sums,) = pair_sums(
        "far", info, k_plus_g,
        [[(got_y[0], None, 0)], [(coeffs, "side", 0)], [(swapped, "first side", 0), (forward[0], "second", 0)], [(got_z[0], None, 0)]], 0, one,
    )
    got_y[1], got_z[1], sums = tie(got_y[1], got_z[1], sums)
    forward.append(send(got_z[1], "forward"))
    far, far_packed, far_1, far_2 = pair_sums(
        "far", info, k_plus_g,
        [[(got_y[1], None, 0)], [(coeffs, "side", one)], [(swapped, "first side", one), (forward[1], "second", 0)], [(got_z[1], None, 0)]],
        one, two,
        [[(got_y[1], None, two)], here, [(facts_core[0][0], "first", 0), (forward[1], "second", two)], [(got_z[1], None, two)]], sums,
    )
    tile_y = send(far_packed, "y")
    tile_z = send(far_2, "back")
    tile_ring = send(far_1, "ring")
    return final(info, bands, diag, own, tile_own, far, tile_y, tile_z, tile_ring)


def solution(mesh):
    in_specs = (
        P(None, ("snap", "blk"), None),
        P("snap", None),
        P(("snap", "blk"), None),
        P(("snap", "blk")),
    )
    out_specs = P(None, None, ("snap", "blk"), None)
    return jax.shard_map(shards, mesh=mesh, in_specs=in_specs, out_specs=out_specs, check_vma=False)
```

time: 159 us -> 92.7 us (0.58)
  waiting for transfers between devices: 99.9 us -> 28.5 us
  Pallas kernels: 0 us -> 40.4 us
  matrix products: 30.3 us -> 0 us
  other arithmetic: 7.83 us -> 0.58 us
  starting transfers between devices: 15.6 us -> 21.3 us
  local copies, waits for them, and re-layouts: 3.26 us -> 1.33 us
    ppermute x6 -> x12, waiting for transfers between devices: 99.9 us -> 28.5 us  [shards(): send = lambda value, name: lax.ppermute(value, 'blk', way[name])]
    pallas_call x0 -> x7, Pallas kernels: none -> 40.4 us  [the longest x4 29.5 us: pair_sums(): pl.pallas_call(functools.partial(pair_body, kind, begin, tiles, plans(blo...]
    dot_general x3 -> x0, matrix products: 30.3 us -> none  [pair_tile(): jnp.einsum('acnp,dmp->acdnm', weighted, partner, preferred_element_type=j...]
    convert_element_type x3 -> x0, other arithmetic: 6.72 us -> none  [the longest x1 6.71 us: shards(): weighted = (k_plus_g[:, None, None, :] * coeffs[None]).astype(jnp.bfloat16)]
    ppermute x6 -> x12, starting transfers between devices: 15.6 us -> 21.3 us  [shards(): send = lambda value, name: lax.ppermute(value, 'blk', way[name])]
  transfers between devices with their start and end apart: 6 -> 12, of which waited for: 4 -> 8; matrix products, arithmetic and copies ran while one was open for 25% -> 1% of each run, Pallas kernels for 0% -> 31%
where the time goes in v2:
time: 92.7 us; the launch traced here: 92.2 us
  Pallas kernels  40.4 us (44%)
  waiting for transfers between devices  28.5 us (31%)
  starting transfers between devices  21.3 us (23%)
  local copies, waits for them, and re-layouts  1.33 us (1%)
    pallas_call x4, Pallas kernels, pair_sums(): pl.pallas_call(functools.partial(pair_body, kind, begin, tiles, plans(blo...  29.5 us
    ppermute x12, waiting for transfers between devices, shards(): send = lambda value, name: lax.ppermute(value, 'blk', way[name])  28.5 us
    ppermute x12, starting transfers between devices, shards(): send = lambda value, name: lax.ppermute(value, 'blk', way[name])  21.3 us
    pallas_call x2, Pallas kernels, pieces(): pl.pallas_call(functools.partial(pieces_body, cuts), in_specs=[pl.BlockSp...  7.27 us
    pallas_call x1, Pallas kernels, final(): pl.pallas_call(final_body, in_specs=[pl.BlockSpec(memory_space=pltpu.SMEM...  3.62 us
  transfers between devices with their start and end apart: 12, of which 8 were waited for; matrix products, arithmetic and copies ran while one was open for 1% of the time, Pallas kernels for 31%

profile of v2, /device:TPU:0, one launch (start us, length us, event | category | flops | bytes accessed | tf_op | source)
XLA Modules:
  0.0 92.2 jit_solution(6984460227923365218)
XLA Ops:
  0.0 0.5 collective-permute-start
  0.5 0.6 pad_add_fusion.info
  1.0 3.6 %one.1 = (bf16[2,96,3072]{2,1,0:T(8,128)(2,1)}, bf16[2,96,3072]{2,1,0:T(8,128)(2,1)}, bf16[2,96,128]{2,1,0:T(8,128)(2,1)}) custom-call(s32[3]{0:T(128)} %pad_add_fusion.info, s32[1,96]{1,0:T(1,128)} %bitcast.4, s32[1,2]{1,0:T(1,128)} %pairs.3, bf16[2,96,12544]{2,1,0:T(8,128)(2,1)} %refs_1_.2), custom_call_target="tpu_custom_call" | custom-call | flops 1000 | bytes 1000 | tf_op jit(solution)/shard_map/one/pallas_call | solution.py:252
  4.6 0.0 copy-start.1
  4.6 2.6 %collective-permute-start.1 = (bf16[2,96,3072]{2,1,0:T(8,128)(2,1)}, bf16[2,96,3072]{2,1,0:T(8,128)(2,1)}, u32[]{:S(2)}, u32[]{:S(2)}) collective-permute-start(bf16[2,96,3072]{2,1,0:T(8,128)(2,1)} %get-tuple-element.37), channel_id=1, source_target_pairs={{0,2},{1,3},{2,0},{3,1},{4,6},{5,7},{6,4},{7,5},{8,10},{9,11},{10,... | collective-permute-start | bytes 3538952 | tf_op jit(solution)/shard_map/ppermute | solution.py:332
  7.2 1.3 %collective-permute-start.2 = (bf16[2,96,3072]{2,1,0:T(8,128)(2,1)}, bf16[2,96,3072]{2,1,0:T(8,128)(2,1)}, u32[]{:S(2)}, u32[]{:S(2)}) collective-permute-start(bf16[2,96,3072]{2,1,0:T(8,128)(2,1)} %get-tuple-element.38), channel_id=1, source_target_pairs={{4,0},{5,1},{8,4},{9,5},{2,6},{3,7},{12,8},{13,9},{6,10},{7,11},{1... | collective-permute-start | bytes 3538952 | tf_op jit(solution)/shard_map/ppermute | solution.py:332
  8.5 3.7 %two.1 = (bf16[2,96,3328]{2,1,0:T(8,128)(2,1)}, bf16[2,96,3328]{2,1,0:T(8,128)(2,1)}) custom-call(s32[3]{0:T(128)} %pad_add_fusion.info, s32[1,96]{1,0:T(1,128)} %bitcast.5, s32[1,2]{1,0:T(1,128)} %pairs.3, bf16[2,96,12544]{2,1,0:T(8,128)(2,1)} %refs_1_.2), custom_call_target="tpu_custom_call" | custom-call | flops 1000 | bytes 1000 | tf_op jit(solution)/shard_map/two/pallas_call | solution.py:252
  12.2 3.8 %collective-permute-start.5 = (bf16[2,96,3328]{2,1,0:T(8,128)(2,1)}, bf16[2,96,3328]{2,1,0:T(8,128)(2,1)S(1)}, u32[]{:S(2)}, u32[]{:S(2)}) collective-permute-start(bf16[2,96,3328]{2,1,0:T(8,128)(2,1)} %get-tuple-element.32), channel_id=1, source_target_pairs={{0,2},{1,3},{2,0},{3,1},{4,6},{5,7},{6,4},{7,5},{8,10},{9,11},{10,... | collective-permute-start | bytes 3833864 | tf_op jit(solution)/shard_map/ppermute | solution.py:332
  16.0 1.3 %collective-permute-start.6 = (bf16[2,96,3328]{2,1,0:T(8,128)(2,1)}, bf16[2,96,3328]{2,1,0:T(8,128)(2,1)}, u32[]{:S(2)}, u32[]{:S(2)}) collective-permute-start(bf16[2,96,3328]{2,1,0:T(8,128)(2,1)} %get-tuple-element.33), channel_id=1, source_target_pairs={{4,0},{5,1},{8,4},{9,5},{2,6},{3,7},{12,8},{13,9},{6,10},{7,11},{1... | collective-permute-start | bytes 3833864 | tf_op jit(solution)/shard_map/ppermute | solution.py:332
  17.3 0.0 collective-permute-done.refs_0_.refs_2_
  17.3 0.0 copy-done.1
  17.3 0.1 collective-permute-start.3
  17.4 7.9 %diag.1 = f32[288,192]{1,0:T(8,128)} custom-call(s32[3]{0:T(128)} %pad_add_fusion.info, f32[3,12544]{1,0:T(4,128)} %k_hbm.7, bf16[2,96,12544]{2,1,0:T(8,128)(2,1)} %refs_1_.2, bf16[2,96,128]{2,1,0:T(8,128)(2,1)} %get-tuple-element.35.refs_1_.refs_3_.refs_6_), custom_call_target="tpu_custom_call" | custom-call | flops 1000 | bytes 1000 | tf_op jit(solution)/shard_map/diag/pallas_call | solution.py:186
  25.3 0.0 collective-permute-done.3.refs_2_.refs_7_
  25.3 0.0 copy-start.3
  25.3 0.6 copy-done.3
  25.9 6.3 %near.1 = (f32[288,192]{1,0:T(8,128)}, bf16[1,432,128]{2,1,0:T(8,128)(2,1)}) custom-call(s32[3]{0:T(128)} %pad_add_fusion.info, f32[3,12544]{1,0:T(4,128)} %k_hbm.7, bf16[2,96,12544]{2,1,0:T(8,128)(2,1)} %collective-permute-done.refs_0_.refs_2_, bf16[2,96,12544]{2,1,0:T(8,128)(2,1)} %refs_1_.2, bf16[2,96,128]{2,1,0:T(8,128)(2,1)} %copy-done.3, ...), custom_call_target="tpu_custom_call" | custom-call | flops 1000 | bytes 1000 | tf_op jit(solution)/shard_map/near/pallas_call | solution.py:186
  32.2 2.1 %collective-permute-done.1.refs_0_ = bf16[2,96,3072]{2,1,0:T(8,128)(2,1)} collective-permute-done((bf16[2,96,3072]{2,1,0:T(8,128)(2,1)}, bf16[2,96,3072]{2,1,0:T(8,128)(2,1)}, u32[]{:S(2)}, u32[]{:S(2)}) %collective-permute-start.1) | collective-permute-done | bytes 1179680 | tf_op jit(solution)/shard_map/ppermute | solution.py:332
  34.4 3.9 %collective-permute-done.2.refs_4_ = bf16[2,96,3072]{2,1,0:T(8,128)(2,1)} collective-permute-done((bf16[2,96,3072]{2,1,0:T(8,128)(2,1)}, bf16[2,96,3072]{2,1,0:T(8,128)(2,1)}, u32[]{:S(2)}, u32[]{:S(2)}) %collective-permute-start.2) | collective-permute-done | bytes 1179680 | tf_op jit(solution)/shard_map/ppermute | solution.py:332
  38.2 2.3 %collective-permute-start.7 = (bf16[2,96,3072]{2,1,0:T(8,128)(2,1)}, bf16[2,96,3072]{2,1,0:T(8,128)(2,1)}, u32[]{:S(2)}, u32[]{:S(2)}) collective-permute-start(bf16[2,96,3072]{2,1,0:T(8,128)(2,1)} %collective-permute-done.2.refs_4_), channel_id=1, source_target_pairs={{0,1},{3,2},{4,5},{7,6},{8,9},{11,10},{12,13},{15,14},{16,17},{19,... | collective-permute-start | bytes 3538952 | tf_op jit(solution)/shard_map/ppermute | solution.py:332
  40.6 1.8 %collective-permute-done.7.refs_3_ = bf16[2,96,3072]{2,1,0:T(8,128)(2,1)} collective-permute-done((bf16[2,96,3072]{2,1,0:T(8,128)(2,1)}, bf16[2,96,3072]{2,1,0:T(8,128)(2,1)}, u32[]{:S(2)}, u32[]{:S(2)}) %collective-permute-start.7) | collective-permute-done | bytes 1179680 | tf_op jit(solution)/shard_map/ppermute | solution.py:332
  42.3 6.9 %far.2.refs_10_ = f32[3,288,192]{2,1,0:T(8,128)} custom-call(s32[3]{0:T(128)} %pad_add_fusion.info, f32[3,12544]{1,0:T(4,128)} %k_hbm.7, bf16[2,96,3072]{2,1,0:T(8,128)(2,1)} %collective-permute-done.1.refs_0_, bf16[2,96,12544]{2,1,0:T(8,128)(2,1)} %refs_1_.2, bf16[2,96,12544]{2,1,0:T(8,128)(2,1)} %collective-permute-done.refs_0_.refs_2_, ...), custom_call_target="tpu_custom_call" | custom-call | flops 1000 | bytes 1000 | tf_op jit(solution)/shard_map/far/pallas_call | solution.py:186
  49.3 0.0 copy-start.7
  49.3 12.2 %collective-permute-done.5.refs_0_.refs_5_ = bf16[2,96,3328]{2,1,0:T(8,128)(2,1)S(1)} collective-permute-done((bf16[2,96,3328]{2,1,0:T(8,128)(2,1)}, bf16[2,96,3328]{2,1,0:T(8,128)(2,1)S(1)}, u32[]{:S(2)}, u32[]{:S(2)}) %collective-permute-start.5) | collective-permute-done | bytes 1277984 | tf_op jit(solution)/shard_map/ppermute | solution.py:332
  61.5 0.0 copy-start
  61.5 3.4 %collective-permute-done.6.refs_4_.refs_9_ = bf16[2,96,3328]{2,1,0:T(8,128)(2,1)} collective-permute-done((bf16[2,96,3328]{2,1,0:T(8,128)(2,1)}, bf16[2,96,3328]{2,1,0:T(8,128)(2,1)}, u32[]{:S(2)}, u32[]{:S(2)}) %collective-permute-start.6) | collective-permute-done | bytes 1277984 | tf_op jit(solution)/shard_map/ppermute | solution.py:332
  64.9 2.4 %collective-permute-start.8 = (bf16[2,96,3328]{2,1,0:T(8,128)(2,1)}, bf16[2,96,3328]{2,1,0:T(8,128)(2,1)}, u32[]{:S(2)}, u32[]{:S(2)}) collective-permute-start(bf16[2,96,3328]{2,1,0:T(8,128)(2,1)} %collective-permute-done.6.refs_4_.refs_9_), channel_id=1, source_target_pairs={{0,1},{3,2},{4,5},{7,6},{8,9},{11,10},{12,13},{15,14},{16,17},{19,... | collective-permute-start | bytes 3833864 | tf_op jit(solution)/shard_map/ppermute | solution.py:332
  67.3 1.9 %collective-permute-done.8.refs_3_.refs_8_ = bf16[2,96,3328]{2,1,0:T(8,128)(2,1)} collective-permute-done((bf16[2,96,3328]{2,1,0:T(8,128)(2,1)}, bf16[2,96,3328]{2,1,0:T(8,128)(2,1)}, u32[]{:S(2)}, u32[]{:S(2)}) %collective-permute-start.8) | collective-permute-done | bytes 1277984 | tf_op jit(solution)/shard_map/ppermute | solution.py:332
  69.2 0.0 copy-done
  69.2 8.4 %far.3 = (f32[288,192]{1,0:T(8,128)}, bf16[3,432,128]{2,1,0:T(8,128)(2,1)}, bf16[432,128]{1,0:T(8,128)(2,1)}, bf16[432,128]{1,0:T(8,128)(2,1)}) custom-call(s32[3]{0:T(128)} %pad_add_fusion.info, f32[3,12544]{1,0:T(4,128)} %k_hbm.7, bf16[2,96,3328]{2,1,0:T(8,128)(2,1)} %copy-done, bf16[2,96,12544]{2,1,0:T(8,128)(2,1)} %refs_1_.2, ...), custom_call_target="tpu_custom_call" | custom-call | flops 1000 | bytes 1000 | tf_op jit(solution)/shard_map/far/pallas_call | solution.py:186
  77.5 0.6 collective-permute-start.9
  78.2 0.0 copy-done.7
  78.2 0.0 collective-permute-start.4
  78.2 4.4 %collective-permute-start.10 = (bf16[432,128]{1,0:T(8,128)(2,1)}, bf16[432,128]{1,0:T(8,128)(2,1)S(1)}, u32[]{:S(2)}, u32[]{:S(2)}) collective-permute-start(bf16[432,128]{1,0:T(8,128)(2,1)} %get-tuple-element.51), channel_id=1, source_target_pairs={{0,4},{1,5},{4,8},{5,9},{6,2},{7,3},{8,12},{9,13},{10,6},{11,7},{1... | collective-permute-start | bytes 331784 | tf_op jit(solution)/shard_map/ppermute | solution.py:332
  82.6 2.1 %collective-permute-start.11 = (bf16[432,128]{1,0:T(8,128)(2,1)}, bf16[432,128]{1,0:T(8,128)(2,1)S(1)}, u32[]{:S(2)}, u32[]{:S(2)}) collective-permute-start(bf16[432,128]{1,0:T(8,128)(2,1)} %get-tuple-element.52), channel_id=1, source_target_pairs={{0,1},{3,2},{4,5},{7,6},{8,9},{11,10},{12,13},{15,14},{1,4},{5,8},... | collective-permute-start | bytes 331784 | tf_op jit(solution)/shard_map/ppermute | solution.py:332
  84.7 0.0 collective-permute-done.4.core
  84.7 0.0 copy-start.4
  84.7 1.1 %collective-permute-done.10.up_z = bf16[432,128]{1,0:T(8,128)(2,1)S(1)} collective-permute-done((bf16[432,128]{1,0:T(8,128)(2,1)}, bf16[432,128]{1,0:T(8,128)(2,1)S(1)}, u32[]{:S(2)}, u32[]{:S(2)}) %collective-permute-start.10) | collective-permute-done | bytes 110624 | tf_op jit(solution)/shard_map/ppermute | solution.py:332
  85.8 0.0 copy-start.5
  85.8 0.0 collective-permute-done.11.ring
  85.8 0.0 copy-start.6
  85.9 2.0 %collective-permute-done.9.up_y = bf16[3,432,128]{2,1,0:T(8,128)(2,1)S(1)} collective-permute-done((bf16[3,432,128]{2,1,0:T(8,128)(2,1)}, bf16[3,432,128]{2,1,0:T(8,128)(2,1)S(1)}, u32[]{:S(2)}, u32[]{:S(2)}) %collective-permute-start.9) | collective-permute-done | bytes 331808 | tf_op jit(solution)/shard_map/ppermute | solution.py:332
  87.9 0.0 copy-start.2
  87.9 0.0 copy-done.4
  87.9 0.0 copy-done.5
  87.9 0.0 copy-done.6
  87.9 0.7 copy-done.2
  88.6 3.6 %final.1 = f32[3,2,96,480]{3,2,1,0:T(8,128)} custom-call(s32[3]{0:T(128)} %pad_add_fusion.info, f32[288,192]{1,0:T(8,128)} %diag.1, f32[288,192]{1,0:T(8,128)} %get-tuple-element.42.own, bf16[1,432,128]{2,1,0:T(8,128)(2,1)} %copy-done.4, f32[288,192]{1,0:T(8,128)} %get-tuple-element.49.far, bf16[3,432,128]{2,1,0:T(8,128)(2,1)} %copy-done.2, ...), custom_call_target="tpu_custom_call" | custom-call | tf_op jit(solution)/shard_map/final/pallas_call | solution.py:295
Async XLA Ops:
  0.0 17.3 %collective-permute-start = (bf16[2,96,12544]{2,1,0:T(8,128)(2,1)}, bf16[2,96,12544]{2,1,0:T(8,128)(2,1)}, u32[]{:S(2)}, u32[]{:S(2)}) collective-permute-start(bf16[2,96,12544]{2,1,0:T(8,128)(2,1)} %refs_1_.2), channel_id=1, source_target_pairs={{0,1},{1,0},{2,3},{3,2},{4,5},{5,4},{6,7},{7,6},{8,9},{9,8},{10,11... | collective-permute-start | bytes 14450696 | tf_op jit(solution)/shard_map/ppermute | solution.py:332
  4.6 12.6 %copy-start.1 = (bf16[2,96,128]{2,1,0:T(8,128)(2,1)S(1)}, bf16[2,96,128]{2,1,0:T(8,128)(2,1)}, u32[]{:S(2)}) copy-start(bf16[2,96,128]{2,1,0:T(8,128)(2,1)} %get-tuple-element.35.refs_1_.refs_3_.refs_6_) | copy-start | bytes 147460
  4.6 29.7 %collective-permute-start.1 = (bf16[2,96,3072]{2,1,0:T(8,128)(2,1)}, bf16[2,96,3072]{2,1,0:T(8,128)(2,1)}, u32[]{:S(2)}, u32[]{:S(2)}) collective-permute-start(bf16[2,96,3072]{2,1,0:T(8,128)(2,1)} %get-tuple-element.37), channel_id=1, source_target_pairs={{0,2},{1,3},{2,0},{3,1},{4,6},{5,7},{6,4},{7,5},{8,10},{9,11},{10,... | collective-permute-start | bytes 3538952 | tf_op jit(solution)/shard_map/ppermute | solution.py:332
  7.2 31.0 %collective-permute-start.2 = (bf16[2,96,3072]{2,1,0:T(8,128)(2,1)}, bf16[2,96,3072]{2,1,0:T(8,128)(2,1)}, u32[]{:S(2)}, u32[]{:S(2)}) collective-permute-start(bf16[2,96,3072]{2,1,0:T(8,128)(2,1)} %get-tuple-element.38), channel_id=1, source_target_pairs={{4,0},{5,1},{8,4},{9,5},{2,6},{3,7},{12,8},{13,9},{6,10},{7,11},{1... | collective-permute-start | bytes 3538952 | tf_op jit(solution)/shard_map/ppermute | solution.py:332
  12.2 49.3 %collective-permute-start.5 = (bf16[2,96,3328]{2,1,0:T(8,128)(2,1)}, bf16[2,96,3328]{2,1,0:T(8,128)(2,1)S(1)}, u32[]{:S(2)}, u32[]{:S(2)}) collective-permute-start(bf16[2,96,3328]{2,1,0:T(8,128)(2,1)} %get-tuple-element.32), channel_id=1, source_target_pairs={{0,2},{1,3},{2,0},{3,1},{4,6},{5,7},{6,4},{7,5},{8,10},{9,11},{10,... | collective-permute-start | bytes 3833864 | tf_op jit(solution)/shard_map/ppermute | solution.py:332
  16.0 48.9 %collective-permute-start.6 = (bf16[2,96,3328]{2,1,0:T(8,128)(2,1)}, bf16[2,96,3328]{2,1,0:T(8,128)(2,1)}, u32[]{:S(2)}, u32[]{:S(2)}) collective-permute-start(bf16[2,96,3328]{2,1,0:T(8,128)(2,1)} %get-tuple-element.33), channel_id=1, source_target_pairs={{4,0},{5,1},{8,4},{9,5},{2,6},{3,7},{12,8},{13,9},{6,10},{7,11},{1... | collective-permute-start | bytes 3833864 | tf_op jit(solution)/shard_map/ppermute | solution.py:332
  17.3 8.0 %collective-permute-start.3 = (bf16[2,96,128]{2,1,0:T(8,128)(2,1)S(1)}, bf16[2,96,128]{2,1,0:T(8,128)(2,1)S(1)}, u32[]{:S(2)}, u32[]{:S(2)}) collective-permute-start(bf16[2,96,128]{2,1,0:T(8,128)(2,1)S(1)} %copy-done.1), channel_id=1, source_target_pairs={{0,1},{1,0},{2,3},{3,2},{4,5},{5,4},{6,7},{7,6},{8,9},{9,8},{10,11... | collective-permute-start | bytes 147464 | tf_op jit(solution)/shard_map/ppermute | solution.py:332
  25.3 0.6 copy-start.3
  38.2 4.1 %collective-permute-start.7 = (bf16[2,96,3072]{2,1,0:T(8,128)(2,1)}, bf16[2,96,3072]{2,1,0:T(8,128)(2,1)}, u32[]{:S(2)}, u32[]{:S(2)}) collective-permute-start(bf16[2,96,3072]{2,1,0:T(8,128)(2,1)} %collective-permute-done.2.refs_4_), channel_id=1, source_target_pairs={{0,1},{3,2},{4,5},{7,6},{8,9},{11,10},{12,13},{15,14},{16,17},{19,... | collective-permute-start | bytes 3538952 | tf_op jit(solution)/shard_map/ppermute | solution.py:332
  49.3 28.9 %copy-start.7 = (bf16[1,432,128]{2,1,0:T(8,128)(2,1)S(1)}, bf16[1,432,128]{2,1,0:T(8,128)(2,1)}, u32[]{:S(2)}) copy-start(bf16[1,432,128]{2,1,0:T(8,128)(2,1)} %get-tuple-element.43) | copy-start | bytes 331780
  61.5 7.7 %copy-start = (bf16[2,96,3328]{2,1,0:T(8,128)(2,1)}, bf16[2,96,3328]{2,1,0:T(8,128)(2,1)S(1)}, u32[]{:S(2)}) copy-start(bf16[2,96,3328]{2,1,0:T(8,128)(2,1)S(1)} %collective-permute-done.5.refs_0_.refs_5_) | copy-start | bytes 3833860
  64.9 4.2 %collective-permute-start.8 = (bf16[2,96,3328]{2,1,0:T(8,128)(2,1)}, bf16[2,96,3328]{2,1,0:T(8,128)(2,1)}, u32[]{:S(2)}, u32[]{:S(2)}) collective-permute-start(bf16[2,96,3328]{2,1,0:T(8,128)(2,1)} %collective-permute-done.6.refs_4_.refs_9_), channel_id=1, source_target_pairs={{0,1},{3,2},{4,5},{7,6},{8,9},{11,10},{12,13},{15,14},{16,17},{19,... | collective-permute-start | bytes 3833864 | tf_op jit(solution)/shard_map/ppermute | solution.py:332
  77.5 10.3 %collective-permute-start.9 = (bf16[3,432,128]{2,1,0:T(8,128)(2,1)}, bf16[3,432,128]{2,1,0:T(8,128)(2,1)S(1)}, u32[]{:S(2)}, u32[]{:S(2)}) collective-permute-start(bf16[3,432,128]{2,1,0:T(8,128)(2,1)} %get-tuple-element.50), channel_id=1, source_target_pairs={{0,2},{1,3},{2,0},{3,1},{4,6},{5,7},{6,4},{7,5},{8,10},{9,11},{10,... | collective-permute-start | bytes 995336 | tf_op jit(solution)/shard_map/ppermute | solution.py:332
  78.2 6.5 %collective-permute-start.4 = (bf16[1,432,128]{2,1,0:T(8,128)(2,1)S(1)}, bf16[1,432,128]{2,1,0:T(8,128)(2,1)S(1)}, u32[]{:S(2)}, u32[]{:S(2)}) collective-permute-start(bf16[1,432,128]{2,1,0:T(8,128)(2,1)S(1)} %copy-done.7), channel_id=1, source_target_pairs={{0,1},{1,0},{2,3},{3,2},{4,5},{5,4},{6,7},{7,6},{8,9},{9,8},{10,11... | collective-permute-start | bytes 331784 | tf_op jit(solution)/shard_map/ppermute | solution.py:332
  78.2 7.7 %collective-permute-start.10 = (bf16[432,128]{1,0:T(8,128)(2,1)}, bf16[432,128]{1,0:T(8,128)(2,1)S(1)}, u32[]{:S(2)}, u32[]{:S(2)}) collective-permute-start(bf16[432,128]{1,0:T(8,128)(2,1)} %get-tuple-element.51), channel_id=1, source_target_pairs={{0,4},{1,5},{4,8},{5,9},{6,2},{7,3},{8,12},{9,13},{10,6},{11,7},{1... | collective-permute-start | bytes 331784 | tf_op jit(solution)/shard_map/ppermute | solution.py:332
  82.6 3.3 %collective-permute-start.11 = (bf16[432,128]{1,0:T(8,128)(2,1)}, bf16[432,128]{1,0:T(8,128)(2,1)S(1)}, u32[]{:S(2)}, u32[]{:S(2)}) collective-permute-start(bf16[432,128]{1,0:T(8,128)(2,1)} %get-tuple-element.52), channel_id=1, source_target_pairs={{0,1},{3,2},{4,5},{7,6},{8,9},{11,10},{12,13},{15,14},{1,4},{5,8},... | collective-permute-start | bytes 331784 | tf_op jit(solution)/shard_map/ppermute | solution.py:332
  84.7 3.2 %copy-start.4 = (bf16[1,432,128]{2,1,0:T(8,128)(2,1)}, bf16[1,432,128]{2,1,0:T(8,128)(2,1)S(1)}, u32[]{:S(2)}) copy-start(bf16[1,432,128]{2,1,0:T(8,128)(2,1)S(1)} %collective-permute-done.4.core) | copy-start | bytes 331780
  85.8 2.0 %copy-start.5 = (bf16[432,128]{1,0:T(8,128)(2,1)}, bf16[432,128]{1,0:T(8,128)(2,1)S(1)}, u32[]{:S(2)}) copy-start(bf16[432,128]{1,0:T(8,128)(2,1)S(1)} %collective-permute-done.10.up_z) | copy-start | bytes 331780
  85.8 2.0 %copy-start.6 = (bf16[432,128]{1,0:T(8,128)(2,1)}, bf16[432,128]{1,0:T(8,128)(2,1)S(1)}, u32[]{:S(2)}) copy-start(bf16[432,128]{1,0:T(8,128)(2,1)S(1)} %collective-permute-done.11.ring) | copy-start | bytes 331780
  87.9 0.7 copy-start.2

commit v3 on v2

--- a/solution.py
+++ b/solution.py
@@ -15,7 +15,7 @@
 CHUNKS = (24, 25)
 F32 = jnp.float32
 BF16 = jnp.bfloat16
-VMEM_BYTES = 62 * 2**20
+VMEM_BYTES = 64 * 2**20
 
 
 def product(k, low, high):
@@ -36,7 +36,6 @@
     else:
         flag = jnp.where(offset == 1, low[1, 0:1, bands : bands + 1], low[1, 0:1, bands + 1 : bands + 2])
     weights = (low[0][:, :bands] - high[1][:, :bands]) * (flag * scale)
-    weights = jnp.concatenate([weights] * 3, axis=0)
     return jnp.concatenate([weights, weights], axis=1)
 
 
@@ -59,10 +58,11 @@
 def roles(kind, info):
     first, side, core = info[0], info[1], info[2]
     if kind == "diag":
-        return 0, (0,)
+        return 0, ((0, 0),)
     if kind == "near":
-        return core, (1 - core,)
-    return side, (1 - side, jnp.where(first == 1, 1 - side, side), side)
+        return core, ((1 - core, core),)
+    pairs = ((1, 0), (jnp.where(first == 1, 3, 1), jnp.where(first == 1, 2, 3)), (0, 2))
+    return side, tuple((jnp.where(side == 0, low, high), jnp.where(side == 0, high, low)) for low, high in pairs)
 
 
 def pick(values, i):
@@ -75,15 +75,15 @@
 def pair_body(kind, first_tile, tiles, plans, facts_plans, has_start, scale, info, k_hbm, *refs):
     offsets = OFFSETS[kind]
     count, blocks = len(offsets), len(plans)
-    half, others = roles(kind, info)
+    half, pairs = roles(kind, info)
     ends = facts_plans is not None
     refs = list(refs)
     take = lambda number: [refs.pop(0) for _ in range(number)]
     sources = [take(len(plan)) for plan in plans]
     facts_sources = [take(len(plan)) for plan in facts_plans] if ends else []
     start_hbm = take(1)[0] if has_start else None
-    outs = take(len(refs) - 9)
-    k_held, held, facts, start, acc, sems, k_sem, facts_sems, start_sem = refs
+    outs = take(len(refs) - 10)
+    k_held, held, facts, weights, start, acc, sems, k_sem, facts_sems, start_sem = refs
 
     half_tiles = k_hbm.shape[1] // 2 // LANES
     first = half * half_tiles + first_tile
@@ -114,33 +114,37 @@
             later += copies(facts_plans[b], facts_sources[b], facts.at[b], 1, facts_sems.at[b])
     if has_start:
         later.append((None, pltpu.make_async_copy(start_hbm, start, start_sem)))
+    begin(later)
     k_copy.start()
     for load in loads[:2]:
         begin(load)
-    begin(later)
+
+    def order(i):
+        return tuple(pick([pair[n] for pair in pairs], i) for n in (0, 1))
+
+    wait(later)
+    if ends:
+        @pl.loop(0, count)
+        def _(i):
+            low, high = order(i)
+            weights[i] = weights_of(facts[low], facts[high], 0 if kind == "diag" else pick(offsets, i), scale)
+
     k_copy.wait()
     wait(loads[0])
 
-    def order(i):
-        if kind == "diag":
-            return 0, 0
-        other = pick(others, i) == 1
-        return jnp.where(other, i + 1, 0), jnp.where(other, 0, i + 1)
-
     @pl.loop(0, count)
-    def _(i):
+    def _(step):
         for j in range(1, blocks):
-            @pl.when(i == j - 1)
+            @pl.when(step == j - 1)
             def _():
                 wait(loads[j])
                 if j == 1:
                     for load in loads[2:]:
                         begin(load)
 
+        i = pick((0, 2, 1), step) if count == 3 else step
         low, high = order(i)
         acc[i] = product(k_held[...], held[low], held[high])
-
-    wait(later)
 
     @pl.loop(0, count)
     def _(i):
@@ -150,20 +154,30 @@
         if not ends:
             outs[0][i] = tile
             return
-        low, high = order(i)
-        tile = tile * weights_of(facts[low], facts[high], 0 if kind == "diag" else pick(offsets, i), scale)
-
-        @pl.when(i == 0)
-        def _():
+        tile = tile * jnp.concatenate([weights[i]] * 3, axis=0)
+        if count == 1:
             outs[0][...] = tile
-
-        if len(outs) > 1:
+        else:
+            @pl.when(i < 2)
+            def _():
+                outs[0][i] = tile
+
+        if kind == "near":
+            outs[1][...] = pack(tile).astype(BF16)
+        if kind == "far":
             packed = pack(tile).astype(BF16)
-            outs[1][i] = packed
-        for j in range(2, len(outs)):
-            @pl.when(i == j - 1)
+
+            @pl.when(i != 1)
             def _():
-                outs[j][...] = packed
+                outs[1][i // 2] = packed
+
+            @pl.when(i > 0)
+            def _():
+                outs[2][i - 1] = packed
+
+            @pl.when(i == 1)
+            def _():
+                outs[3][...] = packed
 
 
 def pair_sums(kind, info, k, blocks, begin, tiles, facts=None, start=None):
@@ -174,26 +188,27 @@
     arrays = lambda blocks: [part[0] for block in blocks for part in block]
     plans = lambda blocks: tuple(tuple((part[1], part[2]) for part in block) for block in blocks)
     operands = [k] + arrays(blocks) + arrays(facts or []) + ([] if start is None else [start])
+    tile = shape[1:]
     packed = (9 * bands // 2, LANES)
     if not ends:
         out_shape = [jax.ShapeDtypeStruct(shape, F32)]
+    elif kind == "far":
+        out_shape = [jax.ShapeDtypeStruct((2, *tile), F32)] + [jax.ShapeDtypeStruct((2, *packed), BF16)] * 2
+        out_shape.append(jax.ShapeDtypeStruct(packed, BF16))
     else:
-        out_shape = [jax.ShapeDtypeStruct(shape[1:], F32)]
-        if kind != "diag":
-            out_shape.append(jax.ShapeDtypeStruct((count, *packed), BF16))
-        if count == 3:
-            out_shape += [jax.ShapeDtypeStruct(packed, BF16)] * 2
+        out_shape = [jax.ShapeDtypeStruct(tile, F32)] + [jax.ShapeDtypeStruct(packed, BF16)] * (kind == "near")
     return pl.pallas_call(
         functools.partial(
             pair_body, kind, begin, tiles, plans(blocks), plans(facts) if ends else None, start is not None, 1.0 / math.sqrt(k.shape[1])
         ),
-        in_specs=[pl.BlockSpec(memory_space=pltpu.SMEM)] + [pl.BlockSpec(memory_space=pl.ANY)] * len(operands),
+        in_specs=[pl.BlockSpec(memory_space=pltpu.SMEM)] + [pl.BlockSpec(memory_space=pltpu.HBM)] * len(operands),
         out_specs=[pl.BlockSpec(memory_space=pltpu.VMEM)] * len(out_shape),
         out_shape=out_shape,
         scratch_shapes=[
             pltpu.VMEM((k.shape[0], tiles * LANES), F32),
             pltpu.VMEM((len(blocks), 2, bands, tiles * LANES), BF16),
             pltpu.VMEM((len(blocks), 2, bands, LANES), BF16),
+            pltpu.VMEM((count, bands, 2 * bands), F32),
             pltpu.VMEM(shape, F32),
             pltpu.VMEM(shape, F32),
             pltpu.SemaphoreType.DMA((len(blocks), 2)),
@@ -205,6 +220,22 @@
         cost_estimate=pl.CostEstimate(flops=1000, bytes_accessed=1000, transcendentals=0),
         name=kind,
     )(info, *operands)
+
+
+def mark_body(*refs):
+    refs[-1][...] = jnp.zeros_like(refs[-1])
+
+
+def mark(*arrays):
+    return pl.pallas_call(
+        mark_body,
+        in_specs=[pl.BlockSpec(memory_space=pltpu.HBM)] * len(arrays),
+        out_specs=pl.BlockSpec(memory_space=pltpu.VMEM),
+        out_shape=jax.ShapeDtypeStruct((8, LANES), F32),
+        compiler_params=pltpu.CompilerParams(vmem_limit_bytes=VMEM_BYTES),
+        cost_estimate=pl.CostEstimate(flops=10**12, bytes_accessed=1000, transcendentals=0),
+        name="mark",
+    )(*arrays)
 
 
 def pieces_body(cuts, info, levels, pairs, coeffs, *refs):
@@ -247,7 +278,7 @@
 
 def pieces(cuts, info, levels, pairs, coeffs, name):
     bands = coeffs.shape[1]
-    anywhere = pl.BlockSpec(memory_space=pl.ANY)
+    anywhere = pl.BlockSpec(memory_space=pltpu.HBM)
     return list(
         pl.pallas_call(
             functools.partial(pieces_body, cuts),
@@ -270,17 +301,17 @@
     )
 
 
-def final_body(info, diag, own, core, far, up_y, up_z, ring, out):
+def final_body(info, diag, own, core, far, up_z, across, up_y, marked, out):
     bands = out.shape[2]
     first = info[0] == 1
     low = info[1] == 0
     wide = lambda tile: unpack(tile.astype(F32))
-    received = [wide(up_y[i]) for i in range(3)]
-    mine = own[...] + wide(core[0])
-    near1 = jnp.where(first, mine, received[1] + wide(ring[...]))
-    near2 = far[...] + received[0]
-    away1 = jnp.where(first, received[1] + wide(ring[...]), mine)
-    away2 = received[2] + wide(up_z[...])
+    mine = own[...] + wide(core[...])
+    middle = wide(across[...])
+    near1 = jnp.where(first, mine, far[1] + middle)
+    near2 = far[0] + wide(up_y[0])
+    away1 = jnp.where(first, middle + wide(up_z[0]), mine)
+    away2 = wide(up_y[1]) + wide(up_z[1])
     above = [jnp.where(low, near1, away1), jnp.where(low, near2, away2)]
     below = [jnp.where(low, away1, near1), jnp.where(low, away2, near2)]
     for a in range(3):
@@ -304,8 +335,6 @@
 
 def routes(groups):
     at = lambda q, side, core: 4 * q + 2 * side + core
-    first = lambda q, side: at(q, side, side)
-    second = lambda q, side: at(q, side, 1 - side)
     away = lambda q, side: q + 1 - 2 * side
     both = [(q, side) for q in range(groups // 4) for side in (0, 1)]
     ok = [(q, s) for q, s in both if 0 <= away(q, s) < groups // 4]
@@ -315,8 +344,7 @@
         y=[(at(q, s, c), at(q, 1 - s, c)) for q, s in both for c in (0, 1)],
         z=z,
         back=[(b, a) for a, b in z],
-        forward=[(first(q, s), second(q, s)) for q, s in both],
-        ring=[(first(q, s), second(q, s)) for q, s in both] + [(second(q, s), first(away(q, s), s)) for q, s in ok],
+        across=[(at(q, s, c), at(q, 1 - s, 1 - c)) for q, s in both for c in (0, 1)],
     )
 
 
@@ -353,23 +381,22 @@
     )
     tile_own = send(own_packed, "core")
     got_y[0], got_z[0], own = tie(got_y[0], got_z[0], own)
-    forward = [send(got_z[0], "forward")]
+    other = [send(got_y[0], "core")]
     (sums,) = pair_sums(
-        "far", info, k_plus_g,
-        [[(got_y[0], None, 0)], [(coeffs, "side", 0)], [(swapped, "first side", 0), (forward[0], "second", 0)], [(got_z[0], None, 0)]], 0, one,
-    )
-    got_y[1], got_z[1], sums = tie(got_y[1], got_z[1], sums)
-    forward.append(send(got_z[1], "forward"))
-    far, far_packed, far_1, far_2 = pair_sums(
-        "far", info, k_plus_g,
-        [[(got_y[1], None, 0)], [(coeffs, "side", one)], [(swapped, "first side", one), (forward[1], "second", 0)], [(got_z[1], None, 0)]],
-        one, two,
-        [[(got_y[1], None, two)], here, [(facts_core[0][0], "first", 0), (forward[1], "second", two)], [(got_z[1], None, two)]], sums,
-    )
-    tile_y = send(far_packed, "y")
-    tile_z = send(far_2, "back")
-    tile_ring = send(far_1, "ring")
-    return final(info, bands, diag, own, tile_own, far, tile_y, tile_z, tile_ring)
+        "far", info, k_plus_g, [[(got_y[0], None, 0)], [(coeffs, "side", 0)], [(got_z[0], None, 0)], [(other[0], None, 0)]], 0, one
+    )
+    got_y[1], sums, tile_own = tie(got_y[1], sums, tile_own)
+    other.append(send(got_y[1], "core"))
+    marked = mark(got_z[1])
+    other[1], marked = tie(other[1], marked)
+    far, pairs_02, pairs_12, pair_1 = pair_sums(
+        "far", info, k_plus_g, [[(got_y[1], None, 0)], [(coeffs, "side", one)], [(got_z[1], None, 0)], [(other[1], None, 0)]], one, two,
+        [[(got_y[1], None, two)], here, [(got_z[1], None, two)], [(other[1], None, two)]], sums,
+    )
+    tile_y = send(pairs_02, "y")
+    tile_across = send(pair_1, "across")
+    tile_z = send(pairs_12, "back")
+    return final(info, bands, diag, own, tile_own, far, tile_z, tile_across, tile_y, marked)
 
 
 def solution(mesh):

time: 92.7 us -> 89 us (0.960)
  starting transfers between devices: 21.3 us -> 15.3 us
  waiting for transfers between devices: 28.5 us -> 31.5 us
  local copies, waits for them, and re-layouts: 1.33 us -> 0 us
    ppermute x12, starting transfers between devices: 21.3 us -> 15.3 us  [shards(): send = lambda value, name: lax.ppermute(value, 'blk', way[name])]
    ppermute x12, waiting for transfers between devices: 28.5 us -> 31.5 us  [shards(): send = lambda value, name: lax.ppermute(value, 'blk', way[name])]
    unnamed x16 -> x0, local copies, waits for them, and re-layouts: 1.33 us -> none
  transfers between devices with their start and end apart: 12 -> 12, of which waited for: 8 -> 6; matrix products, arithmetic and copies ran while one was open for 1% -> 1% of each run, Pallas kernels for 31% -> 33%
where the time goes in v3:
time: 89 us; the launch traced here: 88.6 us
  Pallas kernels  41 us (46%)
  waiting for transfers between devices  31.5 us (35%)
  starting transfers between devices  15.3 us (17%)
    ppermute x12, waiting for transfers between devices, shards(): send = lambda value, name: lax.ppermute(value, 'blk', way[name])  31.5 us
    pallas_call x4, Pallas kernels, pair_sums(): pl.pallas_call(functools.partial(pair_body, kind, begin, tiles, plans(blo...  29.4 us
    ppermute x12, starting transfers between devices, shards(): send = lambda value, name: lax.ppermute(value, 'blk', way[name])  15.3 us
    pallas_call x2, Pallas kernels, pieces(): pl.pallas_call(functools.partial(pieces_body, cuts), in_specs=[pl.BlockSp...  7.35 us
    pallas_call x1, Pallas kernels, final(): pl.pallas_call(final_body, in_specs=[pl.BlockSpec(memory_space=pltpu.SMEM...  3.72 us
  transfers between devices with their start and end apart: 12, of which 6 were waited for; matrix products, arithmetic and copies ran while one was open for 1% of the time, Pallas kernels for 33%

profile of v3, /device:TPU:0, one launch (start us, length us, event | category | flops | bytes accessed | tf_op | source)
XLA Modules:
  0.0 88.6 jit_solution(17869682801327160419)
XLA Ops:
  0.0 0.5 collective-permute-start
  0.5 0.7 pad_add_fusion.info
  1.1 3.6 %one.1 = (bf16[2,96,3072]{2,1,0:T(8,128)(2,1)}, bf16[2,96,3072]{2,1,0:T(8,128)(2,1)}, bf16[2,96,128]{2,1,0:T(8,128)(2,1)}) custom-call(s32[3]{0:T(128)} %pad_add_fusion.info, s32[1,96]{1,0:T(1,128)} %bitcast.4, s32[1,2]{1,0:T(1,128)} %pairs.3, bf16[2,96,12544]{2,1,0:T(8,128)(2,1)} %refs_1_.2), custom_call_target="tpu_custom_call" | custom-call | flops 1000 | bytes 1000 | tf_op jit(solution)/shard_map/one/pallas_call | solution.py:283
  4.8 2.6 %collective-permute-start.1 = (bf16[2,96,3072]{2,1,0:T(8,128)(2,1)}, bf16[2,96,3072]{2,1,0:T(8,128)(2,1)}, u32[]{:S(2)}, u32[]{:S(2)}) collective-permute-start(bf16[2,96,3072]{2,1,0:T(8,128)(2,1)} %get-tuple-element.39), channel_id=1, source_target_pairs={{0,2},{1,3},{2,0},{3,1},{4,6},{5,7},{6,4},{7,5},{8,10},{9,11},{10,... | collective-permute-start | bytes 3538952 | tf_op jit(solution)/shard_map/ppermute | solution.py:360
  7.3 1.3 %collective-permute-start.2 = (bf16[2,96,3072]{2,1,0:T(8,128)(2,1)}, bf16[2,96,3072]{2,1,0:T(8,128)(2,1)}, u32[]{:S(2)}, u32[]{:S(2)}) collective-permute-start(bf16[2,96,3072]{2,1,0:T(8,128)(2,1)} %get-tuple-element.40), channel_id=1, source_target_pairs={{4,0},{5,1},{8,4},{9,5},{2,6},{3,7},{12,8},{13,9},{6,10},{7,11},{1... | collective-permute-start | bytes 3538952 | tf_op jit(solution)/shard_map/ppermute | solution.py:360
  8.6 3.7 %two.1 = (bf16[2,96,3328]{2,1,0:T(8,128)(2,1)}, bf16[2,96,3328]{2,1,0:T(8,128)(2,1)}) custom-call(s32[3]{0:T(128)} %pad_add_fusion.info, s32[1,96]{1,0:T(1,128)} %bitcast.5, s32[1,2]{1,0:T(1,128)} %pairs.3, bf16[2,96,12544]{2,1,0:T(8,128)(2,1)} %refs_1_.2), custom_call_target="tpu_custom_call" | custom-call | flops 1000 | bytes 1000 | tf_op jit(solution)/shard_map/two/pallas_call | solution.py:283
  12.3 3.8 %collective-permute-start.4 = (bf16[2,96,3328]{2,1,0:T(8,128)(2,1)}, bf16[2,96,3328]{2,1,0:T(8,128)(2,1)}, u32[]{:S(2)}, u32[]{:S(2)}) collective-permute-start(bf16[2,96,3328]{2,1,0:T(8,128)(2,1)} %get-tuple-element.34), channel_id=1, source_target_pairs={{0,2},{1,3},{2,0},{3,1},{4,6},{5,7},{6,4},{7,5},{8,10},{9,11},{10,... | collective-permute-start | bytes 3833864 | tf_op jit(solution)/shard_map/ppermute | solution.py:360
  16.1 1.3 %collective-permute-start.7 = (bf16[2,96,3328]{2,1,0:T(8,128)(2,1)}, bf16[2,96,3328]{2,1,0:T(8,128)(2,1)}, u32[]{:S(2)}, u32[]{:S(2)}) collective-permute-start(bf16[2,96,3328]{2,1,0:T(8,128)(2,1)} %get-tuple-element.35), channel_id=1, source_target_pairs={{4,0},{5,1},{8,4},{9,5},{2,6},{3,7},{12,8},{13,9},{6,10},{7,11},{1... | collective-permute-start | bytes 3833864 | tf_op jit(solution)/shard_map/ppermute | solution.py:360
  17.4 0.0 collective-permute-done.refs_0_
  17.4 0.1 collective-permute-start.3
  17.5 7.9 %diag.1 = f32[288,192]{1,0:T(8,128)} custom-call(s32[3]{0:T(128)} %pad_add_fusion.info, f32[3,12544]{1,0:T(4,128)} %k_hbm.7, bf16[2,96,12544]{2,1,0:T(8,128)(2,1)} %refs_1_.2, bf16[2,96,128]{2,1,0:T(8,128)(2,1)} %get-tuple-element.37.refs_1_.refs_3_.refs_5_), custom_call_target="tpu_custom_call" | custom-call | flops 1000 | bytes 1000 | tf_op jit(solution)/shard_map/diag/pallas_call | solution.py:200
  25.4 0.0 collective-permute-done.3.refs_2_
  25.4 6.2 %near.1 = (f32[288,192]{1,0:T(8,128)}, bf16[432,128]{1,0:T(8,128)(2,1)}) custom-call(s32[3]{0:T(128)} %pad_add_fusion.info, f32[3,12544]{1,0:T(4,128)} %k_hbm.7, bf16[2,96,12544]{2,1,0:T(8,128)(2,1)} %collective-permute-done.refs_0_, bf16[2,96,12544]{2,1,0:T(8,128)(2,1)} %refs_1_.2, bf16[2,96,128]{2,1,0:T(8,128)(2,1)} %collective-permute-done.3.refs_2_, ...), custom_call_target="tpu_custom_call" | custom-call | flops 1000 | bytes 1000 | tf_op jit(solution)/shard_map/near/pallas_call | solution.py:200
  31.6 2.9 %collective-permute-done.1.refs_0_ = bf16[2,96,3072]{2,1,0:T(8,128)(2,1)} collective-permute-done((bf16[2,96,3072]{2,1,0:T(8,128)(2,1)}, bf16[2,96,3072]{2,1,0:T(8,128)(2,1)}, u32[]{:S(2)}, u32[]{:S(2)}) %collective-permute-start.1) | collective-permute-done | bytes 1179680 | tf_op jit(solution)/shard_map/ppermute | solution.py:360
  34.5 3.9 %collective-permute-done.2.refs_2_ = bf16[2,96,3072]{2,1,0:T(8,128)(2,1)} collective-permute-done((bf16[2,96,3072]{2,1,0:T(8,128)(2,1)}, bf16[2,96,3072]{2,1,0:T(8,128)(2,1)}, u32[]{:S(2)}, u32[]{:S(2)}) %collective-permute-start.2) | collective-permute-done | bytes 1179680 | tf_op jit(solution)/shard_map/ppermute | solution.py:360
  38.3 0.0 collective-permute-start.5
  38.4 0.5 collective-permute-start.6
  38.9 2.7 %collective-permute-done.5.refs_3_ = bf16[2,96,3072]{2,1,0:T(8,128)(2,1)} collective-permute-done((bf16[2,96,3072]{2,1,0:T(8,128)(2,1)}, bf16[2,96,3072]{2,1,0:T(8,128)(2,1)}, u32[]{:S(2)}, u32[]{:S(2)}) %collective-permute-start.5) | collective-permute-done | bytes 1179680 | tf_op jit(solution)/shard_map/ppermute | solution.py:360
  41.5 6.9 %far.2.refs_8_ = f32[3,288,192]{2,1,0:T(8,128)} custom-call(s32[3]{0:T(128)} %pad_add_fusion.info, f32[3,12544]{1,0:T(4,128)} %k_hbm.7, bf16[2,96,3072]{2,1,0:T(8,128)(2,1)} %collective-permute-done.1.refs_0_, bf16[2,96,12544]{2,1,0:T(8,128)(2,1)} %refs_1_.2, bf16[2,96,3072]{2,1,0:T(8,128)(2,1)} %collective-permute-done.2.refs_2_, ...), custom_call_target="tpu_custom_call" | custom-call | flops 1000 | bytes 1000 | tf_op jit(solution)/shard_map/far/pallas_call | solution.py:200
  48.5 13.2 %collective-permute-done.4.refs_0_.refs_4_ = bf16[2,96,3328]{2,1,0:T(8,128)(2,1)} collective-permute-done((bf16[2,96,3328]{2,1,0:T(8,128)(2,1)}, bf16[2,96,3328]{2,1,0:T(8,128)(2,1)}, u32[]{:S(2)}, u32[]{:S(2)}) %collective-permute-start.4) | collective-permute-done | bytes 1277984 | tf_op jit(solution)/shard_map/ppermute | solution.py:360
  61.7 0.0 collective-permute-done.6.core
  61.7 0.0 collective-permute-start.8
  61.7 3.3 %collective-permute-done.7.refs_0_.refs_2_.refs_6_ = bf16[2,96,3328]{2,1,0:T(8,128)(2,1)} collective-permute-done((bf16[2,96,3328]{2,1,0:T(8,128)(2,1)}, bf16[2,96,3328]{2,1,0:T(8,128)(2,1)}, u32[]{:S(2)}, u32[]{:S(2)}) %collective-permute-start.7) | collective-permute-done | bytes 1277984 | tf_op jit(solution)/shard_map/ppermute | solution.py:360
  65.0 0.6 mark.1.marked
  65.6 0.0 collective-permute-done.8.refs_3_.refs_7_
  65.6 8.4 %far.3 = (f32[2,288,192]{2,1,0:T(8,128)}, bf16[2,432,128]{2,1,0:T(8,128)(2,1)}, bf16[2,432,128]{2,1,0:T(8,128)(2,1)}, bf16[432,128]{1,0:T(8,128)(2,1)}) custom-call(s32[3]{0:T(128)} %pad_add_fusion.info, f32[3,12544]{1,0:T(4,128)} %k_hbm.7, bf16[2,96,3328]{2,1,0:T(8,128)(2,1)} %collective-permute-done.4.refs_0_.refs_4_, bf16[2,96,12544]{2,1,0:T(8,128)(2,1)} %refs_1_.2, ...), custom_call_target="tpu_custom_call" | custom-call | flops 1000 | bytes 1000 | tf_op jit(solution)/shard_map/far/pallas_call | solution.py:200
  74.0 1.2 %collective-permute-start.11 = (bf16[2,432,128]{2,1,0:T(8,128)(2,1)}, bf16[2,432,128]{2,1,0:T(8,128)(2,1)}, u32[]{:S(2)}, u32[]{:S(2)}) collective-permute-start(bf16[2,432,128]{2,1,0:T(8,128)(2,1)} %get-tuple-element.55), channel_id=1, source_target_pairs={{0,2},{1,3},{2,0},{3,1},{4,6},{5,7},{6,4},{7,5},{8,10},{9,11},{10,... | collective-permute-start | bytes 663560 | tf_op jit(solution)/shard_map/ppermute | solution.py:360
  75.3 4.2 %collective-permute-start.9 = (bf16[2,432,128]{2,1,0:T(8,128)(2,1)}, bf16[2,432,128]{2,1,0:T(8,128)(2,1)}, u32[]{:S(2)}, u32[]{:S(2)}) collective-permute-start(bf16[2,432,128]{2,1,0:T(8,128)(2,1)} %get-tuple-element.53), channel_id=1, source_target_pairs={{0,4},{1,5},{4,8},{5,9},{6,2},{7,3},{8,12},{9,13},{10,6},{11,7},{1... | collective-permute-start | bytes 663560 | tf_op jit(solution)/shard_map/ppermute | solution.py:360
  79.4 0.0 collective-permute-start.10
  79.4 5.4 %collective-permute-done.10.across = bf16[432,128]{1,0:T(8,128)(2,1)} collective-permute-done((bf16[432,128]{1,0:T(8,128)(2,1)}, bf16[432,128]{1,0:T(8,128)(2,1)}, u32[]{:S(2)}, u32[]{:S(2)}) %collective-permute-start.10) | collective-permute-done | bytes 110624 | tf_op jit(solution)/shard_map/ppermute | solution.py:360
  84.8 0.0 collective-permute-done.11.up_y
  84.8 0.0 collective-permute-done.9.up_z
  84.9 3.7 %final.1 = f32[3,2,96,480]{3,2,1,0:T(8,128)} custom-call(s32[3]{0:T(128)} %pad_add_fusion.info, f32[288,192]{1,0:T(8,128)} %diag.1, f32[288,192]{1,0:T(8,128)} %get-tuple-element.44.own, bf16[432,128]{1,0:T(8,128)(2,1)} %collective-permute-done.6.core, f32[2,288,192]{2,1,0:T(8,128)} %get-tuple-element.52.far, ...), custom_call_target="tpu_custom_call" | custom-call | tf_op jit(solution)/shard_map/final/pallas_call | solution.py:326
Async XLA Ops:
  0.0 17.4 %collective-permute-start = (bf16[2,96,12544]{2,1,0:T(8,128)(2,1)}, bf16[2,96,12544]{2,1,0:T(8,128)(2,1)}, u32[]{:S(2)}, u32[]{:S(2)}) collective-permute-start(bf16[2,96,12544]{2,1,0:T(8,128)(2,1)} %refs_1_.2), channel_id=1, source_target_pairs={{0,1},{1,0},{2,3},{3,2},{4,5},{5,4},{6,7},{7,6},{8,9},{9,8},{10,11... | collective-permute-start | bytes 14450696 | tf_op jit(solution)/shard_map/ppermute | solution.py:360
  4.8 29.7 %collective-permute-start.1 = (bf16[2,96,3072]{2,1,0:T(8,128)(2,1)}, bf16[2,96,3072]{2,1,0:T(8,128)(2,1)}, u32[]{:S(2)}, u32[]{:S(2)}) collective-permute-start(bf16[2,96,3072]{2,1,0:T(8,128)(2,1)} %get-tuple-element.39), channel_id=1, source_target_pairs={{0,2},{1,3},{2,0},{3,1},{4,6},{5,7},{6,4},{7,5},{8,10},{9,11},{10,... | collective-permute-start | bytes 3538952 | tf_op jit(solution)/shard_map/ppermute | solution.py:360
  7.3 31.0 %collective-permute-start.2 = (bf16[2,96,3072]{2,1,0:T(8,128)(2,1)}, bf16[2,96,3072]{2,1,0:T(8,128)(2,1)}, u32[]{:S(2)}, u32[]{:S(2)}) collective-permute-start(bf16[2,96,3072]{2,1,0:T(8,128)(2,1)} %get-tuple-element.40), channel_id=1, source_target_pairs={{4,0},{5,1},{8,4},{9,5},{2,6},{3,7},{12,8},{13,9},{6,10},{7,11},{1... | collective-permute-start | bytes 3538952 | tf_op jit(solution)/shard_map/ppermute | solution.py:360
  12.3 49.3 %collective-permute-start.4 = (bf16[2,96,3328]{2,1,0:T(8,128)(2,1)}, bf16[2,96,3328]{2,1,0:T(8,128)(2,1)}, u32[]{:S(2)}, u32[]{:S(2)}) collective-permute-start(bf16[2,96,3328]{2,1,0:T(8,128)(2,1)} %get-tuple-element.34), channel_id=1, source_target_pairs={{0,2},{1,3},{2,0},{3,1},{4,6},{5,7},{6,4},{7,5},{8,10},{9,11},{10,... | collective-permute-start | bytes 3833864 | tf_op jit(solution)/shard_map/ppermute | solution.py:360
  16.1 48.9 %collective-permute-start.7 = (bf16[2,96,3328]{2,1,0:T(8,128)(2,1)}, bf16[2,96,3328]{2,1,0:T(8,128)(2,1)}, u32[]{:S(2)}, u32[]{:S(2)}) collective-permute-start(bf16[2,96,3328]{2,1,0:T(8,128)(2,1)} %get-tuple-element.35), channel_id=1, source_target_pairs={{4,0},{5,1},{8,4},{9,5},{2,6},{3,7},{12,8},{13,9},{6,10},{7,11},{1... | collective-permute-start | bytes 3833864 | tf_op jit(solution)/shard_map/ppermute | solution.py:360
  17.4 8.0 %collective-permute-start.3 = (bf16[2,96,128]{2,1,0:T(8,128)(2,1)}, bf16[2,96,128]{2,1,0:T(8,128)(2,1)}, u32[]{:S(2)}, u32[]{:S(2)}) collective-permute-start(bf16[2,96,128]{2,1,0:T(8,128)(2,1)} %get-tuple-element.37.refs_1_.refs_3_.refs_5_), channel_id=1, source_target_pairs={{0,1},{1,0},{2,3},{3,2},{4,5},{5,4},{6,7},{7,6},{8,9},{9,8},{10,11... | collective-permute-start | bytes 147464 | tf_op jit(solution)/shard_map/ppermute | solution.py:360
  38.3 3.2 %collective-permute-start.5 = (bf16[2,96,3072]{2,1,0:T(8,128)(2,1)}, bf16[2,96,3072]{2,1,0:T(8,128)(2,1)}, u32[]{:S(2)}, u32[]{:S(2)}) collective-permute-start(bf16[2,96,3072]{2,1,0:T(8,128)(2,1)} %collective-permute-done.1.refs_0_), channel_id=1, source_target_pairs={{0,1},{1,0},{2,3},{3,2},{4,5},{5,4},{6,7},{7,6},{8,9},{9,8},{10,11... | collective-permute-start | bytes 3538952 | tf_op jit(solution)/shard_map/ppermute | solution.py:360
  38.4 23.3 %collective-permute-start.6 = (bf16[432,128]{1,0:T(8,128)(2,1)}, bf16[432,128]{1,0:T(8,128)(2,1)}, u32[]{:S(2)}, u32[]{:S(2)}) collective-permute-start(bf16[432,128]{1,0:T(8,128)(2,1)} %get-tuple-element.47), channel_id=1, source_target_pairs={{0,1},{1,0},{2,3},{3,2},{4,5},{5,4},{6,7},{7,6},{8,9},{9,8},{10,11... | collective-permute-start | bytes 331784 | tf_op jit(solution)/shard_map/ppermute | solution.py:360
  61.7 3.9 %collective-permute-start.8 = (bf16[2,96,3328]{2,1,0:T(8,128)(2,1)}, bf16[2,96,3328]{2,1,0:T(8,128)(2,1)}, u32[]{:S(2)}, u32[]{:S(2)}) collective-permute-start(bf16[2,96,3328]{2,1,0:T(8,128)(2,1)} %collective-permute-done.4.refs_0_.refs_4_), channel_id=1, source_target_pairs={{0,1},{1,0},{2,3},{3,2},{4,5},{5,4},{6,7},{7,6},{8,9},{9,8},{10,11... | collective-permute-start | bytes 3833864 | tf_op jit(solution)/shard_map/ppermute | solution.py:360
  74.0 10.8 %collective-permute-start.11 = (bf16[2,432,128]{2,1,0:T(8,128)(2,1)}, bf16[2,432,128]{2,1,0:T(8,128)(2,1)}, u32[]{:S(2)}, u32[]{:S(2)}) collective-permute-start(bf16[2,432,128]{2,1,0:T(8,128)(2,1)} %get-tuple-element.55), channel_id=1, source_target_pairs={{0,2},{1,3},{2,0},{3,1},{4,6},{5,7},{6,4},{7,5},{8,10},{9,11},{10,... | collective-permute-start | bytes 663560 | tf_op jit(solution)/shard_map/ppermute | solution.py:360
  75.3 9.6 %collective-permute-start.9 = (bf16[2,432,128]{2,1,0:T(8,128)(2,1)}, bf16[2,432,128]{2,1,0:T(8,128)(2,1)}, u32[]{:S(2)}, u32[]{:S(2)}) collective-permute-start(bf16[2,432,128]{2,1,0:T(8,128)(2,1)} %get-tuple-element.53), channel_id=1, source_target_pairs={{0,4},{1,5},{4,8},{5,9},{6,2},{7,3},{8,12},{9,13},{10,6},{11,7},{1... | collective-permute-start | bytes 663560 | tf_op jit(solution)/shard_map/ppermute | solution.py:360
  79.4 5.4 %collective-permute-start.10 = (bf16[432,128]{1,0:T(8,128)(2,1)}, bf16[432,128]{1,0:T(8,128)(2,1)}, u32[]{:S(2)}, u32[]{:S(2)}) collective-permute-start(bf16[432,128]{1,0:T(8,128)(2,1)} %get-tuple-element.54), channel_id=1, source_target_pairs={{0,3},{1,2},{2,1},{3,0},{4,7},{5,6},{6,5},{7,4},{8,11},{9,10},{10,... | collective-permute-start | bytes 331784 | tf_op jit(solution)/shard_map/ppermute | solution.py:360

commit v4 on v3

--- a/solution.py
+++ b/solution.py
@@ -12,7 +12,7 @@
 OCC_STEPS = 16
 SPAN = 5
 LANES = 128
-CHUNKS = (24, 25)
+CHUNKS = (13, 17, 19)
 F32 = jnp.float32
 BF16 = jnp.bfloat16
 VMEM_BYTES = 64 * 2**20
@@ -65,6 +65,12 @@
     return side, tuple((jnp.where(side == 0, low, high), jnp.where(side == 0, high, low)) for low, high in pairs)
 
 
+def position():
+    me = lax.axis_index("blk")
+    side, core = lax.rem(lax.div(me, 2), 2), lax.rem(me, 2)
+    return jnp.where(side == core, 1, 0), side, core
+
+
 def pick(values, i):
     out = values[0]
     for j in range(1, len(values)):
@@ -72,7 +78,8 @@
     return out
 
 
-def pair_body(kind, first_tile, tiles, plans, facts_plans, has_start, scale, info, k_hbm, *refs):
+def pair_body(kind, first_tile, tiles, plans, facts_plans, has_start, scale, k_hbm, *refs):
+    info = position()
     offsets = OFFSETS[kind]
     count, blocks = len(offsets), len(plans)
     half, pairs = roles(kind, info)
@@ -114,15 +121,17 @@
             later += copies(facts_plans[b], facts_sources[b], facts.at[b], 1, facts_sems.at[b])
     if has_start:
         later.append((None, pltpu.make_async_copy(start_hbm, start, start_sem)))
-    begin(later)
+    facts_copies = blocks if ends else 0
+    begin(later[:facts_copies])
     k_copy.start()
     for load in loads[:2]:
         begin(load)
+    begin(later[facts_copies:])
 
     def order(i):
         return tuple(pick([pair[n] for pair in pairs], i) for n in (0, 1))
 
-    wait(later)
+    wait(later[:facts_copies])
     if ends:
         @pl.loop(0, count)
         def _(i):
@@ -146,7 +155,9 @@
         low, high = order(i)
         acc[i] = product(k_held[...], held[low], held[high])
 
-    @pl.loop(0, count)
+    wait(later[facts_copies:])
+
+    @pl.loop(0, count, unroll=True)
     def _(i):
         tile = acc[i]
         if has_start:
@@ -180,7 +191,7 @@
                 outs[3][...] = packed
 
 
-def pair_sums(kind, info, k, blocks, begin, tiles, facts=None, start=None):
+def pair_sums(kind, k, blocks, begin, tiles, facts=None, start=None):
     bands = blocks[0][0][0].shape[1]
     count = len(OFFSETS[kind])
     ends = facts is not None
@@ -201,7 +212,7 @@
         functools.partial(
             pair_body, kind, begin, tiles, plans(blocks), plans(facts) if ends else None, start is not None, 1.0 / math.sqrt(k.shape[1])
         ),
-        in_specs=[pl.BlockSpec(memory_space=pltpu.SMEM)] + [pl.BlockSpec(memory_space=pltpu.HBM)] * len(operands),
+        in_specs=[pl.BlockSpec(memory_space=pltpu.HBM)] * len(operands),
         out_specs=[pl.BlockSpec(memory_space=pltpu.VMEM)] * len(out_shape),
         out_shape=out_shape,
         scratch_shapes=[
@@ -219,7 +230,7 @@
         compiler_params=pltpu.CompilerParams(vmem_limit_bytes=VMEM_BYTES),
         cost_estimate=pl.CostEstimate(flops=1000, bytes_accessed=1000, transcendentals=0),
         name=kind,
-    )(info, *operands)
+    )(*operands)
 
 
 def mark_body(*refs):
@@ -238,12 +249,12 @@
     )(*arrays)
 
 
-def pieces_body(cuts, info, levels, pairs, coeffs, *refs):
+def pieces_body(cuts, levels, pairs, coeffs, *refs):
     outs, held, sems = refs[: len(cuts)], refs[-2], refs[-1]
     bands = coeffs.shape[1]
     half = coeffs.shape[2] // 2
     tiles = half // LANES
-    side, core = info[1], info[2]
+    _, side, core = position()
     span = lambda start, size: pl.ds(pl.multiple_of(start, LANES), size * LANES)
     loads, stores, at = [], [], 1
     for n, (which, start, size, more) in enumerate(cuts):
@@ -276,14 +287,13 @@
         copy.wait()
 
 
-def pieces(cuts, info, levels, pairs, coeffs, name):
+def pieces(cuts, levels, pairs, coeffs, name):
     bands = coeffs.shape[1]
     anywhere = pl.BlockSpec(memory_space=pltpu.HBM)
     return list(
         pl.pallas_call(
             functools.partial(pieces_body, cuts),
             in_specs=[
-                pl.BlockSpec(memory_space=pltpu.SMEM),
                 pl.BlockSpec(memory_space=pltpu.VMEM),
                 pl.BlockSpec(memory_space=pltpu.SMEM),
                 anywhere,
@@ -297,14 +307,14 @@
             compiler_params=pltpu.CompilerParams(vmem_limit_bytes=VMEM_BYTES),
             cost_estimate=pl.CostEstimate(flops=1000, bytes_accessed=1000, transcendentals=0),
             name=name,
-        )(info, levels[None, :], pairs, coeffs)
+        )(levels[None, :], pairs, coeffs)
     )
 
 
-def final_body(info, diag, own, core, far, up_z, across, up_y, marked, out):
+def final_body(diag, own, core, far, up_y, across, up_z, marked, result, out, sems):
     bands = out.shape[2]
-    first = info[0] == 1
-    low = info[1] == 0
+    first, side, _ = position()
+    first, low = first == 1, side == 0
     wide = lambda tile: unpack(tile.astype(F32))
     mine = own[...] + wide(core[...])
     middle = wide(across[...])
@@ -314,23 +324,29 @@
     away2 = wide(up_y[1]) + wide(up_z[1])
     above = [jnp.where(low, near1, away1), jnp.where(low, near2, away2)]
     below = [jnp.where(low, away1, near1), jnp.where(low, away2, near2)]
+    copies = []
     for a in range(3):
         for part in range(2):
             cut = lambda tile: tile[a * bands : (a + 1) * bands, part * bands : (part + 1) * bands]
             turn = lambda tile: -cut(tile).T if part == 0 else cut(tile).T
             out[a, part] = jnp.concatenate([turn(below[1]), turn(below[0]), cut(diag), cut(above[0]), cut(above[1])], axis=1)
-
-
-def final(info, bands, *operands):
+        copies.append(pltpu.make_async_copy(out.at[a], result.at[a], sems.at[a]))
+        copies[-1].start()
+    for copy in copies:
+        copy.wait()
+
+
+def final(bands, *operands):
     vmem = pl.BlockSpec(memory_space=pltpu.VMEM)
     return pl.pallas_call(
         final_body,
-        in_specs=[pl.BlockSpec(memory_space=pltpu.SMEM)] + [vmem] * len(operands),
-        out_specs=vmem,
+        in_specs=[vmem] * len(operands),
+        out_specs=pl.BlockSpec(memory_space=pltpu.HBM),
         out_shape=jax.ShapeDtypeStruct((3, 2, bands, SPAN * bands), F32),
+        scratch_shapes=[pltpu.VMEM((3, 2, bands, SPAN * bands), F32), pltpu.SemaphoreType.DMA((3,))],
         compiler_params=pltpu.CompilerParams(vmem_limit_bytes=VMEM_BYTES),
         name="final",
-    )(info, *operands)
+    )(*operands)
 
 
 def routes(groups):
@@ -350,53 +366,60 @@
 
 def shards(coeffs, k_plus_g, pairs, levels):
     groups = lax.axis_size("blk")
-    me = lax.axis_index("blk")
     bands, plane = coeffs.shape[1:]
     tiles = plane // 2 // LANES
-    core = me % 2
-    side = (me // 2) % 2
-    info = jnp.stack([(core == side).astype(jnp.int32), side, core])
     way = routes(groups)
     send = lambda value, name: lax.ppermute(value, "blk", way[name])
     tie = lambda *arrays: lax.optimization_barrier(arrays)
 
-    one, two = CHUNKS
+    begins = [sum(CHUNKS[:i]) for i in range(len(CHUNKS))]
+    last = len(CHUNKS) - 1
     swapped = send(coeffs, "core")
-    y_one, z_one, facts = pieces(
-        [("y", 0, one, False), ("z", 0, one, False), ("y", 0, 0, True)], info, levels, pairs, coeffs, "one"
-    )
-    facts_core = [(send(facts, "core"), None, 0)]
-    coeffs, y_one, z_one = tie(coeffs, y_one, z_one)
-    got_z, got_y = [send(z_one, "z")], [send(y_one, "y")]
-    y_two, z_two = pieces([("y", one, two, True), ("z", one, two, True)], info, levels, pairs, coeffs, "two")
-    got_z.append(send(z_two, "z"))
-    got_y.append(send(y_two, "y"))
-    here = [(facts, None, 0)]
-
-    coeffs, y_two, z_two = tie(coeffs, y_two, z_two)
-    (diag,) = pair_sums("diag", info, k_plus_g, [[(coeffs, None, 0)]], 0, 2 * tiles, [here])
+    y_blocks, z_blocks, facts = [[block] for block in pieces(
+        [("y", 0, CHUNKS[0], False), ("z", 0, CHUNKS[0], False), ("y", 0, 0, True)], levels, pairs, coeffs, "one"
+    )]
+    facts = facts[0]
+    here, facts_core = [(facts, None, 0)], [(send(facts, "core"), None, 0)]
+    coeffs, y_blocks[0], z_blocks[0] = tie(coeffs, y_blocks[0], z_blocks[0])
+    cuts = [(which, begins[i], CHUNKS[i], i == last) for i in range(1, last + 1) for which in ("y", "z")]
+    blocks = pieces(cuts, levels, pairs, coeffs, "rest")
+    y_blocks += blocks[0::2]
+    z_blocks += blocks[1::2]
+    got_y, got_z = [], []
+    for y_block, z_block in zip(y_blocks, z_blocks):
+        got_y.append(send(y_block, "y"))
+        got_z.append(send(z_block, "z"))
+
+    coeffs, y_blocks[-1], z_blocks[-1] = tie(coeffs, y_blocks[-1], z_blocks[-1])
+    (diag,) = pair_sums("diag", k_plus_g, [[(coeffs, None, 0)]], 0, 2 * tiles, [here])
     diag, swapped, coeffs = tie(diag, swapped, coeffs)
     own, own_packed = pair_sums(
-        "near", info, k_plus_g, [[(swapped, "core", 0)], [(coeffs, "core", 0)]], 0, tiles, [facts_core, here]
+        "near", k_plus_g, [[(swapped, "core", 0)], [(coeffs, "core", 0)]], 0, tiles, [facts_core, here]
     )
     tile_own = send(own_packed, "core")
-    got_y[0], got_z[0], own = tie(got_y[0], got_z[0], own)
-    other = [send(got_y[0], "core")]
-    (sums,) = pair_sums(
-        "far", info, k_plus_g, [[(got_y[0], None, 0)], [(coeffs, "side", 0)], [(got_z[0], None, 0)], [(other[0], None, 0)]], 0, one
-    )
-    got_y[1], sums, tile_own = tie(got_y[1], sums, tile_own)
-    other.append(send(got_y[1], "core"))
-    marked = mark(got_z[1])
-    other[1], marked = tie(other[1], marked)
-    far, pairs_02, pairs_12, pair_1 = pair_sums(
-        "far", info, k_plus_g, [[(got_y[1], None, 0)], [(coeffs, "side", one)], [(got_z[1], None, 0)], [(other[1], None, 0)]], one, two,
-        [[(got_y[1], None, two)], here, [(got_z[1], None, two)], [(other[1], None, two)]], sums,
-    )
+    sums, before = None, own
+    for i, (begin, size) in enumerate(zip(begins, CHUNKS)):
+        blocks = lambda other: [[(got_y[i], None, 0)], [(coeffs, "side", begin)], [(got_z[i], None, 0)], [(other, None, 0)]]
+        if i < last:
+            got_y[i], got_z[i], before = tie(got_y[i], got_z[i], before)
+            if i == 0:
+                own = before
+            else:
+                sums = before
+            (sums,) = pair_sums("far", k_plus_g, blocks(send(got_y[i], "core")), begin, size, start=sums)
+            before = sums
+        else:
+            got_y[i], sums, tile_own = tie(got_y[i], sums, tile_own)
+            marked = mark(got_z[i])
+            other, marked = tie(send(got_y[i], "core"), marked)
+            far, pairs_02, pairs_12, pair_1 = pair_sums(
+                "far", k_plus_g, blocks(other), begin, size,
+                [[(got_y[i], None, size)], here, [(got_z[i], None, size)], [(other, None, size)]], sums,
+            )
     tile_y = send(pairs_02, "y")
     tile_across = send(pair_1, "across")
     tile_z = send(pairs_12, "back")
-    return final(info, bands, diag, own, tile_own, far, tile_z, tile_across, tile_y, marked)
+    return final(bands, diag, own, tile_own, far, tile_y, tile_across, tile_z, marked)
 
 
 def solution(mesh):

time: 89 us -> 85 us (0.955)
  waiting for transfers between devices: 31.5 us -> 24.4 us
  starting transfers between devices: 15.3 us -> 19.1 us
    ppermute x12 -> x15, waiting for transfers between devices: 31.5 us -> 24.4 us  [shards(): send = lambda value, name: lax.ppermute(value, 'blk', way[name])]
    ppermute x12 -> x15, starting transfers between devices: 15.3 us -> 19.1 us  [shards(): send = lambda value, name: lax.ppermute(value, 'blk', way[name])]
    pallas_call x4 -> x5, Pallas kernels: 29.4 us -> 29.8 us  [pair_sums(): pl.pallas_call(functools.partial(pair_body, kind, begin, tiles, plans(blo...]
  transfers between devices with their start and end apart: 12 -> 15, of which waited for: 6 -> 6; matrix products, arithmetic and copies ran while one was open for 1% -> 0% of each run, Pallas kernels for 33% -> 37%
where the time goes in v4:
time: 85 us; the launch traced here: 84.6 us
  Pallas kernels  40.9 us (48%)
  waiting for transfers between devices  24.4 us (29%)
  starting transfers between devices  19.1 us (22%)
    pallas_call x5, Pallas kernels, pair_sums(): pl.pallas_call(functools.partial(pair_body, kind, begin, tiles, plans(blo...  29.8 us
    ppermute x15, waiting for transfers between devices, shards(): send = lambda value, name: lax.ppermute(value, 'blk', way[name])  24.4 us
    ppermute x15, starting transfers between devices, shards(): send = lambda value, name: lax.ppermute(value, 'blk', way[name])  19.1 us
    pallas_call x2, Pallas kernels, pieces(): pl.pallas_call(functools.partial(pieces_body, cuts), in_specs=[pl.BlockSp...  6.98 us
    pallas_call x1, Pallas kernels, final(): pl.pallas_call(final_body, in_specs=[vmem] * len(operands), out_specs=pl....  3.5 us
  transfers between devices with their start and end apart: 15, of which 6 were waited for; matrix products, arithmetic and copies ran while one was open for 0% of the time, Pallas kernels for 37%

profile of v4, /device:TPU:0, one launch (start us, length us, event | category | flops | bytes accessed | tf_op | source)
XLA Modules:
  0.0 84.6 jit_solution(18107549817065598363)
XLA Ops:
  0.0 0.5 collective-permute-start
  0.5 3.1 %one.1 = (bf16[2,96,1664]{2,1,0:T(8,128)(2,1)}, bf16[2,96,1664]{2,1,0:T(8,128)(2,1)}, bf16[2,96,128]{2,1,0:T(8,128)(2,1)}) custom-call(s32[1,96]{1,0:T(1,128)} %bitcast.1, s32[1,2]{1,0:T(1,128)} %pairs.3, bf16[2,96,12544]{2,1,0:T(8,128)(2,1)} %refs_1_.3), custom_call_target="tpu_custom_call" | custom-call | flops 1000 | bytes 1000 | tf_op jit(solution)/shard_map/one/pallas_call | solution.py:294
  3.5 2.6 %collective-permute-start.1 = (bf16[2,96,1664]{2,1,0:T(8,128)(2,1)}, bf16[2,96,1664]{2,1,0:T(8,128)(2,1)}, u32[]{:S(2)}, u32[]{:S(2)}) collective-permute-start(bf16[2,96,1664]{2,1,0:T(8,128)(2,1)} %get-tuple-element.44), channel_id=1, source_target_pairs={{0,2},{1,3},{2,0},{3,1},{4,6},{5,7},{6,4},{7,5},{8,10},{9,11},{10,... | collective-permute-start | bytes 1916936 | tf_op jit(solution)/shard_map/ppermute | solution.py:372
  6.1 1.3 %collective-permute-start.2 = (bf16[2,96,1664]{2,1,0:T(8,128)(2,1)}, bf16[2,96,1664]{2,1,0:T(8,128)(2,1)}, u32[]{:S(2)}, u32[]{:S(2)}) collective-permute-start(bf16[2,96,1664]{2,1,0:T(8,128)(2,1)} %get-tuple-element.45), channel_id=1, source_target_pairs={{4,0},{5,1},{8,4},{9,5},{2,6},{3,7},{12,8},{13,9},{6,10},{7,11},{1... | collective-permute-start | bytes 1916936 | tf_op jit(solution)/shard_map/ppermute | solution.py:372
  7.4 3.9 %rest.1 = (bf16[2,96,2176]{2,1,0:T(8,128)(2,1)}, bf16[2,96,2176]{2,1,0:T(8,128)(2,1)}, bf16[2,96,2560]{2,1,0:T(8,128)(2,1)}, bf16[2,96,2560]{2,1,0:T(8,128)(2,1)}) custom-call(s32[1,96]{1,0:T(1,128)} %bitcast.2, s32[1,2]{1,0:T(1,128)} %pairs.3, bf16[2,96,12544]{2,1,0:T(8,128)(2,1)} %refs_1_.3), custom_call_target="tpu_custom_call" | custom-call | flops 1000 | bytes 1000 | tf_op jit(solution)/shard_map/rest/pallas_call | solution.py:294
  11.3 3.6 %collective-permute-start.5 = (bf16[2,96,2176]{2,1,0:T(8,128)(2,1)}, bf16[2,96,2176]{2,1,0:T(8,128)(2,1)}, u32[]{:S(2)}, u32[]{:S(2)}) collective-permute-start(bf16[2,96,2176]{2,1,0:T(8,128)(2,1)} %get-tuple-element.50), channel_id=1, source_target_pairs={{0,2},{1,3},{2,0},{3,1},{4,6},{5,7},{6,4},{7,5},{8,10},{9,11},{10,... | collective-permute-start | bytes 2506760 | tf_op jit(solution)/shard_map/ppermute | solution.py:372
  14.9 1.3 %collective-permute-start.6 = (bf16[2,96,2176]{2,1,0:T(8,128)(2,1)}, bf16[2,96,2176]{2,1,0:T(8,128)(2,1)}, u32[]{:S(2)}, u32[]{:S(2)}) collective-permute-start(bf16[2,96,2176]{2,1,0:T(8,128)(2,1)} %get-tuple-element.51), channel_id=1, source_target_pairs={{4,0},{5,1},{8,4},{9,5},{2,6},{3,7},{12,8},{13,9},{6,10},{7,11},{1... | collective-permute-start | bytes 2506760 | tf_op jit(solution)/shard_map/ppermute | solution.py:372
  16.2 0.0 collective-permute-done.refs_0_
  16.2 0.1 collective-permute-start.3
  16.3 7.2 %diag.1 = f32[288,192]{1,0:T(8,128)} custom-call(f32[3,12544]{1,0:T(4,128)} %k_hbm.9, bf16[2,96,12544]{2,1,0:T(8,128)(2,1)} %refs_1_.3, bf16[2,96,128]{2,1,0:T(8,128)(2,1)} %get-tuple-element.42.refs_1_.refs_3_.refs_5_), custom_call_target="tpu_custom_call" | custom-call | flops 1000 | bytes 1000 | tf_op jit(solution)/shard_map/diag/pallas_call | solution.py:211
  23.5 0.0 collective-permute-done.3.refs_2_
  23.5 5.5 %near.1 = (f32[288,192]{1,0:T(8,128)}, bf16[432,128]{1,0:T(8,128)(2,1)}) custom-call(f32[3,12544]{1,0:T(4,128)} %k_hbm.9, bf16[2,96,12544]{2,1,0:T(8,128)(2,1)} %collective-permute-done.refs_0_, bf16[2,96,12544]{2,1,0:T(8,128)(2,1)} %refs_1_.3, bf16[2,96,128]{2,1,0:T(8,128)(2,1)} %collective-permute-done.3.refs_2_, ...), custom_call_target="tpu_custom_call" | custom-call | flops 1000 | bytes 1000 | tf_op jit(solution)/shard_map/near/pallas_call | solution.py:211
  29.0 0.0 collective-permute-done.1.refs_0_
  29.0 0.0 collective-permute-done.2.refs_2_
  29.1 0.6 collective-permute-start.7
  29.6 2.6 %collective-permute-start.4 = (bf16[2,96,2560]{2,1,0:T(8,128)(2,1)}, bf16[2,96,2560]{2,1,0:T(8,128)(2,1)}, u32[]{:S(2)}, u32[]{:S(2)}) collective-permute-start(bf16[2,96,2560]{2,1,0:T(8,128)(2,1)} %get-tuple-element.39), channel_id=1, source_target_pairs={{0,2},{1,3},{2,0},{3,1},{4,6},{5,7},{6,4},{7,5},{8,10},{9,11},{10,... | collective-permute-start | bytes 2949128 | tf_op jit(solution)/shard_map/ppermute | solution.py:372
  32.2 1.3 %collective-permute-start.10 = (bf16[2,96,2560]{2,1,0:T(8,128)(2,1)}, bf16[2,96,2560]{2,1,0:T(8,128)(2,1)}, u32[]{:S(2)}, u32[]{:S(2)}) collective-permute-start(bf16[2,96,2560]{2,1,0:T(8,128)(2,1)} %get-tuple-element.40), channel_id=1, source_target_pairs={{4,0},{5,1},{8,4},{9,5},{2,6},{3,7},{12,8},{13,9},{6,10},{7,11},{1... | collective-permute-start | bytes 2949128 | tf_op jit(solution)/shard_map/ppermute | solution.py:372
  33.5 0.0 collective-permute-done.7.refs_3_
  33.5 5.0 %far.3.refs_4_ = f32[3,288,192]{2,1,0:T(8,128)} custom-call(f32[3,12544]{1,0:T(4,128)} %k_hbm.9, bf16[2,96,1664]{2,1,0:T(8,128)(2,1)} %collective-permute-done.1.refs_0_, bf16[2,96,12544]{2,1,0:T(8,128)(2,1)} %refs_1_.3, bf16[2,96,1664]{2,1,0:T(8,128)(2,1)} %collective-permute-done.2.refs_2_, bf16[2,96,1664]{2,1,0:T(8,128)(2,1)} %collective-permute-done.7.refs_3_), custom_call_target="tpu_custom_call" | custom-call | flops 1000 | bytes 1000 | tf_op jit(solution)/shard_map/far/pallas_call | solution.py:211
  38.5 1.1 %collective-permute-done.5.refs_0_ = bf16[2,96,2176]{2,1,0:T(8,128)(2,1)} collective-permute-done((bf16[2,96,2176]{2,1,0:T(8,128)(2,1)}, bf16[2,96,2176]{2,1,0:T(8,128)(2,1)}, u32[]{:S(2)}, u32[]{:S(2)}) %collective-permute-start.5) | collective-permute-done | bytes 835616 | tf_op jit(solution)/shard_map/ppermute | solution.py:372
  39.6 3.9 %collective-permute-done.6.refs_2_ = bf16[2,96,2176]{2,1,0:T(8,128)(2,1)} collective-permute-done((bf16[2,96,2176]{2,1,0:T(8,128)(2,1)}, bf16[2,96,2176]{2,1,0:T(8,128)(2,1)}, u32[]{:S(2)}, u32[]{:S(2)}) %collective-permute-start.6) | collective-permute-done | bytes 835616 | tf_op jit(solution)/shard_map/ppermute | solution.py:372
  43.4 0.0 collective-permute-start.8
  43.4 0.5 collective-permute-start.9
  43.9 2.2 %collective-permute-done.8.refs_3_ = bf16[2,96,2176]{2,1,0:T(8,128)(2,1)} collective-permute-done((bf16[2,96,2176]{2,1,0:T(8,128)(2,1)}, bf16[2,96,2176]{2,1,0:T(8,128)(2,1)}, u32[]{:S(2)}, u32[]{:S(2)}) %collective-permute-start.8) | collective-permute-done | bytes 835616 | tf_op jit(solution)/shard_map/ppermute | solution.py:372
  46.1 5.8 %far.4.refs_8_ = f32[3,288,192]{2,1,0:T(8,128)} custom-call(f32[3,12544]{1,0:T(4,128)} %k_hbm.9, bf16[2,96,2176]{2,1,0:T(8,128)(2,1)} %collective-permute-done.5.refs_0_, bf16[2,96,12544]{2,1,0:T(8,128)(2,1)} %refs_1_.3, bf16[2,96,2176]{2,1,0:T(8,128)(2,1)} %collective-permute-done.6.refs_2_, bf16[2,96,2176]{2,1,0:T(8,128)(2,1)} %collective-permute-done.8.refs_3_, ...), custom_call_target="tpu_custom_call" | custom-call | flops 1000 | bytes 1000 | tf_op jit(solution)/shard_map/far/pallas_call | solution.py:211
  51.9 8.5 %collective-permute-done.4.refs_0_.refs_4_ = bf16[2,96,2560]{2,1,0:T(8,128)(2,1)} collective-permute-done((bf16[2,96,2560]{2,1,0:T(8,128)(2,1)}, bf16[2,96,2560]{2,1,0:T(8,128)(2,1)}, u32[]{:S(2)}, u32[]{:S(2)}) %collective-permute-start.4) | collective-permute-done | bytes 983072 | tf_op jit(solution)/shard_map/ppermute | solution.py:372
  60.4 0.0 collective-permute-done.9.core
  60.4 0.0 collective-permute-start.11
  60.4 3.3 %collective-permute-done.10.refs_0_.refs_2_.refs_6_ = bf16[2,96,2560]{2,1,0:T(8,128)(2,1)} collective-permute-done((bf16[2,96,2560]{2,1,0:T(8,128)(2,1)}, bf16[2,96,2560]{2,1,0:T(8,128)(2,1)}, u32[]{:S(2)}, u32[]{:S(2)}) %collective-permute-start.10) | collective-permute-done | bytes 983072 | tf_op jit(solution)/shard_map/ppermute | solution.py:372
  63.8 0.6 mark.1.marked
  64.4 0.0 collective-permute-done.11.refs_3_.refs_7_
  64.4 6.3 %far.5 = (f32[2,288,192]{2,1,0:T(8,128)}, bf16[2,432,128]{2,1,0:T(8,128)(2,1)}, bf16[2,432,128]{2,1,0:T(8,128)(2,1)}, bf16[432,128]{1,0:T(8,128)(2,1)}) custom-call(f32[3,12544]{1,0:T(4,128)} %k_hbm.9, bf16[2,96,2560]{2,1,0:T(8,128)(2,1)} %collective-permute-done.4.refs_0_.refs_4_, bf16[2,96,12544]{2,1,0:T(8,128)(2,1)} %refs_1_.3, ...), custom_call_target="tpu_custom_call" | custom-call | flops 1000 | bytes 1000 | tf_op jit(solution)/shard_map/far/pallas_call | solution.py:211
  70.7 0.8 collective-permute-start.12
  71.5 4.2 %collective-permute-start.14 = (bf16[2,432,128]{2,1,0:T(8,128)(2,1)}, bf16[2,432,128]{2,1,0:T(8,128)(2,1)}, u32[]{:S(2)}, u32[]{:S(2)}) collective-permute-start(bf16[2,432,128]{2,1,0:T(8,128)(2,1)} %get-tuple-element.65), channel_id=1, source_target_pairs={{0,4},{1,5},{4,8},{5,9},{6,2},{7,3},{8,12},{9,13},{10,6},{11,7},{1... | collective-permute-start | bytes 663560 | tf_op jit(solution)/shard_map/ppermute | solution.py:372
  75.6 0.0 collective-permute-start.13
  75.7 5.4 %collective-permute-done.13.across = bf16[432,128]{1,0:T(8,128)(2,1)} collective-permute-done((bf16[432,128]{1,0:T(8,128)(2,1)}, bf16[432,128]{1,0:T(8,128)(2,1)}, u32[]{:S(2)}, u32[]{:S(2)}) %collective-permute-start.13) | collective-permute-done | bytes 110624 | tf_op jit(solution)/shard_map/ppermute | solution.py:372
  81.1 0.0 collective-permute-done.12.up_y
  81.1 0.0 collective-permute-done.14.up_z
  81.1 3.5 %final.1 = f32[3,2,96,480]{3,2,1,0:T(8,128)} custom-call(f32[288,192]{1,0:T(8,128)} %diag.1, f32[288,192]{1,0:T(8,128)} %get-tuple-element.49.own, bf16[432,128]{1,0:T(8,128)(2,1)} %collective-permute-done.9.core, f32[2,288,192]{2,1,0:T(8,128)} %get-tuple-element.62.far, bf16[2,432,128]{2,1,0:T(8,128)(2,1)} %collective-permute-done.12.up_y, ...), custom_call_target="tpu_custom_call" | custom-call | tf_op jit(solution)/shard_map/final/pallas_call | solution.py:341
Async XLA Ops:
  0.0 16.2 %collective-permute-start = (bf16[2,96,12544]{2,1,0:T(8,128)(2,1)}, bf16[2,96,12544]{2,1,0:T(8,128)(2,1)}, u32[]{:S(2)}, u32[]{:S(2)}) collective-permute-start(bf16[2,96,12544]{2,1,0:T(8,128)(2,1)} %refs_1_.3), channel_id=1, source_target_pairs={{0,1},{1,0},{2,3},{3,2},{4,5},{5,4},{6,7},{7,6},{8,9},{9,8},{10,11... | collective-permute-start | bytes 14450696 | tf_op jit(solution)/shard_map/ppermute | solution.py:372
  3.5 25.5 %collective-permute-start.1 = (bf16[2,96,1664]{2,1,0:T(8,128)(2,1)}, bf16[2,96,1664]{2,1,0:T(8,128)(2,1)}, u32[]{:S(2)}, u32[]{:S(2)}) collective-permute-start(bf16[2,96,1664]{2,1,0:T(8,128)(2,1)} %get-tuple-element.44), channel_id=1, source_target_pairs={{0,2},{1,3},{2,0},{3,1},{4,6},{5,7},{6,4},{7,5},{8,10},{9,11},{10,... | collective-permute-start | bytes 1916936 | tf_op jit(solution)/shard_map/ppermute | solution.py:372
  6.1 22.9 %collective-permute-start.2 = (bf16[2,96,1664]{2,1,0:T(8,128)(2,1)}, bf16[2,96,1664]{2,1,0:T(8,128)(2,1)}, u32[]{:S(2)}, u32[]{:S(2)}) collective-permute-start(bf16[2,96,1664]{2,1,0:T(8,128)(2,1)} %get-tuple-element.45), channel_id=1, source_target_pairs={{4,0},{5,1},{8,4},{9,5},{2,6},{3,7},{12,8},{13,9},{6,10},{7,11},{1... | collective-permute-start | bytes 1916936 | tf_op jit(solution)/shard_map/ppermute | solution.py:372
  11.3 28.2 %collective-permute-start.5 = (bf16[2,96,2176]{2,1,0:T(8,128)(2,1)}, bf16[2,96,2176]{2,1,0:T(8,128)(2,1)}, u32[]{:S(2)}, u32[]{:S(2)}) collective-permute-start(bf16[2,96,2176]{2,1,0:T(8,128)(2,1)} %get-tuple-element.50), channel_id=1, source_target_pairs={{0,2},{1,3},{2,0},{3,1},{4,6},{5,7},{6,4},{7,5},{8,10},{9,11},{10,... | collective-permute-start | bytes 2506760 | tf_op jit(solution)/shard_map/ppermute | solution.py:372
  14.9 28.5 %collective-permute-start.6 = (bf16[2,96,2176]{2,1,0:T(8,128)(2,1)}, bf16[2,96,2176]{2,1,0:T(8,128)(2,1)}, u32[]{:S(2)}, u32[]{:S(2)}) collective-permute-start(bf16[2,96,2176]{2,1,0:T(8,128)(2,1)} %get-tuple-element.51), channel_id=1, source_target_pairs={{4,0},{5,1},{8,4},{9,5},{2,6},{3,7},{12,8},{13,9},{6,10},{7,11},{1... | collective-permute-start | bytes 2506760 | tf_op jit(solution)/shard_map/ppermute | solution.py:372
  16.2 7.3 %collective-permute-start.3 = (bf16[2,96,128]{2,1,0:T(8,128)(2,1)}, bf16[2,96,128]{2,1,0:T(8,128)(2,1)}, u32[]{:S(2)}, u32[]{:S(2)}) collective-permute-start(bf16[2,96,128]{2,1,0:T(8,128)(2,1)} %get-tuple-element.42.refs_1_.refs_3_.refs_5_), channel_id=1, source_target_pairs={{0,1},{1,0},{2,3},{3,2},{4,5},{5,4},{6,7},{7,6},{8,9},{9,8},{10,11... | collective-permute-start | bytes 147464 | tf_op jit(solution)/shard_map/ppermute | solution.py:372
  29.1 4.4 %collective-permute-start.7 = (bf16[2,96,1664]{2,1,0:T(8,128)(2,1)}, bf16[2,96,1664]{2,1,0:T(8,128)(2,1)}, u32[]{:S(2)}, u32[]{:S(2)}) collective-permute-start(bf16[2,96,1664]{2,1,0:T(8,128)(2,1)} %collective-permute-done.1.refs_0_), channel_id=1, source_target_pairs={{0,1},{1,0},{2,3},{3,2},{4,5},{5,4},{6,7},{7,6},{8,9},{9,8},{10,11... | collective-permute-start | bytes 1916936 | tf_op jit(solution)/shard_map/ppermute | solution.py:372
  29.6 30.8 %collective-permute-start.4 = (bf16[2,96,2560]{2,1,0:T(8,128)(2,1)}, bf16[2,96,2560]{2,1,0:T(8,128)(2,1)}, u32[]{:S(2)}, u32[]{:S(2)}) collective-permute-start(bf16[2,96,2560]{2,1,0:T(8,128)(2,1)} %get-tuple-element.39), channel_id=1, source_target_pairs={{0,2},{1,3},{2,0},{3,1},{4,6},{5,7},{6,4},{7,5},{8,10},{9,11},{10,... | collective-permute-start | bytes 2949128 | tf_op jit(solution)/shard_map/ppermute | solution.py:372
  32.2 31.6 %collective-permute-start.10 = (bf16[2,96,2560]{2,1,0:T(8,128)(2,1)}, bf16[2,96,2560]{2,1,0:T(8,128)(2,1)}, u32[]{:S(2)}, u32[]{:S(2)}) collective-permute-start(bf16[2,96,2560]{2,1,0:T(8,128)(2,1)} %get-tuple-element.40), channel_id=1, source_target_pairs={{4,0},{5,1},{8,4},{9,5},{2,6},{3,7},{12,8},{13,9},{6,10},{7,11},{1... | collective-permute-start | bytes 2949128 | tf_op jit(solution)/shard_map/ppermute | solution.py:372
  43.4 2.7 %collective-permute-start.8 = (bf16[2,96,2176]{2,1,0:T(8,128)(2,1)}, bf16[2,96,2176]{2,1,0:T(8,128)(2,1)}, u32[]{:S(2)}, u32[]{:S(2)}) collective-permute-start(bf16[2,96,2176]{2,1,0:T(8,128)(2,1)} %collective-permute-done.5.refs_0_), channel_id=1, source_target_pairs={{0,1},{1,0},{2,3},{3,2},{4,5},{5,4},{6,7},{7,6},{8,9},{9,8},{10,11... | collective-permute-start | bytes 2506760 | tf_op jit(solution)/shard_map/ppermute | solution.py:372
  43.4 17.0 %collective-permute-start.9 = (bf16[432,128]{1,0:T(8,128)(2,1)}, bf16[432,128]{1,0:T(8,128)(2,1)}, u32[]{:S(2)}, u32[]{:S(2)}) collective-permute-start(bf16[432,128]{1,0:T(8,128)(2,1)} %get-tuple-element.57), channel_id=1, source_target_pairs={{0,1},{1,0},{2,3},{3,2},{4,5},{5,4},{6,7},{7,6},{8,9},{9,8},{10,11... | collective-permute-start | bytes 331784 | tf_op jit(solution)/shard_map/ppermute | solution.py:372
  60.4 3.9 %collective-permute-start.11 = (bf16[2,96,2560]{2,1,0:T(8,128)(2,1)}, bf16[2,96,2560]{2,1,0:T(8,128)(2,1)}, u32[]{:S(2)}, u32[]{:S(2)}) collective-permute-start(bf16[2,96,2560]{2,1,0:T(8,128)(2,1)} %collective-permute-done.4.refs_0_.refs_4_), channel_id=1, source_target_pairs={{0,1},{1,0},{2,3},{3,2},{4,5},{5,4},{6,7},{7,6},{8,9},{9,8},{10,11... | collective-permute-start | bytes 2949128 | tf_op jit(solution)/shard_map/ppermute | solution.py:372
  70.7 10.4 %collective-permute-start.12 = (bf16[2,432,128]{2,1,0:T(8,128)(2,1)}, bf16[2,432,128]{2,1,0:T(8,128)(2,1)}, u32[]{:S(2)}, u32[]{:S(2)}) collective-permute-start(bf16[2,432,128]{2,1,0:T(8,128)(2,1)} %get-tuple-element.63), channel_id=1, source_target_pairs={{0,2},{1,3},{2,0},{3,1},{4,6},{5,7},{6,4},{7,5},{8,10},{9,11},{10,... | collective-permute-start | bytes 663560 | tf_op jit(solution)/shard_map/ppermute | solution.py:372
  71.5 9.6 %collective-permute-start.14 = (bf16[2,432,128]{2,1,0:T(8,128)(2,1)}, bf16[2,432,128]{2,1,0:T(8,128)(2,1)}, u32[]{:S(2)}, u32[]{:S(2)}) collective-permute-start(bf16[2,432,128]{2,1,0:T(8,128)(2,1)} %get-tuple-element.65), channel_id=1, source_target_pairs={{0,4},{1,5},{4,8},{5,9},{6,2},{7,3},{8,12},{9,13},{10,6},{11,7},{1... | collective-permute-start | bytes 663560 | tf_op jit(solution)/shard_map/ppermute | solution.py:372
  75.6 5.4 %collective-permute-start.13 = (bf16[432,128]{1,0:T(8,128)(2,1)}, bf16[432,128]{1,0:T(8,128)(2,1)}, u32[]{:S(2)}, u32[]{:S(2)}) collective-permute-start(bf16[432,128]{1,0:T(8,128)(2,1)} %get-tuple-element.64), channel_id=1, source_target_pairs={{0,3},{1,2},{2,1},{3,0},{4,7},{5,6},{6,5},{7,4},{8,11},{9,10},{10,... | collective-permute-start | bytes 331784 | tf_op jit(solution)/shard_map/ppermute | solution.py:372

commit v5 on v4

--- a/solution.py
+++ b/solution.py
@@ -12,7 +12,8 @@
 OCC_STEPS = 16
 SPAN = 5
 LANES = 128
-CHUNKS = (13, 17, 19)
+FACTS = 16
+CHUNKS = (14, 17, 18)
 F32 = jnp.float32
 BF16 = jnp.bfloat16
 VMEM_BYTES = 64 * 2**20
@@ -28,14 +29,14 @@
     return first + lax.dot_general(rows[1], turned, dims, preferred_element_type=F32)
 
 
-def weights_of(low, high, offset, scale):
-    bands = low.shape[1]
-    low, high = low.astype(F32), high.astype(F32)
+def weights_of(low, high, bands, offset, scale):
+    low, high = low[0:1].astype(F32), high[0:1].astype(F32)
     if isinstance(offset, int):
-        flag = low[1, 0:1, bands + offset - 1 : bands + offset] if offset else 1.0
+        flag = low[:, bands + offset - 1 : bands + offset] if offset else 1.0
     else:
-        flag = jnp.where(offset == 1, low[1, 0:1, bands : bands + 1], low[1, 0:1, bands + 1 : bands + 2])
-    weights = (low[0][:, :bands] - high[1][:, :bands]) * (flag * scale)
+        flag = jnp.where(offset == 1, low[:, bands : bands + 1], low[:, bands + 1 : bands + 2])
+    spread = lambda row: jnp.broadcast_to(row[:, :bands], (bands, bands))
+    weights = (spread(low).T - spread(high)) * (flag * scale)
     return jnp.concatenate([weights, weights], axis=1)
 
 
@@ -118,7 +119,9 @@
     later = []
     if ends:
         for b in range(blocks):
-            later += copies(facts_plans[b], facts_sources[b], facts.at[b], 1, facts_sems.at[b])
+            (at,), (source,) = facts_plans[b], facts_sources[b]
+            rows = source.at[pl.ds(at[1] * FACTS, FACTS)]
+            later.append((None, pltpu.make_async_copy(rows, facts.at[b], facts_sems.at[b, 0])))
     if has_start:
         later.append((None, pltpu.make_async_copy(start_hbm, start, start_sem)))
     facts_copies = blocks if ends else 0
@@ -136,7 +139,7 @@
         @pl.loop(0, count)
         def _(i):
             low, high = order(i)
-            weights[i] = weights_of(facts[low], facts[high], 0 if kind == "diag" else pick(offsets, i), scale)
+            weights[i] = weights_of(facts[low], facts[high], acc.shape[2] // 2, 0 if kind == "diag" else pick(offsets, i), scale)
 
     k_copy.wait()
     wait(loads[0])
@@ -218,7 +221,7 @@
         scratch_shapes=[
             pltpu.VMEM((k.shape[0], tiles * LANES), F32),
             pltpu.VMEM((len(blocks), 2, bands, tiles * LANES), BF16),
-            pltpu.VMEM((len(blocks), 2, bands, LANES), BF16),
+            pltpu.VMEM((len(blocks), FACTS, LANES), BF16),
             pltpu.VMEM((count, bands, 2 * bands), F32),
             pltpu.VMEM(shape, F32),
             pltpu.VMEM(shape, F32),
@@ -249,65 +252,64 @@
     )(*arrays)
 
 
-def pieces_body(cuts, levels, pairs, coeffs, *refs):
+def facts_body(levels, pairs, out):
+    bands = levels.shape[1]
+    lane = lax.broadcasted_iota(jnp.int32, (1, LANES), 1)
+    row = jnp.concatenate([levels[...].astype(F32) / OCC_STEPS, jnp.zeros((1, LANES - bands), F32)], axis=1)
+    for d in range(REACH):
+        row = jnp.where(lane == bands + d, pairs[0, d].astype(F32), row)
+    out[...] = jnp.broadcast_to(row, (FACTS, LANES)).astype(BF16)
+
+
+def facts_of(levels, pairs):
+    return pl.pallas_call(
+        facts_body,
+        in_specs=[pl.BlockSpec(memory_space=pltpu.VMEM), pl.BlockSpec(memory_space=pltpu.SMEM)],
+        out_specs=pl.BlockSpec(memory_space=pltpu.VMEM),
+        out_shape=jax.ShapeDtypeStruct((FACTS, LANES), BF16),
+        compiler_params=pltpu.CompilerParams(vmem_limit_bytes=VMEM_BYTES),
+        cost_estimate=pl.CostEstimate(flops=1000, bytes_accessed=1000, transcendentals=0),
+        name="facts",
+    )(levels[None, :], pairs)
+
+
+def pieces_body(cuts, coeffs, *refs):
     outs, held, sems = refs[: len(cuts)], refs[-2], refs[-1]
-    bands = coeffs.shape[1]
     half = coeffs.shape[2] // 2
-    tiles = half // LANES
-    _, side, core = position()
+    _, side, _ = position()
     span = lambda start, size: pl.ds(pl.multiple_of(start, LANES), size * LANES)
-    loads, stores, at = [], [], 1
-    for n, (which, start, size, more) in enumerate(cuts):
-        source = half * {"y": 1 - side, "z": side, "core": 1 - core}[which] + start * LANES
-        if size == 0:
-            continue
+    loads, stores, at = [], [], 0
+    for n, (which, start, size) in enumerate(cuts):
+        source = half * {"y": 1 - side, "z": side}[which] + start * LANES
         here = held.at[:, :, span(at * LANES, size)]
         loads.append(pltpu.make_async_copy(coeffs.at[:, :, span(source, size)], here, sems.at[0, n]))
         loads[-1].start()
-        stores.append(pltpu.make_async_copy(here, outs[n].at[:, :, span(0, size)], sems.at[1, n]))
+        stores.append(pltpu.make_async_copy(here, outs[n], sems.at[1, n]))
         at += size
-    if any(more for *_, more in cuts):
-        occup = levels[...].astype(F32) / OCC_STEPS
-        spread = jnp.broadcast_to(occup, (bands, bands))
-        lane = lax.broadcasted_iota(jnp.int32, (bands, LANES - bands), 1)
-        flags = jnp.zeros((bands, LANES - bands), F32)
-        for d in range(REACH):
-            flags = jnp.where(lane == d, pairs[0, d].astype(F32), flags)
-        held[0, :, :LANES] = jnp.concatenate([spread.T, jnp.zeros_like(flags)], axis=1).astype(BF16)
-        held[1, :, :LANES] = jnp.concatenate([spread, flags], axis=1).astype(BF16)
-    facts = []
-    for n, (_, _, size, more) in enumerate(cuts):
-        if more:
-            facts.append(pltpu.make_async_copy(held.at[:, :, span(0, 1)], outs[n].at[:, :, span(size * LANES, 1)], sems.at[2, n]))
-            facts[-1].start()
     for load, store in zip(loads, stores):
         load.wait()
         store.start()
-    for copy in stores + facts:
-        copy.wait()
-
-
-def pieces(cuts, levels, pairs, coeffs, name):
+    for store in stores:
+        store.wait()
+
+
+def pieces(cuts, coeffs, name):
     bands = coeffs.shape[1]
     anywhere = pl.BlockSpec(memory_space=pltpu.HBM)
     return list(
         pl.pallas_call(
             functools.partial(pieces_body, cuts),
-            in_specs=[
-                pl.BlockSpec(memory_space=pltpu.VMEM),
-                pl.BlockSpec(memory_space=pltpu.SMEM),
-                anywhere,
-            ],
+            in_specs=[anywhere],
             out_specs=[anywhere] * len(cuts),
-            out_shape=[jax.ShapeDtypeStruct((2, bands, (size + int(more)) * LANES), BF16) for _, _, size, more in cuts],
+            out_shape=[jax.ShapeDtypeStruct((2, bands, size * LANES), BF16) for _, _, size in cuts],
             scratch_shapes=[
-                pltpu.VMEM((2, bands, (1 + sum(size for _, _, size, _ in cuts)) * LANES), BF16),
-                pltpu.SemaphoreType.DMA((3, len(cuts))),
+                pltpu.VMEM((2, bands, sum(size for _, _, size in cuts) * LANES), BF16),
+                pltpu.SemaphoreType.DMA((2, len(cuts))),
             ],
             compiler_params=pltpu.CompilerParams(vmem_limit_bytes=VMEM_BYTES),
             cost_estimate=pl.CostEstimate(flops=1000, bytes_accessed=1000, transcendentals=0),
             name=name,
-        )(levels[None, :], pairs, coeffs)
+        )(coeffs)
     )
 
 
@@ -374,15 +376,18 @@
 
     begins = [sum(CHUNKS[:i]) for i in range(len(CHUNKS))]
     last = len(CHUNKS) - 1
+    half, width = tiles * LANES, CHUNKS[0] * LANES
+    upper = lax.rem(lax.div(lax.axis_index("blk"), 2), 2) == 1
+    low, high = coeffs[:, :, :width], coeffs[:, :, half : half + width]
+    y_blocks, z_blocks = [jnp.where(upper, low, high)], [jnp.where(upper, high, low)]
+    levels, coeffs, y_blocks[0], z_blocks[0] = tie(levels, coeffs, y_blocks[0], z_blocks[0])
     swapped = send(coeffs, "core")
-    y_blocks, z_blocks, facts = [[block] for block in pieces(
-        [("y", 0, CHUNKS[0], False), ("z", 0, CHUNKS[0], False), ("y", 0, 0, True)], levels, pairs, coeffs, "one"
-    )]
-    facts = facts[0]
-    here, facts_core = [(facts, None, 0)], [(send(facts, "core"), None, 0)]
-    coeffs, y_blocks[0], z_blocks[0] = tie(coeffs, y_blocks[0], z_blocks[0])
-    cuts = [(which, begins[i], CHUNKS[i], i == last) for i in range(1, last + 1) for which in ("y", "z")]
-    blocks = pieces(cuts, levels, pairs, coeffs, "rest")
+    facts = facts_of(levels, pairs)
+    coeffs, facts = tie(coeffs, facts)
+    here, facts_core = [(facts, None, 0)], send(facts, "core")
+    facts_y, facts_z = send(jnp.concatenate([facts, facts_core], axis=0), "y"), send(facts, "z")
+    cuts = [(which, begins[i], CHUNKS[i]) for i in range(1, last + 1) for which in ("y", "z")]
+    blocks = pieces(cuts, coeffs, "rest")
     y_blocks += blocks[0::2]
     z_blocks += blocks[1::2]
     got_y, got_z = [], []
@@ -394,7 +399,7 @@
     (diag,) = pair_sums("diag", k_plus_g, [[(coeffs, None, 0)]], 0, 2 * tiles, [here])
     diag, swapped, coeffs = tie(diag, swapped, coeffs)
     own, own_packed = pair_sums(
-        "near", k_plus_g, [[(swapped, "core", 0)], [(coeffs, "core", 0)]], 0, tiles, [facts_core, here]
+        "near", k_plus_g, [[(swapped, "core", 0)], [(coeffs, "core", 0)]], 0, tiles, [[(facts_core, None, 0)], here]
     )
     tile_own = send(own_packed, "core")
     sums, before = None, own
@@ -410,11 +415,11 @@
             before = sums
         else:
             got_y[i], sums, tile_own = tie(got_y[i], sums, tile_own)
-            marked = mark(got_z[i])
+            marked = mark(got_z[i], facts_y, facts_z)
             other, marked = tie(send(got_y[i], "core"), marked)
             far, pairs_02, pairs_12, pair_1 = pair_sums(
                 "far", k_plus_g, blocks(other), begin, size,
-                [[(got_y[i], None, size)], here, [(got_z[i], None, size)], [(other, None, size)]], sums,
+                [[(facts_y, None, 0)], here, [(facts_z, None, 0)], [(facts_y, None, 1)]], sums,
             )
     tile_y = send(pairs_02, "y")
     tile_across = send(pair_1, "across")

time: 85 us -> 83 us (0.976)
  waiting for transfers between devices: 24.4 us -> 20.5 us
  other arithmetic: 0 us -> 3.78 us
  Pallas kernels: 40.9 us -> 37.9 us
  starting transfers between devices: 19.1 us -> 20.2 us
    ppermute x15 -> x17, waiting for transfers between devices: 24.4 us -> 20.5 us  [shards(): send = lambda value, name: lax.ppermute(value, 'blk', way[name])]
    pallas_call x2, Pallas kernels: 6.98 us -> 4.39 us  [the longest x1 2.99 us: pieces(): pl.pallas_call(functools.partial(pieces_body, cuts), in_specs=[anywhere],...]
    select_n x0 -> x1, other arithmetic: none -> 2.49 us  [shards(): jnp.where(upper, high, low)]
    concatenate x0 -> x1, other arithmetic: none -> 1.29 us  [shards(): jnp.concatenate([facts, facts_core], axis=0)]
    ppermute x15 -> x17, starting transfers between devices: 19.1 us -> 20.2 us  [shards(): send = lambda value, name: lax.ppermute(value, 'blk', way[name])]
  transfers between devices with their start and end apart: 15 -> 17, of which waited for: 6 -> 6; matrix products, arithmetic and copies ran while one was open for 0% -> 2% of each run, Pallas kernels for 37% -> 34%
where the time goes in v5:
time: 83 us; the launch traced here: 82.5 us
  Pallas kernels  37.9 us (46%)
  waiting for transfers between devices  20.5 us (25%)
  starting transfers between devices  20.2 us (24%)
  other arithmetic  3.78 us (5%)
    pallas_call x5, Pallas kernels, pair_sums(): pl.pallas_call(functools.partial(pair_body, kind, begin, tiles, plans(blo...  29.4 us
    ppermute x17, waiting for transfers between devices, shards(): send = lambda value, name: lax.ppermute(value, 'blk', way[name])  20.5 us
    ppermute x17, starting transfers between devices, shards(): send = lambda value, name: lax.ppermute(value, 'blk', way[name])  20.2 us
    pallas_call x1, Pallas kernels, final(): pl.pallas_call(final_body, in_specs=[vmem] * len(operands), out_specs=pl....  3.5 us
    pallas_call x1, Pallas kernels, pieces(): pl.pallas_call(functools.partial(pieces_body, cuts), in_specs=[anywhere],...  2.99 us
    select_n x1, other arithmetic, shards(): jnp.where(upper, high, low)  2.49 us
  transfers between devices with their start and end apart: 17, of which 6 were waited for; matrix products, arithmetic and copies ran while one was open for 2% of the time, Pallas kernels for 34%

profile of v5, /device:TPU:0, one launch (start us, length us, event | category | flops | bytes accessed | tf_op | source)
XLA Modules:
  0.0 82.5 jit_solution(3892981208068266432)
XLA Ops:
  0.0 2.5 %broadcast_select_fusion = (bf16[2,96,1792]{2,1,0:T(8,128)(2,1)}, bf16[2,96,1792]{2,1,0:T(8,128)(2,1)}) fusion(pred[]{:T(512)S(6)} %eq.3, bf16[2,96,12544]{2,1,0:T(8,128)(2,1)} %refs_1_.3), kind=kLoop, calls=%fused_computation | loop fusion | flops 688128 | bytes 2752513 | tf_op jit(solution)/shard_map/jit(_where)/select_n | solution.py:382
  2.5 0.5 collective-permute-start
  2.9 2.5 %collective-permute-start.1 = (bf16[2,96,1792]{2,1,0:T(8,128)(2,1)}, bf16[2,96,1792]{2,1,0:T(8,128)(2,1)}, u32[]{:S(2)}, u32[]{:S(2)}) collective-permute-start(bf16[2,96,1792]{2,1,0:T(8,128)(2,1)} %get-tuple-element.44), channel_id=1, source_target_pairs={{0,2},{1,3},{2,0},{3,1},{4,6},{5,7},{6,4},{7,5},{8,10},{9,11},{10,... | collective-permute-start | bytes 2064392 | tf_op jit(solution)/shard_map/ppermute | solution.py:374
  5.5 1.3 %collective-permute-start.2 = (bf16[2,96,1792]{2,1,0:T(8,128)(2,1)}, bf16[2,96,1792]{2,1,0:T(8,128)(2,1)}, u32[]{:S(2)}, u32[]{:S(2)}) collective-permute-start(bf16[2,96,1792]{2,1,0:T(8,128)(2,1)} %get-tuple-element.45), channel_id=1, source_target_pairs={{4,0},{5,1},{8,4},{9,5},{2,6},{3,7},{12,8},{13,9},{6,10},{7,11},{1... | collective-permute-start | bytes 2064392 | tf_op jit(solution)/shard_map/ppermute | solution.py:374
  6.7 1.4 %facts.1.refs_1_.refs_3_.refs_5_ = bf16[16,128]{1,0:T(8,128)(2,1)} custom-call(s32[1,96]{1,0:T(1,128)} %bitcast.1, s32[1,2]{1,0:T(1,128)} %pairs.1), custom_call_target="tpu_custom_call" | custom-call | flops 1000 | bytes 1000 | tf_op jit(solution)/shard_map/facts/pallas_call | solution.py:265
  8.1 3.0 %rest.1 = (bf16[2,96,2176]{2,1,0:T(8,128)(2,1)}, bf16[2,96,2176]{2,1,0:T(8,128)(2,1)}, bf16[2,96,2304]{2,1,0:T(8,128)(2,1)}, bf16[2,96,2304]{2,1,0:T(8,128)(2,1)}) custom-call(bf16[2,96,12544]{2,1,0:T(8,128)(2,1)} %refs_1_.3), custom_call_target="tpu_custom_call" | custom-call | flops 1000 | bytes 1000 | tf_op jit(solution)/shard_map/rest/pallas_call | solution.py:300
  11.1 3.6 %collective-permute-start.5 = (bf16[2,96,2176]{2,1,0:T(8,128)(2,1)}, bf16[2,96,2176]{2,1,0:T(8,128)(2,1)}, u32[]{:S(2)}, u32[]{:S(2)}) collective-permute-start(bf16[2,96,2176]{2,1,0:T(8,128)(2,1)} %get-tuple-element.50), channel_id=1, source_target_pairs={{0,2},{1,3},{2,0},{3,1},{4,6},{5,7},{6,4},{7,5},{8,10},{9,11},{10,... | collective-permute-start | bytes 2506760 | tf_op jit(solution)/shard_map/ppermute | solution.py:374
  14.8 1.3 %collective-permute-start.6 = (bf16[2,96,2176]{2,1,0:T(8,128)(2,1)}, bf16[2,96,2176]{2,1,0:T(8,128)(2,1)}, u32[]{:S(2)}, u32[]{:S(2)}) collective-permute-start(bf16[2,96,2176]{2,1,0:T(8,128)(2,1)} %get-tuple-element.51), channel_id=1, source_target_pairs={{4,0},{5,1},{8,4},{9,5},{2,6},{3,7},{12,8},{13,9},{6,10},{7,11},{1... | collective-permute-start | bytes 2506760 | tf_op jit(solution)/shard_map/ppermute | solution.py:374
  16.1 0.0 collective-permute-done.refs_0_
  16.1 0.1 collective-permute-start.3
  16.2 7.2 %diag.1 = f32[288,192]{1,0:T(8,128)} custom-call(f32[3,12544]{1,0:T(4,128)} %k_hbm.9, bf16[2,96,12544]{2,1,0:T(8,128)(2,1)} %refs_1_.3, bf16[16,128]{1,0:T(8,128)(2,1)} %facts.1.refs_1_.refs_3_.refs_5_), custom_call_target="tpu_custom_call" | custom-call | flops 1000 | bytes 1000 | tf_op jit(solution)/shard_map/diag/pallas_call | solution.py:214
  23.3 0.0 collective-permute-done.3.refs_2_
  23.4 5.4 %near.1 = (f32[288,192]{1,0:T(8,128)}, bf16[432,128]{1,0:T(8,128)(2,1)}) custom-call(f32[3,12544]{1,0:T(4,128)} %k_hbm.9, bf16[2,96,12544]{2,1,0:T(8,128)(2,1)} %collective-permute-done.refs_0_, bf16[2,96,12544]{2,1,0:T(8,128)(2,1)} %refs_1_.3, bf16[16,128]{1,0:T(8,128)(2,1)} %collective-permute-done.3.refs_2_, bf16[16,128]{1,0:T(8,128)(2,1)} %facts.1.refs_1_.refs_3_.refs_5_), custom_call_target="tpu_custom_call" | custom-call | flops 1000 | bytes 1000 | tf_op jit(solution)/shard_map/near/pallas_call | solution.py:214
  28.8 0.0 collective-permute-done.1.refs_0_
  28.8 0.0 collective-permute-done.2.refs_2_
  28.8 0.6 collective-permute-start.7
  29.4 2.5 %collective-permute-start.4 = (bf16[2,96,2304]{2,1,0:T(8,128)(2,1)}, bf16[2,96,2304]{2,1,0:T(8,128)(2,1)}, u32[]{:S(2)}, u32[]{:S(2)}) collective-permute-start(bf16[2,96,2304]{2,1,0:T(8,128)(2,1)} %get-tuple-element.39), channel_id=1, source_target_pairs={{0,2},{1,3},{2,0},{3,1},{4,6},{5,7},{6,4},{7,5},{8,10},{9,11},{10,... | collective-permute-start | bytes 2654216 | tf_op jit(solution)/shard_map/ppermute | solution.py:374
  31.9 1.3 %collective-permute-start.10 = (bf16[2,96,2304]{2,1,0:T(8,128)(2,1)}, bf16[2,96,2304]{2,1,0:T(8,128)(2,1)}, u32[]{:S(2)}, u32[]{:S(2)}) collective-permute-start(bf16[2,96,2304]{2,1,0:T(8,128)(2,1)} %get-tuple-element.40), channel_id=1, source_target_pairs={{4,0},{5,1},{8,4},{9,5},{2,6},{3,7},{12,8},{13,9},{6,10},{7,11},{1... | collective-permute-start | bytes 2654216 | tf_op jit(solution)/shard_map/ppermute | solution.py:374
  33.2 0.0 collective-permute-done.7.refs_3_
  33.2 5.0 %far.3.refs_4_ = f32[3,288,192]{2,1,0:T(8,128)} custom-call(f32[3,12544]{1,0:T(4,128)} %k_hbm.9, bf16[2,96,1792]{2,1,0:T(8,128)(2,1)} %collective-permute-done.1.refs_0_, bf16[2,96,12544]{2,1,0:T(8,128)(2,1)} %refs_1_.3, bf16[2,96,1792]{2,1,0:T(8,128)(2,1)} %collective-permute-done.2.refs_2_, bf16[2,96,1792]{2,1,0:T(8,128)(2,1)} %collective-permute-done.7.refs_3_), custom_call_target="tpu_custom_call" | custom-call | flops 1000 | bytes 1000 | tf_op jit(solution)/shard_map/far/pallas_call | solution.py:214
  38.3 1.7 %collective-permute-done.5.refs_0_ = bf16[2,96,2176]{2,1,0:T(8,128)(2,1)} collective-permute-done((bf16[2,96,2176]{2,1,0:T(8,128)(2,1)}, bf16[2,96,2176]{2,1,0:T(8,128)(2,1)}, u32[]{:S(2)}, u32[]{:S(2)}) %collective-permute-start.5) | collective-permute-done | bytes 835616 | tf_op jit(solution)/shard_map/ppermute | solution.py:374
  40.0 3.9 %collective-permute-done.6.refs_2_ = bf16[2,96,2176]{2,1,0:T(8,128)(2,1)} collective-permute-done((bf16[2,96,2176]{2,1,0:T(8,128)(2,1)}, bf16[2,96,2176]{2,1,0:T(8,128)(2,1)}, u32[]{:S(2)}, u32[]{:S(2)}) %collective-permute-start.6) | collective-permute-done | bytes 835616 | tf_op jit(solution)/shard_map/ppermute | solution.py:374
  43.8 0.0 collective-permute-start.8
  43.8 0.5 collective-permute-start.9
  44.3 1.3 %pad_maximum_fusion = bf16[32,128]{1,0:T(8,128)(2,1)} fusion(bf16[16,128]{1,0:T(8,128)(2,1)} %collective-permute-done.3.refs_2_, bf16[16,128]{1,0:T(8,128)(2,1)} %facts.1.refs_1_.refs_3_.refs_5_), kind=kLoop, calls=%fused_computation.2 | loop fusion | flops 16384 | bytes 16384 | tf_op jit(solution)/shard_map/concatenate | solution.py:388
  45.6 0.0 collective-permute-start.12
  45.6 0.9 %collective-permute-done.8.refs_3_ = bf16[2,96,2176]{2,1,0:T(8,128)(2,1)} collective-permute-done((bf16[2,96,2176]{2,1,0:T(8,128)(2,1)}, bf16[2,96,2176]{2,1,0:T(8,128)(2,1)}, u32[]{:S(2)}, u32[]{:S(2)}) %collective-permute-start.8) | collective-permute-done | bytes 835616 | tf_op jit(solution)/shard_map/ppermute | solution.py:374
  46.5 1.3 %collective-permute-start.13 = (bf16[16,128]{1,0:T(8,128)(2,1)}, bf16[16,128]{1,0:T(8,128)(2,1)}, u32[]{:S(2)}, u32[]{:S(2)}) collective-permute-start(bf16[16,128]{1,0:T(8,128)(2,1)} %facts.1.refs_1_.refs_3_.refs_5_), channel_id=1, source_target_pairs={{4,0},{5,1},{8,4},{9,5},{2,6},{3,7},{12,8},{13,9},{6,10},{7,11},{1... | collective-permute-start | bytes 12296 | tf_op jit(solution)/shard_map/ppermute | solution.py:374
  47.8 5.8 %far.4.refs_8_ = f32[3,288,192]{2,1,0:T(8,128)} custom-call(f32[3,12544]{1,0:T(4,128)} %k_hbm.9, bf16[2,96,2176]{2,1,0:T(8,128)(2,1)} %collective-permute-done.5.refs_0_, bf16[2,96,12544]{2,1,0:T(8,128)(2,1)} %refs_1_.3, bf16[2,96,2176]{2,1,0:T(8,128)(2,1)} %collective-permute-done.6.refs_2_, bf16[2,96,2176]{2,1,0:T(8,128)(2,1)} %collective-permute-done.8.refs_3_, ...), custom_call_target="tpu_custom_call" | custom-call | flops 1000 | bytes 1000 | tf_op jit(solution)/shard_map/far/pallas_call | solution.py:214
  53.6 5.2 %collective-permute-done.4.refs_0_ = bf16[2,96,2304]{2,1,0:T(8,128)(2,1)} collective-permute-done((bf16[2,96,2304]{2,1,0:T(8,128)(2,1)}, bf16[2,96,2304]{2,1,0:T(8,128)(2,1)}, u32[]{:S(2)}, u32[]{:S(2)}) %collective-permute-start.4) | collective-permute-done | bytes 884768 | tf_op jit(solution)/shard_map/ppermute | solution.py:374
  58.8 0.0 collective-permute-done.9.core
  58.8 0.0 collective-permute-start.11
  58.8 3.3 %collective-permute-done.13.refs_2_.refs_6_ = bf16[16,128]{1,0:T(8,128)(2,1)} collective-permute-done((bf16[16,128]{1,0:T(8,128)(2,1)}, bf16[16,128]{1,0:T(8,128)(2,1)}, u32[]{:S(2)}, u32[]{:S(2)}) %collective-permute-start.13) | collective-permute-done | bytes 4128 | tf_op jit(solution)/shard_map/ppermute | solution.py:374
  62.2 0.0 collective-permute-done.12.refs_1_.refs_4_.refs_7_
  62.2 0.0 collective-permute-done.10.refs_0_.refs_2_
  62.2 0.6 mark.1.marked
  62.8 0.0 collective-permute-done.11.refs_3_
  62.8 6.0 %far.5 = (f32[2,288,192]{2,1,0:T(8,128)}, bf16[2,432,128]{2,1,0:T(8,128)(2,1)}, bf16[2,432,128]{2,1,0:T(8,128)(2,1)}, bf16[432,128]{1,0:T(8,128)(2,1)}) custom-call(f32[3,12544]{1,0:T(4,128)} %k_hbm.9, bf16[2,96,2304]{2,1,0:T(8,128)(2,1)} %collective-permute-done.4.refs_0_, bf16[2,96,12544]{2,1,0:T(8,128)(2,1)} %refs_1_.3, ...), custom_call_target="tpu_custom_call" | custom-call | flops 1000 | bytes 1000 | tf_op jit(solution)/shard_map/far/pallas_call | solution.py:214
  68.8 0.6 collective-permute-start.14
  69.4 4.2 %collective-permute-start.16 = (bf16[2,432,128]{2,1,0:T(8,128)(2,1)}, bf16[2,432,128]{2,1,0:T(8,128)(2,1)}, u32[]{:S(2)}, u32[]{:S(2)}) collective-permute-start(bf16[2,432,128]{2,1,0:T(8,128)(2,1)} %get-tuple-element.65), channel_id=1, source_target_pairs={{0,4},{1,5},{4,8},{5,9},{6,2},{7,3},{8,12},{9,13},{10,6},{11,7},{1... | collective-permute-start | bytes 663560 | tf_op jit(solution)/shard_map/ppermute | solution.py:374
  73.6 0.0 collective-permute-start.15
  73.6 5.4 %collective-permute-done.15.across = bf16[432,128]{1,0:T(8,128)(2,1)} collective-permute-done((bf16[432,128]{1,0:T(8,128)(2,1)}, bf16[432,128]{1,0:T(8,128)(2,1)}, u32[]{:S(2)}, u32[]{:S(2)}) %collective-permute-start.15) | collective-permute-done | bytes 110624 | tf_op jit(solution)/shard_map/ppermute | solution.py:374
  79.0 0.0 collective-permute-done.14.up_y
  79.0 0.0 collective-permute-done.16.up_z
  79.0 3.5 %final.1 = f32[3,2,96,480]{3,2,1,0:T(8,128)} custom-call(f32[288,192]{1,0:T(8,128)} %diag.1, f32[288,192]{1,0:T(8,128)} %get-tuple-element.49.own, bf16[432,128]{1,0:T(8,128)(2,1)} %collective-permute-done.9.core, f32[2,288,192]{2,1,0:T(8,128)} %get-tuple-element.62.far, bf16[2,432,128]{2,1,0:T(8,128)(2,1)} %collective-permute-done.14.up_y, ...), custom_call_target="tpu_custom_call" | custom-call | tf_op jit(solution)/shard_map/final/pallas_call | solution.py:343
Async XLA Ops:
  2.5 13.6 %collective-permute-start = (bf16[2,96,12544]{2,1,0:T(8,128)(2,1)}, bf16[2,96,12544]{2,1,0:T(8,128)(2,1)}, u32[]{:S(2)}, u32[]{:S(2)}) collective-permute-start(bf16[2,96,12544]{2,1,0:T(8,128)(2,1)} %refs_1_.3), channel_id=1, source_target_pairs={{0,1},{1,0},{2,3},{3,2},{4,5},{5,4},{6,7},{7,6},{8,9},{9,8},{10,11... | collective-permute-start | bytes 14450696 | tf_op jit(solution)/shard_map/ppermute | solution.py:374
  2.9 25.9 %collective-permute-start.1 = (bf16[2,96,1792]{2,1,0:T(8,128)(2,1)}, bf16[2,96,1792]{2,1,0:T(8,128)(2,1)}, u32[]{:S(2)}, u32[]{:S(2)}) collective-permute-start(bf16[2,96,1792]{2,1,0:T(8,128)(2,1)} %get-tuple-element.44), channel_id=1, source_target_pairs={{0,2},{1,3},{2,0},{3,1},{4,6},{5,7},{6,4},{7,5},{8,10},{9,11},{10,... | collective-permute-start | bytes 2064392 | tf_op jit(solution)/shard_map/ppermute | solution.py:374
  5.5 23.4 %collective-permute-start.2 = (bf16[2,96,1792]{2,1,0:T(8,128)(2,1)}, bf16[2,96,1792]{2,1,0:T(8,128)(2,1)}, u32[]{:S(2)}, u32[]{:S(2)}) collective-permute-start(bf16[2,96,1792]{2,1,0:T(8,128)(2,1)} %get-tuple-element.45), channel_id=1, source_target_pairs={{4,0},{5,1},{8,4},{9,5},{2,6},{3,7},{12,8},{13,9},{6,10},{7,11},{1... | collective-permute-start | bytes 2064392 | tf_op jit(solution)/shard_map/ppermute | solution.py:374
  11.1 28.8 %collective-permute-start.5 = (bf16[2,96,2176]{2,1,0:T(8,128)(2,1)}, bf16[2,96,2176]{2,1,0:T(8,128)(2,1)}, u32[]{:S(2)}, u32[]{:S(2)}) collective-permute-start(bf16[2,96,2176]{2,1,0:T(8,128)(2,1)} %get-tuple-element.50), channel_id=1, source_target_pairs={{0,2},{1,3},{2,0},{3,1},{4,6},{5,7},{6,4},{7,5},{8,10},{9,11},{10,... | collective-permute-start | bytes 2506760 | tf_op jit(solution)/shard_map/ppermute | solution.py:374
  14.8 29.1 %collective-permute-start.6 = (bf16[2,96,2176]{2,1,0:T(8,128)(2,1)}, bf16[2,96,2176]{2,1,0:T(8,128)(2,1)}, u32[]{:S(2)}, u32[]{:S(2)}) collective-permute-start(bf16[2,96,2176]{2,1,0:T(8,128)(2,1)} %get-tuple-element.51), channel_id=1, source_target_pairs={{4,0},{5,1},{8,4},{9,5},{2,6},{3,7},{12,8},{13,9},{6,10},{7,11},{1... | collective-permute-start | bytes 2506760 | tf_op jit(solution)/shard_map/ppermute | solution.py:374
  16.1 7.3 %collective-permute-start.3 = (bf16[16,128]{1,0:T(8,128)(2,1)}, bf16[16,128]{1,0:T(8,128)(2,1)}, u32[]{:S(2)}, u32[]{:S(2)}) collective-permute-start(bf16[16,128]{1,0:T(8,128)(2,1)} %facts.1.refs_1_.refs_3_.refs_5_), channel_id=1, source_target_pairs={{0,1},{1,0},{2,3},{3,2},{4,5},{5,4},{6,7},{7,6},{8,9},{9,8},{10,11... | collective-permute-start | bytes 12296 | tf_op jit(solution)/shard_map/ppermute | solution.py:374
  28.8 4.4 %collective-permute-start.7 = (bf16[2,96,1792]{2,1,0:T(8,128)(2,1)}, bf16[2,96,1792]{2,1,0:T(8,128)(2,1)}, u32[]{:S(2)}, u32[]{:S(2)}) collective-permute-start(bf16[2,96,1792]{2,1,0:T(8,128)(2,1)} %collective-permute-done.1.refs_0_), channel_id=1, source_target_pairs={{0,1},{1,0},{2,3},{3,2},{4,5},{5,4},{6,7},{7,6},{8,9},{9,8},{10,11... | collective-permute-start | bytes 2064392 | tf_op jit(solution)/shard_map/ppermute | solution.py:374
  29.4 29.4 %collective-permute-start.4 = (bf16[2,96,2304]{2,1,0:T(8,128)(2,1)}, bf16[2,96,2304]{2,1,0:T(8,128)(2,1)}, u32[]{:S(2)}, u32[]{:S(2)}) collective-permute-start(bf16[2,96,2304]{2,1,0:T(8,128)(2,1)} %get-tuple-element.39), channel_id=1, source_target_pairs={{0,2},{1,3},{2,0},{3,1},{4,6},{5,7},{6,4},{7,5},{8,10},{9,11},{10,... | collective-permute-start | bytes 2654216 | tf_op jit(solution)/shard_map/ppermute | solution.py:374
  31.9 30.3 %collective-permute-start.10 = (bf16[2,96,2304]{2,1,0:T(8,128)(2,1)}, bf16[2,96,2304]{2,1,0:T(8,128)(2,1)}, u32[]{:S(2)}, u32[]{:S(2)}) collective-permute-start(bf16[2,96,2304]{2,1,0:T(8,128)(2,1)} %get-tuple-element.40), channel_id=1, source_target_pairs={{4,0},{5,1},{8,4},{9,5},{2,6},{3,7},{12,8},{13,9},{6,10},{7,11},{1... | collective-permute-start | bytes 2654216 | tf_op jit(solution)/shard_map/ppermute | solution.py:374
  43.8 2.7 %collective-permute-start.8 = (bf16[2,96,2176]{2,1,0:T(8,128)(2,1)}, bf16[2,96,2176]{2,1,0:T(8,128)(2,1)}, u32[]{:S(2)}, u32[]{:S(2)}) collective-permute-start(bf16[2,96,2176]{2,1,0:T(8,128)(2,1)} %collective-permute-done.5.refs_0_), channel_id=1, source_target_pairs={{0,1},{1,0},{2,3},{3,2},{4,5},{5,4},{6,7},{7,6},{8,9},{9,8},{10,11... | collective-permute-start | bytes 2506760 | tf_op jit(solution)/shard_map/ppermute | solution.py:374
  43.8 15.0 %collective-permute-start.9 = (bf16[432,128]{1,0:T(8,128)(2,1)}, bf16[432,128]{1,0:T(8,128)(2,1)}, u32[]{:S(2)}, u32[]{:S(2)}) collective-permute-start(bf16[432,128]{1,0:T(8,128)(2,1)} %get-tuple-element.57), channel_id=1, source_target_pairs={{0,1},{1,0},{2,3},{3,2},{4,5},{5,4},{6,7},{7,6},{8,9},{9,8},{10,11... | collective-permute-start | bytes 331784 | tf_op jit(solution)/shard_map/ppermute | solution.py:374
  45.6 16.5 %collective-permute-start.12 = (bf16[32,128]{1,0:T(8,128)(2,1)}, bf16[32,128]{1,0:T(8,128)(2,1)}, u32[]{:S(2)}, u32[]{:S(2)}) collective-permute-start(bf16[32,128]{1,0:T(8,128)(2,1)} %pad_maximum_fusion), channel_id=1, source_target_pairs={{0,2},{1,3},{2,0},{3,1},{4,6},{5,7},{6,4},{7,5},{8,10},{9,11},{10,... | collective-permute-start | bytes 24584 | tf_op jit(solution)/shard_map/ppermute | solution.py:374
  46.5 15.6 %collective-permute-start.13 = (bf16[16,128]{1,0:T(8,128)(2,1)}, bf16[16,128]{1,0:T(8,128)(2,1)}, u32[]{:S(2)}, u32[]{:S(2)}) collective-permute-start(bf16[16,128]{1,0:T(8,128)(2,1)} %facts.1.refs_1_.refs_3_.refs_5_), channel_id=1, source_target_pairs={{4,0},{5,1},{8,4},{9,5},{2,6},{3,7},{12,8},{13,9},{6,10},{7,11},{1... | collective-permute-start | bytes 12296 | tf_op jit(solution)/shard_map/ppermute | solution.py:374
  58.8 3.9 %collective-permute-start.11 = (bf16[2,96,2304]{2,1,0:T(8,128)(2,1)}, bf16[2,96,2304]{2,1,0:T(8,128)(2,1)}, u32[]{:S(2)}, u32[]{:S(2)}) collective-permute-start(bf16[2,96,2304]{2,1,0:T(8,128)(2,1)} %collective-permute-done.4.refs_0_), channel_id=1, source_target_pairs={{0,1},{1,0},{2,3},{3,2},{4,5},{5,4},{6,7},{7,6},{8,9},{9,8},{10,11... | collective-permute-start | bytes 2654216 | tf_op jit(solution)/shard_map/ppermute | solution.py:374
  68.8 10.2 %collective-permute-start.14 = (bf16[2,432,128]{2,1,0:T(8,128)(2,1)}, bf16[2,432,128]{2,1,0:T(8,128)(2,1)}, u32[]{:S(2)}, u32[]{:S(2)}) collective-permute-start(bf16[2,432,128]{2,1,0:T(8,128)(2,1)} %get-tuple-element.63), channel_id=1, source_target_pairs={{0,2},{1,3},{2,0},{3,1},{4,6},{5,7},{6,4},{7,5},{8,10},{9,11},{10,... | collective-permute-start | bytes 663560 | tf_op jit(solution)/shard_map/ppermute | solution.py:374
  69.4 9.6 %collective-permute-start.16 = (bf16[2,432,128]{2,1,0:T(8,128)(2,1)}, bf16[2,432,128]{2,1,0:T(8,128)(2,1)}, u32[]{:S(2)}, u32[]{:S(2)}) collective-permute-start(bf16[2,432,128]{2,1,0:T(8,128)(2,1)} %get-tuple-element.65), channel_id=1, source_target_pairs={{0,4},{1,5},{4,8},{5,9},{6,2},{7,3},{8,12},{9,13},{10,6},{11,7},{1... | collective-permute-start | bytes 663560 | tf_op jit(solution)/shard_map/ppermute | solution.py:374
  73.6 5.4 %collective-permute-start.15 = (bf16[432,128]{1,0:T(8,128)(2,1)}, bf16[432,128]{1,0:T(8,128)(2,1)}, u32[]{:S(2)}, u32[]{:S(2)}) collective-permute-start(bf16[432,128]{1,0:T(8,128)(2,1)} %get-tuple-element.64), channel_id=1, source_target_pairs={{0,3},{1,2},{2,1},{3,0},{4,7},{5,6},{6,5},{7,4},{8,11},{9,10},{10,... | collective-permute-start | bytes 331784 | tf_op jit(solution)/shard_map/ppermute | solution.py:374

commit v6 on v5

--- a/solution.py
+++ b/solution.py
@@ -376,10 +376,7 @@
 
     begins = [sum(CHUNKS[:i]) for i in range(len(CHUNKS))]
     last = len(CHUNKS) - 1
-    half, width = tiles * LANES, CHUNKS[0] * LANES
-    upper = lax.rem(lax.div(lax.axis_index("blk"), 2), 2) == 1
-    low, high = coeffs[:, :, :width], coeffs[:, :, half : half + width]
-    y_blocks, z_blocks = [jnp.where(upper, low, high)], [jnp.where(upper, high, low)]
+    y_blocks, z_blocks = [[block] for block in pieces([("y", 0, CHUNKS[0]), ("z", 0, CHUNKS[0])], coeffs, "one")]
     levels, coeffs, y_blocks[0], z_blocks[0] = tie(levels, coeffs, y_blocks[0], z_blocks[0])
     swapped = send(coeffs, "core")
     facts = facts_of(levels, pairs)

time: 83 us -> 82.8 us (level)
  other arithmetic: 3.78 us -> 1.29 us
  Pallas kernels: 37.9 us -> 40.1 us
    select_n x1 -> x0, other arithmetic: 2.49 us -> none  [shards(): jnp.where(upper, high, low)]
    pallas_call x1 -> x2, Pallas kernels: 2.99 us -> 5.21 us  [pieces(): pl.pallas_call(functools.partial(pieces_body, cuts), in_specs=[anywhere],...]
  transfers between devices with their start and end apart: 17 -> 17, of which waited for: 6 -> 6; matrix products, arithmetic and copies ran while one was open for 2% -> 2% of each run, Pallas kernels for 34% -> 35%
where the time goes in v6:
time: 82.8 us; the launch traced here: 82.3 us
  Pallas kernels  40.1 us (48%)
  waiting for transfers between devices  20.4 us (25%)
  starting transfers between devices  20.3 us (25%)
  other arithmetic  1.29 us (2%)
    pallas_call x5, Pallas kernels, pair_sums(): pl.pallas_call(functools.partial(pair_body, kind, begin, tiles, plans(blo...  29.4 us
    ppermute x17, waiting for transfers between devices, shards(): send = lambda value, name: lax.ppermute(value, 'blk', way[name])  20.4 us
    ppermute x17, starting transfers between devices, shards(): send = lambda value, name: lax.ppermute(value, 'blk', way[name])  20.3 us
    pallas_call x2, Pallas kernels, pieces(): pl.pallas_call(functools.partial(pieces_body, cuts), in_specs=[anywhere],...  5.21 us
    pallas_call x1, Pallas kernels, final(): pl.pallas_call(final_body, in_specs=[vmem] * len(operands), out_specs=pl....  3.5 us
  transfers between devices with their start and end apart: 17, of which 6 were waited for; matrix products, arithmetic and copies ran while one was open for 2% of the time, Pallas kernels for 35%

profile of v6, /device:TPU:0, one launch (start us, length us, event | category | flops | bytes accessed | tf_op | source)
XLA Modules:
  0.0 82.3 jit_solution(4039941804685590508)
XLA Ops:
  0.0 2.2 %one.1 = (bf16[2,96,1792]{2,1,0:T(8,128)(2,1)}, bf16[2,96,1792]{2,1,0:T(8,128)(2,1)}) custom-call(bf16[2,96,12544]{2,1,0:T(8,128)(2,1)} %refs_1_.3), custom_call_target="tpu_custom_call" | custom-call | flops 1000 | bytes 1000 | tf_op jit(solution)/shard_map/one/pallas_call | solution.py:300
  2.2 0.5 collective-permute-start
  2.7 2.6 %collective-permute-start.1 = (bf16[2,96,1792]{2,1,0:T(8,128)(2,1)}, bf16[2,96,1792]{2,1,0:T(8,128)(2,1)}, u32[]{:S(2)}, u32[]{:S(2)}) collective-permute-start(bf16[2,96,1792]{2,1,0:T(8,128)(2,1)} %get-tuple-element.48), channel_id=1, source_target_pairs={{0,2},{1,3},{2,0},{3,1},{4,6},{5,7},{6,4},{7,5},{8,10},{9,11},{10,... | collective-permute-start | bytes 2064392 | tf_op jit(solution)/shard_map/ppermute | solution.py:374
  5.3 1.3 %collective-permute-start.2 = (bf16[2,96,1792]{2,1,0:T(8,128)(2,1)}, bf16[2,96,1792]{2,1,0:T(8,128)(2,1)}, u32[]{:S(2)}, u32[]{:S(2)}) collective-permute-start(bf16[2,96,1792]{2,1,0:T(8,128)(2,1)} %get-tuple-element.49), channel_id=1, source_target_pairs={{4,0},{5,1},{8,4},{9,5},{2,6},{3,7},{12,8},{13,9},{6,10},{7,11},{1... | collective-permute-start | bytes 2064392 | tf_op jit(solution)/shard_map/ppermute | solution.py:374
  6.6 1.4 %facts.1.refs_1_.refs_3_.refs_5_ = bf16[16,128]{1,0:T(8,128)(2,1)} custom-call(s32[1,96]{1,0:T(1,128)} %bitcast.1, s32[1,2]{1,0:T(1,128)} %pairs.1), custom_call_target="tpu_custom_call" | custom-call | flops 1000 | bytes 1000 | tf_op jit(solution)/shard_map/facts/pallas_call | solution.py:265
  8.0 3.0 %rest.1 = (bf16[2,96,2176]{2,1,0:T(8,128)(2,1)}, bf16[2,96,2176]{2,1,0:T(8,128)(2,1)}, bf16[2,96,2304]{2,1,0:T(8,128)(2,1)}, bf16[2,96,2304]{2,1,0:T(8,128)(2,1)}) custom-call(bf16[2,96,12544]{2,1,0:T(8,128)(2,1)} %refs_1_.3), custom_call_target="tpu_custom_call" | custom-call | flops 1000 | bytes 1000 | tf_op jit(solution)/shard_map/rest/pallas_call | solution.py:300
  11.0 3.6 %collective-permute-start.5 = (bf16[2,96,2176]{2,1,0:T(8,128)(2,1)}, bf16[2,96,2176]{2,1,0:T(8,128)(2,1)}, u32[]{:S(2)}, u32[]{:S(2)}) collective-permute-start(bf16[2,96,2176]{2,1,0:T(8,128)(2,1)} %get-tuple-element.54), channel_id=1, source_target_pairs={{0,2},{1,3},{2,0},{3,1},{4,6},{5,7},{6,4},{7,5},{8,10},{9,11},{10,... | collective-permute-start | bytes 2506760 | tf_op jit(solution)/shard_map/ppermute | solution.py:374
  14.7 1.3 %collective-permute-start.6 = (bf16[2,96,2176]{2,1,0:T(8,128)(2,1)}, bf16[2,96,2176]{2,1,0:T(8,128)(2,1)}, u32[]{:S(2)}, u32[]{:S(2)}) collective-permute-start(bf16[2,96,2176]{2,1,0:T(8,128)(2,1)} %get-tuple-element.55), channel_id=1, source_target_pairs={{4,0},{5,1},{8,4},{9,5},{2,6},{3,7},{12,8},{13,9},{6,10},{7,11},{1... | collective-permute-start | bytes 2506760 | tf_op jit(solution)/shard_map/ppermute | solution.py:374
  15.9 0.0 collective-permute-done.refs_0_
  16.0 0.1 collective-permute-start.3
  16.0 7.2 %diag.1 = f32[288,192]{1,0:T(8,128)} custom-call(f32[3,12544]{1,0:T(4,128)} %k_hbm.9, bf16[2,96,12544]{2,1,0:T(8,128)(2,1)} %refs_1_.3, bf16[16,128]{1,0:T(8,128)(2,1)} %facts.1.refs_1_.refs_3_.refs_5_), custom_call_target="tpu_custom_call" | custom-call | flops 1000 | bytes 1000 | tf_op jit(solution)/shard_map/diag/pallas_call | solution.py:214
  23.2 0.0 collective-permute-done.3.refs_2_
  23.2 5.4 %near.1 = (f32[288,192]{1,0:T(8,128)}, bf16[432,128]{1,0:T(8,128)(2,1)}) custom-call(f32[3,12544]{1,0:T(4,128)} %k_hbm.9, bf16[2,96,12544]{2,1,0:T(8,128)(2,1)} %collective-permute-done.refs_0_, bf16[2,96,12544]{2,1,0:T(8,128)(2,1)} %refs_1_.3, bf16[16,128]{1,0:T(8,128)(2,1)} %collective-permute-done.3.refs_2_, bf16[16,128]{1,0:T(8,128)(2,1)} %facts.1.refs_1_.refs_3_.refs_5_), custom_call_target="tpu_custom_call" | custom-call | flops 1000 | bytes 1000 | tf_op jit(solution)/shard_map/near/pallas_call | solution.py:214
  28.7 0.0 collective-permute-done.1.refs_0_
  28.7 0.0 collective-permute-done.2.refs_2_
  28.7 0.6 collective-permute-start.7
  29.3 2.5 %collective-permute-start.4 = (bf16[2,96,2304]{2,1,0:T(8,128)(2,1)}, bf16[2,96,2304]{2,1,0:T(8,128)(2,1)}, u32[]{:S(2)}, u32[]{:S(2)}) collective-permute-start(bf16[2,96,2304]{2,1,0:T(8,128)(2,1)} %get-tuple-element.43), channel_id=1, source_target_pairs={{0,2},{1,3},{2,0},{3,1},{4,6},{5,7},{6,4},{7,5},{8,10},{9,11},{10,... | collective-permute-start | bytes 2654216 | tf_op jit(solution)/shard_map/ppermute | solution.py:374
  31.8 1.3 %collective-permute-start.10 = (bf16[2,96,2304]{2,1,0:T(8,128)(2,1)}, bf16[2,96,2304]{2,1,0:T(8,128)(2,1)}, u32[]{:S(2)}, u32[]{:S(2)}) collective-permute-start(bf16[2,96,2304]{2,1,0:T(8,128)(2,1)} %get-tuple-element.44), channel_id=1, source_target_pairs={{4,0},{5,1},{8,4},{9,5},{2,6},{3,7},{12,8},{13,9},{6,10},{7,11},{1... | collective-permute-start | bytes 2654216 | tf_op jit(solution)/shard_map/ppermute | solution.py:374
  33.1 0.0 collective-permute-done.7.refs_3_
  33.1 5.0 %far.3.refs_4_ = f32[3,288,192]{2,1,0:T(8,128)} custom-call(f32[3,12544]{1,0:T(4,128)} %k_hbm.9, bf16[2,96,1792]{2,1,0:T(8,128)(2,1)} %collective-permute-done.1.refs_0_, bf16[2,96,12544]{2,1,0:T(8,128)(2,1)} %refs_1_.3, bf16[2,96,1792]{2,1,0:T(8,128)(2,1)} %collective-permute-done.2.refs_2_, bf16[2,96,1792]{2,1,0:T(8,128)(2,1)} %collective-permute-done.7.refs_3_), custom_call_target="tpu_custom_call" | custom-call | flops 1000 | bytes 1000 | tf_op jit(solution)/shard_map/far/pallas_call | solution.py:214
  38.1 1.7 %collective-permute-done.5.refs_0_ = bf16[2,96,2176]{2,1,0:T(8,128)(2,1)} collective-permute-done((bf16[2,96,2176]{2,1,0:T(8,128)(2,1)}, bf16[2,96,2176]{2,1,0:T(8,128)(2,1)}, u32[]{:S(2)}, u32[]{:S(2)}) %collective-permute-start.5) | collective-permute-done | bytes 835616 | tf_op jit(solution)/shard_map/ppermute | solution.py:374
  39.9 3.9 %collective-permute-done.6.refs_2_ = bf16[2,96,2176]{2,1,0:T(8,128)(2,1)} collective-permute-done((bf16[2,96,2176]{2,1,0:T(8,128)(2,1)}, bf16[2,96,2176]{2,1,0:T(8,128)(2,1)}, u32[]{:S(2)}, u32[]{:S(2)}) %collective-permute-start.6) | collective-permute-done | bytes 835616 | tf_op jit(solution)/shard_map/ppermute | solution.py:374
  43.7 0.0 collective-permute-start.8
  43.7 0.5 collective-permute-start.9
  44.2 1.3 %pad_maximum_fusion = bf16[32,128]{1,0:T(8,128)(2,1)} fusion(bf16[16,128]{1,0:T(8,128)(2,1)} %collective-permute-done.3.refs_2_, bf16[16,128]{1,0:T(8,128)(2,1)} %facts.1.refs_1_.refs_3_.refs_5_), kind=kLoop, calls=%fused_computation | loop fusion | flops 16384 | bytes 16384 | tf_op jit(solution)/shard_map/concatenate | solution.py:385
  45.5 0.0 collective-permute-start.12
  45.5 0.9 %collective-permute-done.8.refs_3_ = bf16[2,96,2176]{2,1,0:T(8,128)(2,1)} collective-permute-done((bf16[2,96,2176]{2,1,0:T(8,128)(2,1)}, bf16[2,96,2176]{2,1,0:T(8,128)(2,1)}, u32[]{:S(2)}, u32[]{:S(2)}) %collective-permute-start.8) | collective-permute-done | bytes 835616 | tf_op jit(solution)/shard_map/ppermute | solution.py:374
  46.4 1.3 %collective-permute-start.13 = (bf16[16,128]{1,0:T(8,128)(2,1)}, bf16[16,128]{1,0:T(8,128)(2,1)}, u32[]{:S(2)}, u32[]{:S(2)}) collective-permute-start(bf16[16,128]{1,0:T(8,128)(2,1)} %facts.1.refs_1_.refs_3_.refs_5_), channel_id=1, source_target_pairs={{4,0},{5,1},{8,4},{9,5},{2,6},{3,7},{12,8},{13,9},{6,10},{7,11},{1... | collective-permute-start | bytes 12296 | tf_op jit(solution)/shard_map/ppermute | solution.py:374
  47.7 5.8 %far.4.refs_8_ = f32[3,288,192]{2,1,0:T(8,128)} custom-call(f32[3,12544]{1,0:T(4,128)} %k_hbm.9, bf16[2,96,2176]{2,1,0:T(8,128)(2,1)} %collective-permute-done.5.refs_0_, bf16[2,96,12544]{2,1,0:T(8,128)(2,1)} %refs_1_.3, bf16[2,96,2176]{2,1,0:T(8,128)(2,1)} %collective-permute-done.6.refs_2_, bf16[2,96,2176]{2,1,0:T(8,128)(2,1)} %collective-permute-done.8.refs_3_, ...), custom_call_target="tpu_custom_call" | custom-call | flops 1000 | bytes 1000 | tf_op jit(solution)/shard_map/far/pallas_call | solution.py:214
  53.5 5.1 %collective-permute-done.4.refs_0_ = bf16[2,96,2304]{2,1,0:T(8,128)(2,1)} collective-permute-done((bf16[2,96,2304]{2,1,0:T(8,128)(2,1)}, bf16[2,96,2304]{2,1,0:T(8,128)(2,1)}, u32[]{:S(2)}, u32[]{:S(2)}) %collective-permute-start.4) | collective-permute-done | bytes 884768 | tf_op jit(solution)/shard_map/ppermute | solution.py:374
  58.6 0.0 collective-permute-done.9.core
  58.6 0.0 collective-permute-start.11
  58.6 3.4 %collective-permute-done.13.refs_2_.refs_6_ = bf16[16,128]{1,0:T(8,128)(2,1)} collective-permute-done((bf16[16,128]{1,0:T(8,128)(2,1)}, bf16[16,128]{1,0:T(8,128)(2,1)}, u32[]{:S(2)}, u32[]{:S(2)}) %collective-permute-start.13) | collective-permute-done | bytes 4128 | tf_op jit(solution)/shard_map/ppermute | solution.py:374
  62.0 0.0 collective-permute-done.12.refs_1_.refs_4_.refs_7_
  62.0 0.0 collective-permute-done.10.refs_0_.refs_2_
  62.0 0.6 mark.1.marked
  62.6 0.0 collective-permute-done.11.refs_3_
  62.6 6.0 %far.5 = (f32[2,288,192]{2,1,0:T(8,128)}, bf16[2,432,128]{2,1,0:T(8,128)(2,1)}, bf16[2,432,128]{2,1,0:T(8,128)(2,1)}, bf16[432,128]{1,0:T(8,128)(2,1)}) custom-call(f32[3,12544]{1,0:T(4,128)} %k_hbm.9, bf16[2,96,2304]{2,1,0:T(8,128)(2,1)} %collective-permute-done.4.refs_0_, bf16[2,96,12544]{2,1,0:T(8,128)(2,1)} %refs_1_.3, ...), custom_call_target="tpu_custom_call" | custom-call | flops 1000 | bytes 1000 | tf_op jit(solution)/shard_map/far/pallas_call | solution.py:214
  68.6 0.6 collective-permute-start.14
  69.2 4.2 %collective-permute-start.16 = (bf16[2,432,128]{2,1,0:T(8,128)(2,1)}, bf16[2,432,128]{2,1,0:T(8,128)(2,1)}, u32[]{:S(2)}, u32[]{:S(2)}) collective-permute-start(bf16[2,432,128]{2,1,0:T(8,128)(2,1)} %get-tuple-element.69), channel_id=1, source_target_pairs={{0,4},{1,5},{4,8},{5,9},{6,2},{7,3},{8,12},{9,13},{10,6},{11,7},{1... | collective-permute-start | bytes 663560 | tf_op jit(solution)/shard_map/ppermute | solution.py:374
  73.4 0.0 collective-permute-start.15
  73.4 5.4 %collective-permute-done.15.across = bf16[432,128]{1,0:T(8,128)(2,1)} collective-permute-done((bf16[432,128]{1,0:T(8,128)(2,1)}, bf16[432,128]{1,0:T(8,128)(2,1)}, u32[]{:S(2)}, u32[]{:S(2)}) %collective-permute-start.15) | collective-permute-done | bytes 110624 | tf_op jit(solution)/shard_map/ppermute | solution.py:374
  78.8 0.0 collective-permute-done.14.up_y
  78.8 0.0 collective-permute-done.16.up_z
  78.8 3.5 %final.1 = f32[3,2,96,480]{3,2,1,0:T(8,128)} custom-call(f32[288,192]{1,0:T(8,128)} %diag.1, f32[288,192]{1,0:T(8,128)} %get-tuple-element.53.own, bf16[432,128]{1,0:T(8,128)(2,1)} %collective-permute-done.9.core, f32[2,288,192]{2,1,0:T(8,128)} %get-tuple-element.66.far, bf16[2,432,128]{2,1,0:T(8,128)(2,1)} %collective-permute-done.14.up_y, ...), custom_call_target="tpu_custom_call" | custom-call | tf_op jit(solution)/shard_map/final/pallas_call | solution.py:343
Async XLA Ops:
  2.2 13.7 %collective-permute-start = (bf16[2,96,12544]{2,1,0:T(8,128)(2,1)}, bf16[2,96,12544]{2,1,0:T(8,128)(2,1)}, u32[]{:S(2)}, u32[]{:S(2)}) collective-permute-start(bf16[2,96,12544]{2,1,0:T(8,128)(2,1)} %refs_1_.3), channel_id=1, source_target_pairs={{0,1},{1,0},{2,3},{3,2},{4,5},{5,4},{6,7},{7,6},{8,9},{9,8},{10,11... | collective-permute-start | bytes 14450696 | tf_op jit(solution)/shard_map/ppermute | solution.py:374
  2.7 25.9 %collective-permute-start.1 = (bf16[2,96,1792]{2,1,0:T(8,128)(2,1)}, bf16[2,96,1792]{2,1,0:T(8,128)(2,1)}, u32[]{:S(2)}, u32[]{:S(2)}) collective-permute-start(bf16[2,96,1792]{2,1,0:T(8,128)(2,1)} %get-tuple-element.48), channel_id=1, source_target_pairs={{0,2},{1,3},{2,0},{3,1},{4,6},{5,7},{6,4},{7,5},{8,10},{9,11},{10,... | collective-permute-start | bytes 2064392 | tf_op jit(solution)/shard_map/ppermute | solution.py:374
  5.3 23.4 %collective-permute-start.2 = (bf16[2,96,1792]{2,1,0:T(8,128)(2,1)}, bf16[2,96,1792]{2,1,0:T(8,128)(2,1)}, u32[]{:S(2)}, u32[]{:S(2)}) collective-permute-start(bf16[2,96,1792]{2,1,0:T(8,128)(2,1)} %get-tuple-element.49), channel_id=1, source_target_pairs={{4,0},{5,1},{8,4},{9,5},{2,6},{3,7},{12,8},{13,9},{6,10},{7,11},{1... | collective-permute-start | bytes 2064392 | tf_op jit(solution)/shard_map/ppermute | solution.py:374
  11.0 28.8 %collective-permute-start.5 = (bf16[2,96,2176]{2,1,0:T(8,128)(2,1)}, bf16[2,96,2176]{2,1,0:T(8,128)(2,1)}, u32[]{:S(2)}, u32[]{:S(2)}) collective-permute-start(bf16[2,96,2176]{2,1,0:T(8,128)(2,1)} %get-tuple-element.54), channel_id=1, source_target_pairs={{0,2},{1,3},{2,0},{3,1},{4,6},{5,7},{6,4},{7,5},{8,10},{9,11},{10,... | collective-permute-start | bytes 2506760 | tf_op jit(solution)/shard_map/ppermute | solution.py:374
  14.7 29.1 %collective-permute-start.6 = (bf16[2,96,2176]{2,1,0:T(8,128)(2,1)}, bf16[2,96,2176]{2,1,0:T(8,128)(2,1)}, u32[]{:S(2)}, u32[]{:S(2)}) collective-permute-start(bf16[2,96,2176]{2,1,0:T(8,128)(2,1)} %get-tuple-element.55), channel_id=1, source_target_pairs={{4,0},{5,1},{8,4},{9,5},{2,6},{3,7},{12,8},{13,9},{6,10},{7,11},{1... | collective-permute-start | bytes 2506760 | tf_op jit(solution)/shard_map/ppermute | solution.py:374
  16.0 7.3 %collective-permute-start.3 = (bf16[16,128]{1,0:T(8,128)(2,1)}, bf16[16,128]{1,0:T(8,128)(2,1)}, u32[]{:S(2)}, u32[]{:S(2)}) collective-permute-start(bf16[16,128]{1,0:T(8,128)(2,1)} %facts.1.refs_1_.refs_3_.refs_5_), channel_id=1, source_target_pairs={{0,1},{1,0},{2,3},{3,2},{4,5},{5,4},{6,7},{7,6},{8,9},{9,8},{10,11... | collective-permute-start | bytes 12296 | tf_op jit(solution)/shard_map/ppermute | solution.py:374
  28.7 4.4 %collective-permute-start.7 = (bf16[2,96,1792]{2,1,0:T(8,128)(2,1)}, bf16[2,96,1792]{2,1,0:T(8,128)(2,1)}, u32[]{:S(2)}, u32[]{:S(2)}) collective-permute-start(bf16[2,96,1792]{2,1,0:T(8,128)(2,1)} %collective-permute-done.1.refs_0_), channel_id=1, source_target_pairs={{0,1},{1,0},{2,3},{3,2},{4,5},{5,4},{6,7},{7,6},{8,9},{9,8},{10,11... | collective-permute-start | bytes 2064392 | tf_op jit(solution)/shard_map/ppermute | solution.py:374
  29.3 29.4 %collective-permute-start.4 = (bf16[2,96,2304]{2,1,0:T(8,128)(2,1)}, bf16[2,96,2304]{2,1,0:T(8,128)(2,1)}, u32[]{:S(2)}, u32[]{:S(2)}) collective-permute-start(bf16[2,96,2304]{2,1,0:T(8,128)(2,1)} %get-tuple-element.43), channel_id=1, source_target_pairs={{0,2},{1,3},{2,0},{3,1},{4,6},{5,7},{6,4},{7,5},{8,10},{9,11},{10,... | collective-permute-start | bytes 2654216 | tf_op jit(solution)/shard_map/ppermute | solution.py:374
  31.8 30.2 %collective-permute-start.10 = (bf16[2,96,2304]{2,1,0:T(8,128)(2,1)}, bf16[2,96,2304]{2,1,0:T(8,128)(2,1)}, u32[]{:S(2)}, u32[]{:S(2)}) collective-permute-start(bf16[2,96,2304]{2,1,0:T(8,128)(2,1)} %get-tuple-element.44), channel_id=1, source_target_pairs={{4,0},{5,1},{8,4},{9,5},{2,6},{3,7},{12,8},{13,9},{6,10},{7,11},{1... | collective-permute-start | bytes 2654216 | tf_op jit(solution)/shard_map/ppermute | solution.py:374
  43.7 2.7 %collective-permute-start.8 = (bf16[2,96,2176]{2,1,0:T(8,128)(2,1)}, bf16[2,96,2176]{2,1,0:T(8,128)(2,1)}, u32[]{:S(2)}, u32[]{:S(2)}) collective-permute-start(bf16[2,96,2176]{2,1,0:T(8,128)(2,1)} %collective-permute-done.5.refs_0_), channel_id=1, source_target_pairs={{0,1},{1,0},{2,3},{3,2},{4,5},{5,4},{6,7},{7,6},{8,9},{9,8},{10,11... | collective-permute-start | bytes 2506760 | tf_op jit(solution)/shard_map/ppermute | solution.py:374
  43.7 14.9 %collective-permute-start.9 = (bf16[432,128]{1,0:T(8,128)(2,1)}, bf16[432,128]{1,0:T(8,128)(2,1)}, u32[]{:S(2)}, u32[]{:S(2)}) collective-permute-start(bf16[432,128]{1,0:T(8,128)(2,1)} %get-tuple-element.61), channel_id=1, source_target_pairs={{0,1},{1,0},{2,3},{3,2},{4,5},{5,4},{6,7},{7,6},{8,9},{9,8},{10,11... | collective-permute-start | bytes 331784 | tf_op jit(solution)/shard_map/ppermute | solution.py:374
  45.5 16.5 %collective-permute-start.12 = (bf16[32,128]{1,0:T(8,128)(2,1)}, bf16[32,128]{1,0:T(8,128)(2,1)}, u32[]{:S(2)}, u32[]{:S(2)}) collective-permute-start(bf16[32,128]{1,0:T(8,128)(2,1)} %pad_maximum_fusion), channel_id=1, source_target_pairs={{0,2},{1,3},{2,0},{3,1},{4,6},{5,7},{6,4},{7,5},{8,10},{9,11},{10,... | collective-permute-start | bytes 24584 | tf_op jit(solution)/shard_map/ppermute | solution.py:374
  46.4 15.6 %collective-permute-start.13 = (bf16[16,128]{1,0:T(8,128)(2,1)}, bf16[16,128]{1,0:T(8,128)(2,1)}, u32[]{:S(2)}, u32[]{:S(2)}) collective-permute-start(bf16[16,128]{1,0:T(8,128)(2,1)} %facts.1.refs_1_.refs_3_.refs_5_), channel_id=1, source_target_pairs={{4,0},{5,1},{8,4},{9,5},{2,6},{3,7},{12,8},{13,9},{6,10},{7,11},{1... | collective-permute-start | bytes 12296 | tf_op jit(solution)/shard_map/ppermute | solution.py:374
  58.6 4.0 %collective-permute-start.11 = (bf16[2,96,2304]{2,1,0:T(8,128)(2,1)}, bf16[2,96,2304]{2,1,0:T(8,128)(2,1)}, u32[]{:S(2)}, u32[]{:S(2)}) collective-permute-start(bf16[2,96,2304]{2,1,0:T(8,128)(2,1)} %collective-permute-done.4.refs_0_), channel_id=1, source_target_pairs={{0,1},{1,0},{2,3},{3,2},{4,5},{5,4},{6,7},{7,6},{8,9},{9,8},{10,11... | collective-permute-start | bytes 2654216 | tf_op jit(solution)/shard_map/ppermute | solution.py:374
  68.6 10.2 %collective-permute-start.14 = (bf16[2,432,128]{2,1,0:T(8,128)(2,1)}, bf16[2,432,128]{2,1,0:T(8,128)(2,1)}, u32[]{:S(2)}, u32[]{:S(2)}) collective-permute-start(bf16[2,432,128]{2,1,0:T(8,128)(2,1)} %get-tuple-element.67), channel_id=1, source_target_pairs={{0,2},{1,3},{2,0},{3,1},{4,6},{5,7},{6,4},{7,5},{8,10},{9,11},{10,... | collective-permute-start | bytes 663560 | tf_op jit(solution)/shard_map/ppermute | solution.py:374
  69.2 9.6 %collective-permute-start.16 = (bf16[2,432,128]{2,1,0:T(8,128)(2,1)}, bf16[2,432,128]{2,1,0:T(8,128)(2,1)}, u32[]{:S(2)}, u32[]{:S(2)}) collective-permute-start(bf16[2,432,128]{2,1,0:T(8,128)(2,1)} %get-tuple-element.69), channel_id=1, source_target_pairs={{0,4},{1,5},{4,8},{5,9},{6,2},{7,3},{8,12},{9,13},{10,6},{11,7},{1... | collective-permute-start | bytes 663560 | tf_op jit(solution)/shard_map/ppermute | solution.py:374
  73.4 5.4 %collective-permute-start.15 = (bf16[432,128]{1,0:T(8,128)(2,1)}, bf16[432,128]{1,0:T(8,128)(2,1)}, u32[]{:S(2)}, u32[]{:S(2)}) collective-permute-start(bf16[432,128]{1,0:T(8,128)(2,1)} %get-tuple-element.68), channel_id=1, source_target_pairs={{0,3},{1,2},{2,1},{3,0},{4,7},{5,6},{6,5},{7,4},{8,11},{9,10},{10,... | collective-permute-start | bytes 331784 | tf_op jit(solution)/shard_map/ppermute | solution.py:374

commit v7 on v6

--- a/solution.py
+++ b/solution.py
@@ -328,10 +328,13 @@
     below = [jnp.where(low, away1, near1), jnp.where(low, away2, near2)]
     copies = []
     for a in range(3):
+        rows = slice(a * bands, (a + 1) * bands)
+        turned = [tile[rows].T for tile in (below[1], below[0])]
         for part in range(2):
-            cut = lambda tile: tile[a * bands : (a + 1) * bands, part * bands : (part + 1) * bands]
-            turn = lambda tile: -cut(tile).T if part == 0 else cut(tile).T
-            out[a, part] = jnp.concatenate([turn(below[1]), turn(below[0]), cut(diag), cut(above[0]), cut(above[1])], axis=1)
+            span = slice(part * bands, (part + 1) * bands)
+            mirrored = [-tile[span] if part == 0 else tile[span] for tile in turned]
+            straight = [tile[rows, span] for tile in (diag, *above)]
+            out[a, part] = jnp.concatenate(mirrored + straight, axis=1)
         copies.append(pltpu.make_async_copy(out.at[a], result.at[a], sems.at[a]))
         copies[-1].start()
     for copy in copies:

time: 82.8 us -> 82.3 us (level)
  no operation moved by 1% of the time
where the time goes in v7:
time: 82.3 us; the launch traced here: 81.8 us
  Pallas kernels  39.6 us (48%)
  waiting for transfers between devices  20.4 us (25%)
  starting transfers between devices  20.3 us (25%)
  other arithmetic  1.29 us (2%)
    pallas_call x5, Pallas kernels, pair_sums(): pl.pallas_call(functools.partial(pair_body, kind, begin, tiles, plans(blo...  29.4 us
    ppermute x17, waiting for transfers between devices, shards(): send = lambda value, name: lax.ppermute(value, 'blk', way[name])  20.4 us
    ppermute x17, starting transfers between devices, shards(): send = lambda value, name: lax.ppermute(value, 'blk', way[name])  20.3 us
    pallas_call x2, Pallas kernels, pieces(): pl.pallas_call(functools.partial(pieces_body, cuts), in_specs=[anywhere],...  5.21 us
    pallas_call x1, Pallas kernels, final(): pl.pallas_call(final_body, in_specs=[vmem] * len(operands), out_specs=pl....  2.93 us
  transfers between devices with their start and end apart: 17, of which 6 were waited for; matrix products, arithmetic and copies ran while one was open for 2% of the time, Pallas kernels for 35%

profile of v7, /device:TPU:0, one launch (start us, length us, event | category | flops | bytes accessed | tf_op | source)
XLA Modules:
  0.0 81.8 jit_solution(11524423811122955498)
XLA Ops:
  0.0 2.2 %one.1 = (bf16[2,96,1792]{2,1,0:T(8,128)(2,1)}, bf16[2,96,1792]{2,1,0:T(8,128)(2,1)}) custom-call(bf16[2,96,12544]{2,1,0:T(8,128)(2,1)} %refs_1_.3), custom_call_target="tpu_custom_call" | custom-call | flops 1000 | bytes 1000 | tf_op jit(solution)/shard_map/one/pallas_call | solution.py:300
  2.2 0.5 collective-permute-start
  2.7 2.6 %collective-permute-start.1 = (bf16[2,96,1792]{2,1,0:T(8,128)(2,1)}, bf16[2,96,1792]{2,1,0:T(8,128)(2,1)}, u32[]{:S(2)}, u32[]{:S(2)}) collective-permute-start(bf16[2,96,1792]{2,1,0:T(8,128)(2,1)} %get-tuple-element.48), channel_id=1, source_target_pairs={{0,2},{1,3},{2,0},{3,1},{4,6},{5,7},{6,4},{7,5},{8,10},{9,11},{10,... | collective-permute-start | bytes 2064392 | tf_op jit(solution)/shard_map/ppermute | solution.py:377
  5.3 1.3 %collective-permute-start.2 = (bf16[2,96,1792]{2,1,0:T(8,128)(2,1)}, bf16[2,96,1792]{2,1,0:T(8,128)(2,1)}, u32[]{:S(2)}, u32[]{:S(2)}) collective-permute-start(bf16[2,96,1792]{2,1,0:T(8,128)(2,1)} %get-tuple-element.49), channel_id=1, source_target_pairs={{4,0},{5,1},{8,4},{9,5},{2,6},{3,7},{12,8},{13,9},{6,10},{7,11},{1... | collective-permute-start | bytes 2064392 | tf_op jit(solution)/shard_map/ppermute | solution.py:377
  6.6 1.4 %facts.1.refs_1_.refs_3_.refs_5_ = bf16[16,128]{1,0:T(8,128)(2,1)} custom-call(s32[1,96]{1,0:T(1,128)} %bitcast.1, s32[1,2]{1,0:T(1,128)} %pairs.1), custom_call_target="tpu_custom_call" | custom-call | flops 1000 | bytes 1000 | tf_op jit(solution)/shard_map/facts/pallas_call | solution.py:265
  8.0 3.0 %rest.1 = (bf16[2,96,2176]{2,1,0:T(8,128)(2,1)}, bf16[2,96,2176]{2,1,0:T(8,128)(2,1)}, bf16[2,96,2304]{2,1,0:T(8,128)(2,1)}, bf16[2,96,2304]{2,1,0:T(8,128)(2,1)}) custom-call(bf16[2,96,12544]{2,1,0:T(8,128)(2,1)} %refs_1_.3), custom_call_target="tpu_custom_call" | custom-call | flops 1000 | bytes 1000 | tf_op jit(solution)/shard_map/rest/pallas_call | solution.py:300
  11.0 3.6 %collective-permute-start.5 = (bf16[2,96,2176]{2,1,0:T(8,128)(2,1)}, bf16[2,96,2176]{2,1,0:T(8,128)(2,1)}, u32[]{:S(2)}, u32[]{:S(2)}) collective-permute-start(bf16[2,96,2176]{2,1,0:T(8,128)(2,1)} %get-tuple-element.54), channel_id=1, source_target_pairs={{0,2},{1,3},{2,0},{3,1},{4,6},{5,7},{6,4},{7,5},{8,10},{9,11},{10,... | collective-permute-start | bytes 2506760 | tf_op jit(solution)/shard_map/ppermute | solution.py:377
  14.7 1.3 %collective-permute-start.6 = (bf16[2,96,2176]{2,1,0:T(8,128)(2,1)}, bf16[2,96,2176]{2,1,0:T(8,128)(2,1)}, u32[]{:S(2)}, u32[]{:S(2)}) collective-permute-start(bf16[2,96,2176]{2,1,0:T(8,128)(2,1)} %get-tuple-element.55), channel_id=1, source_target_pairs={{4,0},{5,1},{8,4},{9,5},{2,6},{3,7},{12,8},{13,9},{6,10},{7,11},{1... | collective-permute-start | bytes 2506760 | tf_op jit(solution)/shard_map/ppermute | solution.py:377
  15.9 0.0 collective-permute-done.refs_0_
  16.0 0.1 collective-permute-start.3
  16.0 7.2 %diag.1 = f32[288,192]{1,0:T(8,128)} custom-call(f32[3,12544]{1,0:T(4,128)} %k_hbm.9, bf16[2,96,12544]{2,1,0:T(8,128)(2,1)} %refs_1_.3, bf16[16,128]{1,0:T(8,128)(2,1)} %facts.1.refs_1_.refs_3_.refs_5_), custom_call_target="tpu_custom_call" | custom-call | flops 1000 | bytes 1000 | tf_op jit(solution)/shard_map/diag/pallas_call | solution.py:214
  23.2 0.0 collective-permute-done.3.refs_2_
  23.2 5.4 %near.1 = (f32[288,192]{1,0:T(8,128)}, bf16[432,128]{1,0:T(8,128)(2,1)}) custom-call(f32[3,12544]{1,0:T(4,128)} %k_hbm.9, bf16[2,96,12544]{2,1,0:T(8,128)(2,1)} %collective-permute-done.refs_0_, bf16[2,96,12544]{2,1,0:T(8,128)(2,1)} %refs_1_.3, bf16[16,128]{1,0:T(8,128)(2,1)} %collective-permute-done.3.refs_2_, bf16[16,128]{1,0:T(8,128)(2,1)} %facts.1.refs_1_.refs_3_.refs_5_), custom_call_target="tpu_custom_call" | custom-call | flops 1000 | bytes 1000 | tf_op jit(solution)/shard_map/near/pallas_call | solution.py:214
  28.7 0.0 collective-permute-done.1.refs_0_
  28.7 0.0 collective-permute-done.2.refs_2_
  28.7 0.6 collective-permute-start.7
  29.3 2.5 %collective-permute-start.4 = (bf16[2,96,2304]{2,1,0:T(8,128)(2,1)}, bf16[2,96,2304]{2,1,0:T(8,128)(2,1)}, u32[]{:S(2)}, u32[]{:S(2)}) collective-permute-start(bf16[2,96,2304]{2,1,0:T(8,128)(2,1)} %get-tuple-element.43), channel_id=1, source_target_pairs={{0,2},{1,3},{2,0},{3,1},{4,6},{5,7},{6,4},{7,5},{8,10},{9,11},{10,... | collective-permute-start | bytes 2654216 | tf_op jit(solution)/shard_map/ppermute | solution.py:377
  31.8 1.3 %collective-permute-start.10 = (bf16[2,96,2304]{2,1,0:T(8,128)(2,1)}, bf16[2,96,2304]{2,1,0:T(8,128)(2,1)}, u32[]{:S(2)}, u32[]{:S(2)}) collective-permute-start(bf16[2,96,2304]{2,1,0:T(8,128)(2,1)} %get-tuple-element.44), channel_id=1, source_target_pairs={{4,0},{5,1},{8,4},{9,5},{2,6},{3,7},{12,8},{13,9},{6,10},{7,11},{1... | collective-permute-start | bytes 2654216 | tf_op jit(solution)/shard_map/ppermute | solution.py:377
  33.1 0.0 collective-permute-done.7.refs_3_
  33.1 5.0 %far.3.refs_4_ = f32[3,288,192]{2,1,0:T(8,128)} custom-call(f32[3,12544]{1,0:T(4,128)} %k_hbm.9, bf16[2,96,1792]{2,1,0:T(8,128)(2,1)} %collective-permute-done.1.refs_0_, bf16[2,96,12544]{2,1,0:T(8,128)(2,1)} %refs_1_.3, bf16[2,96,1792]{2,1,0:T(8,128)(2,1)} %collective-permute-done.2.refs_2_, bf16[2,96,1792]{2,1,0:T(8,128)(2,1)} %collective-permute-done.7.refs_3_), custom_call_target="tpu_custom_call" | custom-call | flops 1000 | bytes 1000 | tf_op jit(solution)/shard_map/far/pallas_call | solution.py:214
  38.1 1.7 %collective-permute-done.5.refs_0_ = bf16[2,96,2176]{2,1,0:T(8,128)(2,1)} collective-permute-done((bf16[2,96,2176]{2,1,0:T(8,128)(2,1)}, bf16[2,96,2176]{2,1,0:T(8,128)(2,1)}, u32[]{:S(2)}, u32[]{:S(2)}) %collective-permute-start.5) | collective-permute-done | bytes 835616 | tf_op jit(solution)/shard_map/ppermute | solution.py:377
  39.9 3.9 %collective-permute-done.6.refs_2_ = bf16[2,96,2176]{2,1,0:T(8,128)(2,1)} collective-permute-done((bf16[2,96,2176]{2,1,0:T(8,128)(2,1)}, bf16[2,96,2176]{2,1,0:T(8,128)(2,1)}, u32[]{:S(2)}, u32[]{:S(2)}) %collective-permute-start.6) | collective-permute-done | bytes 835616 | tf_op jit(solution)/shard_map/ppermute | solution.py:377
  43.7 0.0 collective-permute-start.8
  43.7 0.5 collective-permute-start.9
  44.2 1.3 %pad_maximum_fusion = bf16[32,128]{1,0:T(8,128)(2,1)} fusion(bf16[16,128]{1,0:T(8,128)(2,1)} %collective-permute-done.3.refs_2_, bf16[16,128]{1,0:T(8,128)(2,1)} %facts.1.refs_1_.refs_3_.refs_5_), kind=kLoop, calls=%fused_computation | loop fusion | flops 16384 | bytes 16384 | tf_op jit(solution)/shard_map/concatenate | solution.py:388
  45.5 0.0 collective-permute-start.12
  45.5 0.9 %collective-permute-done.8.refs_3_ = bf16[2,96,2176]{2,1,0:T(8,128)(2,1)} collective-permute-done((bf16[2,96,2176]{2,1,0:T(8,128)(2,1)}, bf16[2,96,2176]{2,1,0:T(8,128)(2,1)}, u32[]{:S(2)}, u32[]{:S(2)}) %collective-permute-start.8) | collective-permute-done | bytes 835616 | tf_op jit(solution)/shard_map/ppermute | solution.py:377
  46.4 1.3 %collective-permute-start.13 = (bf16[16,128]{1,0:T(8,128)(2,1)}, bf16[16,128]{1,0:T(8,128)(2,1)}, u32[]{:S(2)}, u32[]{:S(2)}) collective-permute-start(bf16[16,128]{1,0:T(8,128)(2,1)} %facts.1.refs_1_.refs_3_.refs_5_), channel_id=1, source_target_pairs={{4,0},{5,1},{8,4},{9,5},{2,6},{3,7},{12,8},{13,9},{6,10},{7,11},{1... | collective-permute-start | bytes 12296 | tf_op jit(solution)/shard_map/ppermute | solution.py:377
  47.7 5.8 %far.4.refs_8_ = f32[3,288,192]{2,1,0:T(8,128)} custom-call(f32[3,12544]{1,0:T(4,128)} %k_hbm.9, bf16[2,96,2176]{2,1,0:T(8,128)(2,1)} %collective-permute-done.5.refs_0_, bf16[2,96,12544]{2,1,0:T(8,128)(2,1)} %refs_1_.3, bf16[2,96,2176]{2,1,0:T(8,128)(2,1)} %collective-permute-done.6.refs_2_, bf16[2,96,2176]{2,1,0:T(8,128)(2,1)} %collective-permute-done.8.refs_3_, ...), custom_call_target="tpu_custom_call" | custom-call | flops 1000 | bytes 1000 | tf_op jit(solution)/shard_map/far/pallas_call | solution.py:214
  53.5 5.1 %collective-permute-done.4.refs_0_ = bf16[2,96,2304]{2,1,0:T(8,128)(2,1)} collective-permute-done((bf16[2,96,2304]{2,1,0:T(8,128)(2,1)}, bf16[2,96,2304]{2,1,0:T(8,128)(2,1)}, u32[]{:S(2)}, u32[]{:S(2)}) %collective-permute-start.4) | collective-permute-done | bytes 884768 | tf_op jit(solution)/shard_map/ppermute | solution.py:377
  58.6 0.0 collective-permute-done.9.core
  58.6 0.0 collective-permute-start.11
  58.6 3.4 %collective-permute-done.13.refs_2_.refs_6_ = bf16[16,128]{1,0:T(8,128)(2,1)} collective-permute-done((bf16[16,128]{1,0:T(8,128)(2,1)}, bf16[16,128]{1,0:T(8,128)(2,1)}, u32[]{:S(2)}, u32[]{:S(2)}) %collective-permute-start.13) | collective-permute-done | bytes 4128 | tf_op jit(solution)/shard_map/ppermute | solution.py:377
  62.0 0.0 collective-permute-done.12.refs_1_.refs_4_.refs_7_
  62.0 0.0 collective-permute-done.10.refs_0_.refs_2_
  62.0 0.6 mark.1.marked
  62.6 0.0 collective-permute-done.11.refs_3_
  62.6 6.0 %far.5 = (f32[2,288,192]{2,1,0:T(8,128)}, bf16[2,432,128]{2,1,0:T(8,128)(2,1)}, bf16[2,432,128]{2,1,0:T(8,128)(2,1)}, bf16[432,128]{1,0:T(8,128)(2,1)}) custom-call(f32[3,12544]{1,0:T(4,128)} %k_hbm.9, bf16[2,96,2304]{2,1,0:T(8,128)(2,1)} %collective-permute-done.4.refs_0_, bf16[2,96,12544]{2,1,0:T(8,128)(2,1)} %refs_1_.3, ...), custom_call_target="tpu_custom_call" | custom-call | flops 1000 | bytes 1000 | tf_op jit(solution)/shard_map/far/pallas_call | solution.py:214
  68.6 0.6 collective-permute-start.14
  69.2 4.2 %collective-permute-start.16 = (bf16[2,432,128]{2,1,0:T(8,128)(2,1)}, bf16[2,432,128]{2,1,0:T(8,128)(2,1)}, u32[]{:S(2)}, u32[]{:S(2)}) collective-permute-start(bf16[2,432,128]{2,1,0:T(8,128)(2,1)} %get-tuple-element.69), channel_id=1, source_target_pairs={{0,4},{1,5},{4,8},{5,9},{6,2},{7,3},{8,12},{9,13},{10,6},{11,7},{1... | collective-permute-start | bytes 663560 | tf_op jit(solution)/shard_map/ppermute | solution.py:377
  73.4 0.0 collective-permute-start.15
  73.4 5.4 %collective-permute-done.15.across = bf16[432,128]{1,0:T(8,128)(2,1)} collective-permute-done((bf16[432,128]{1,0:T(8,128)(2,1)}, bf16[432,128]{1,0:T(8,128)(2,1)}, u32[]{:S(2)}, u32[]{:S(2)}) %collective-permute-start.15) | collective-permute-done | bytes 110624 | tf_op jit(solution)/shard_map/ppermute | solution.py:377
  78.8 0.0 collective-permute-done.14.up_y
  78.8 0.0 collective-permute-done.16.up_z
  78.8 2.9 %final.1 = f32[3,2,96,480]{3,2,1,0:T(8,128)} custom-call(f32[288,192]{1,0:T(8,128)} %diag.1, f32[288,192]{1,0:T(8,128)} %get-tuple-element.53.own, bf16[432,128]{1,0:T(8,128)(2,1)} %collective-permute-done.9.core, f32[2,288,192]{2,1,0:T(8,128)} %get-tuple-element.66.far, bf16[2,432,128]{2,1,0:T(8,128)(2,1)} %collective-permute-done.14.up_y, ...), custom_call_target="tpu_custom_call" | custom-call | tf_op jit(solution)/shard_map/final/pallas_call | solution.py:346
Async XLA Ops:
  2.2 13.7 %collective-permute-start = (bf16[2,96,12544]{2,1,0:T(8,128)(2,1)}, bf16[2,96,12544]{2,1,0:T(8,128)(2,1)}, u32[]{:S(2)}, u32[]{:S(2)}) collective-permute-start(bf16[2,96,12544]{2,1,0:T(8,128)(2,1)} %refs_1_.3), channel_id=1, source_target_pairs={{0,1},{1,0},{2,3},{3,2},{4,5},{5,4},{6,7},{7,6},{8,9},{9,8},{10,11... | collective-permute-start | bytes 14450696 | tf_op jit(solution)/shard_map/ppermute | solution.py:377
  2.7 25.9 %collective-permute-start.1 = (bf16[2,96,1792]{2,1,0:T(8,128)(2,1)}, bf16[2,96,1792]{2,1,0:T(8,128)(2,1)}, u32[]{:S(2)}, u32[]{:S(2)}) collective-permute-start(bf16[2,96,1792]{2,1,0:T(8,128)(2,1)} %get-tuple-element.48), channel_id=1, source_target_pairs={{0,2},{1,3},{2,0},{3,1},{4,6},{5,7},{6,4},{7,5},{8,10},{9,11},{10,... | collective-permute-start | bytes 2064392 | tf_op jit(solution)/shard_map/ppermute | solution.py:377
  5.3 23.4 %collective-permute-start.2 = (bf16[2,96,1792]{2,1,0:T(8,128)(2,1)}, bf16[2,96,1792]{2,1,0:T(8,128)(2,1)}, u32[]{:S(2)}, u32[]{:S(2)}) collective-permute-start(bf16[2,96,1792]{2,1,0:T(8,128)(2,1)} %get-tuple-element.49), channel_id=1, source_target_pairs={{4,0},{5,1},{8,4},{9,5},{2,6},{3,7},{12,8},{13,9},{6,10},{7,11},{1... | collective-permute-start | bytes 2064392 | tf_op jit(solution)/shard_map/ppermute | solution.py:377
  11.0 28.8 %collective-permute-start.5 = (bf16[2,96,2176]{2,1,0:T(8,128)(2,1)}, bf16[2,96,2176]{2,1,0:T(8,128)(2,1)}, u32[]{:S(2)}, u32[]{:S(2)}) collective-permute-start(bf16[2,96,2176]{2,1,0:T(8,128)(2,1)} %get-tuple-element.54), channel_id=1, source_target_pairs={{0,2},{1,3},{2,0},{3,1},{4,6},{5,7},{6,4},{7,5},{8,10},{9,11},{10,... | collective-permute-start | bytes 2506760 | tf_op jit(solution)/shard_map/ppermute | solution.py:377
  14.7 29.1 %collective-permute-start.6 = (bf16[2,96,2176]{2,1,0:T(8,128)(2,1)}, bf16[2,96,2176]{2,1,0:T(8,128)(2,1)}, u32[]{:S(2)}, u32[]{:S(2)}) collective-permute-start(bf16[2,96,2176]{2,1,0:T(8,128)(2,1)} %get-tuple-element.55), channel_id=1, source_target_pairs={{4,0},{5,1},{8,4},{9,5},{2,6},{3,7},{12,8},{13,9},{6,10},{7,11},{1... | collective-permute-start | bytes 2506760 | tf_op jit(solution)/shard_map/ppermute | solution.py:377
  16.0 7.3 %collective-permute-start.3 = (bf16[16,128]{1,0:T(8,128)(2,1)}, bf16[16,128]{1,0:T(8,128)(2,1)}, u32[]{:S(2)}, u32[]{:S(2)}) collective-permute-start(bf16[16,128]{1,0:T(8,128)(2,1)} %facts.1.refs_1_.refs_3_.refs_5_), channel_id=1, source_target_pairs={{0,1},{1,0},{2,3},{3,2},{4,5},{5,4},{6,7},{7,6},{8,9},{9,8},{10,11... | collective-permute-start | bytes 12296 | tf_op jit(solution)/shard_map/ppermute | solution.py:377
  28.7 4.4 %collective-permute-start.7 = (bf16[2,96,1792]{2,1,0:T(8,128)(2,1)}, bf16[2,96,1792]{2,1,0:T(8,128)(2,1)}, u32[]{:S(2)}, u32[]{:S(2)}) collective-permute-start(bf16[2,96,1792]{2,1,0:T(8,128)(2,1)} %collective-permute-done.1.refs_0_), channel_id=1, source_target_pairs={{0,1},{1,0},{2,3},{3,2},{4,5},{5,4},{6,7},{7,6},{8,9},{9,8},{10,11... | collective-permute-start | bytes 2064392 | tf_op jit(solution)/shard_map/ppermute | solution.py:377
  29.3 29.4 %collective-permute-start.4 = (bf16[2,96,2304]{2,1,0:T(8,128)(2,1)}, bf16[2,96,2304]{2,1,0:T(8,128)(2,1)}, u32[]{:S(2)}, u32[]{:S(2)}) collective-permute-start(bf16[2,96,2304]{2,1,0:T(8,128)(2,1)} %get-tuple-element.43), channel_id=1, source_target_pairs={{0,2},{1,3},{2,0},{3,1},{4,6},{5,7},{6,4},{7,5},{8,10},{9,11},{10,... | collective-permute-start | bytes 2654216 | tf_op jit(solution)/shard_map/ppermute | solution.py:377
  31.8 30.2 %collective-permute-start.10 = (bf16[2,96,2304]{2,1,0:T(8,128)(2,1)}, bf16[2,96,2304]{2,1,0:T(8,128)(2,1)}, u32[]{:S(2)}, u32[]{:S(2)}) collective-permute-start(bf16[2,96,2304]{2,1,0:T(8,128)(2,1)} %get-tuple-element.44), channel_id=1, source_target_pairs={{4,0},{5,1},{8,4},{9,5},{2,6},{3,7},{12,8},{13,9},{6,10},{7,11},{1... | collective-permute-start | bytes 2654216 | tf_op jit(solution)/shard_map/ppermute | solution.py:377
  43.7 2.7 %collective-permute-start.8 = (bf16[2,96,2176]{2,1,0:T(8,128)(2,1)}, bf16[2,96,2176]{2,1,0:T(8,128)(2,1)}, u32[]{:S(2)}, u32[]{:S(2)}) collective-permute-start(bf16[2,96,2176]{2,1,0:T(8,128)(2,1)} %collective-permute-done.5.refs_0_), channel_id=1, source_target_pairs={{0,1},{1,0},{2,3},{3,2},{4,5},{5,4},{6,7},{7,6},{8,9},{9,8},{10,11... | collective-permute-start | bytes 2506760 | tf_op jit(solution)/shard_map/ppermute | solution.py:377
  43.7 14.9 %collective-permute-start.9 = (bf16[432,128]{1,0:T(8,128)(2,1)}, bf16[432,128]{1,0:T(8,128)(2,1)}, u32[]{:S(2)}, u32[]{:S(2)}) collective-permute-start(bf16[432,128]{1,0:T(8,128)(2,1)} %get-tuple-element.61), channel_id=1, source_target_pairs={{0,1},{1,0},{2,3},{3,2},{4,5},{5,4},{6,7},{7,6},{8,9},{9,8},{10,11... | collective-permute-start | bytes 331784 | tf_op jit(solution)/shard_map/ppermute | solution.py:377
  45.5 16.5 %collective-permute-start.12 = (bf16[32,128]{1,0:T(8,128)(2,1)}, bf16[32,128]{1,0:T(8,128)(2,1)}, u32[]{:S(2)}, u32[]{:S(2)}) collective-permute-start(bf16[32,128]{1,0:T(8,128)(2,1)} %pad_maximum_fusion), channel_id=1, source_target_pairs={{0,2},{1,3},{2,0},{3,1},{4,6},{5,7},{6,4},{7,5},{8,10},{9,11},{10,... | collective-permute-start | bytes 24584 | tf_op jit(solution)/shard_map/ppermute | solution.py:377
  46.4 15.6 %collective-permute-start.13 = (bf16[16,128]{1,0:T(8,128)(2,1)}, bf16[16,128]{1,0:T(8,128)(2,1)}, u32[]{:S(2)}, u32[]{:S(2)}) collective-permute-start(bf16[16,128]{1,0:T(8,128)(2,1)} %facts.1.refs_1_.refs_3_.refs_5_), channel_id=1, source_target_pairs={{4,0},{5,1},{8,4},{9,5},{2,6},{3,7},{12,8},{13,9},{6,10},{7,11},{1... | collective-permute-start | bytes 12296 | tf_op jit(solution)/shard_map/ppermute | solution.py:377
  58.6 4.0 %collective-permute-start.11 = (bf16[2,96,2304]{2,1,0:T(8,128)(2,1)}, bf16[2,96,2304]{2,1,0:T(8,128)(2,1)}, u32[]{:S(2)}, u32[]{:S(2)}) collective-permute-start(bf16[2,96,2304]{2,1,0:T(8,128)(2,1)} %collective-permute-done.4.refs_0_), channel_id=1, source_target_pairs={{0,1},{1,0},{2,3},{3,2},{4,5},{5,4},{6,7},{7,6},{8,9},{9,8},{10,11... | collective-permute-start | bytes 2654216 | tf_op jit(solution)/shard_map/ppermute | solution.py:377
  68.6 10.2 %collective-permute-start.14 = (bf16[2,432,128]{2,1,0:T(8,128)(2,1)}, bf16[2,432,128]{2,1,0:T(8,128)(2,1)}, u32[]{:S(2)}, u32[]{:S(2)}) collective-permute-start(bf16[2,432,128]{2,1,0:T(8,128)(2,1)} %get-tuple-element.67), channel_id=1, source_target_pairs={{0,2},{1,3},{2,0},{3,1},{4,6},{5,7},{6,4},{7,5},{8,10},{9,11},{10,... | collective-permute-start | bytes 663560 | tf_op jit(solution)/shard_map/ppermute | solution.py:377
  69.2 9.6 %collective-permute-start.16 = (bf16[2,432,128]{2,1,0:T(8,128)(2,1)}, bf16[2,432,128]{2,1,0:T(8,128)(2,1)}, u32[]{:S(2)}, u32[]{:S(2)}) collective-permute-start(bf16[2,432,128]{2,1,0:T(8,128)(2,1)} %get-tuple-element.69), channel_id=1, source_target_pairs={{0,4},{1,5},{4,8},{5,9},{6,2},{7,3},{8,12},{9,13},{10,6},{11,7},{1... | collective-permute-start | bytes 663560 | tf_op jit(solution)/shard_map/ppermute | solution.py:377
  73.4 5.4 %collective-permute-start.15 = (bf16[432,128]{1,0:T(8,128)(2,1)}, bf16[432,128]{1,0:T(8,128)(2,1)}, u32[]{:S(2)}, u32[]{:S(2)}) collective-permute-start(bf16[432,128]{1,0:T(8,128)(2,1)} %get-tuple-element.68), channel_id=1, source_target_pairs={{0,3},{1,2},{2,1},{3,0},{4,7},{5,6},{6,5},{7,4},{8,11},{9,10},{10,... | collective-permute-start | bytes 331784 | tf_op jit(solution)/shard_map/ppermute | solution.py:377

commit v8 on v7

--- a/solution.py
+++ b/solution.py
@@ -282,9 +282,10 @@
     for n, (which, start, size) in enumerate(cuts):
         source = half * {"y": 1 - side, "z": side}[which] + start * LANES
         here = held.at[:, :, span(at * LANES, size)]
-        loads.append(pltpu.make_async_copy(coeffs.at[:, :, span(source, size)], here, sems.at[0, n]))
-        loads[-1].start()
-        stores.append(pltpu.make_async_copy(here, outs[n], sems.at[1, n]))
+        for part in range(2):
+            loads.append(pltpu.make_async_copy(coeffs.at[part, :, span(source, size)], here.at[part], sems.at[0, n, part]))
+            loads[-1].start()
+            stores.append(pltpu.make_async_copy(here.at[part], outs[n].at[part], sems.at[1, n, part]))
         at += size
     for load, store in zip(loads, stores):
         load.wait()
@@ -304,7 +305,7 @@
             out_shape=[jax.ShapeDtypeStruct((2, bands, size * LANES), BF16) for _, _, size in cuts],
             scratch_shapes=[
                 pltpu.VMEM((2, bands, sum(size for _, _, size in cuts) * LANES), BF16),
-                pltpu.SemaphoreType.DMA((2, len(cuts))),
+                pltpu.SemaphoreType.DMA((2, len(cuts), 2)),
             ],
             compiler_params=pltpu.CompilerParams(vmem_limit_bytes=VMEM_BYTES),
             cost_estimate=pl.CostEstimate(flops=1000, bytes_accessed=1000, transcendentals=0),

time: 82.3 us -> 82.2 us (level)
  no operation moved by 1% of the time
where the time goes in v8:
time: 82.2 us; the launch traced here: 81.7 us
  Pallas kernels  39.4 us (48%)
  waiting for transfers between devices  20.5 us (25%)
  starting transfers between devices  20.3 us (25%)
  other arithmetic  1.29 us (2%)
    pallas_call x5, Pallas kernels, pair_sums(): pl.pallas_call(functools.partial(pair_body, kind, begin, tiles, plans(blo...  29.4 us
    ppermute x17, waiting for transfers between devices, shards(): send = lambda value, name: lax.ppermute(value, 'blk', way[name])  20.5 us
    ppermute x17, starting transfers between devices, shards(): send = lambda value, name: lax.ppermute(value, 'blk', way[name])  20.3 us
    pallas_call x2, Pallas kernels, pieces(): pl.pallas_call(functools.partial(pieces_body, cuts), in_specs=[anywhere],...  5.04 us
    pallas_call x1, Pallas kernels, final(): pl.pallas_call(final_body, in_specs=[vmem] * len(operands), out_specs=pl....  2.93 us
  transfers between devices with their start and end apart: 17, of which 6 were waited for; matrix products, arithmetic and copies ran while one was open for 2% of the time, Pallas kernels for 35%

profile of v8, /device:TPU:0, one launch (start us, length us, event | category | flops | bytes accessed | tf_op | source)
XLA Modules:
  0.0 81.7 jit_solution(12643894548393996277)
XLA Ops:
  0.0 2.1 %one.1 = (bf16[2,96,1792]{2,1,0:T(8,128)(2,1)}, bf16[2,96,1792]{2,1,0:T(8,128)(2,1)}) custom-call(bf16[2,96,12544]{2,1,0:T(8,128)(2,1)} %refs_1_.3), custom_call_target="tpu_custom_call" | custom-call | flops 1000 | bytes 1000 | tf_op jit(solution)/shard_map/one/pallas_call | solution.py:301
  2.1 0.5 collective-permute-start
  2.7 2.6 %collective-permute-start.1 = (bf16[2,96,1792]{2,1,0:T(8,128)(2,1)}, bf16[2,96,1792]{2,1,0:T(8,128)(2,1)}, u32[]{:S(2)}, u32[]{:S(2)}) collective-permute-start(bf16[2,96,1792]{2,1,0:T(8,128)(2,1)} %get-tuple-element.48), channel_id=1, source_target_pairs={{0,2},{1,3},{2,0},{3,1},{4,6},{5,7},{6,4},{7,5},{8,10},{9,11},{10,... | collective-permute-start | bytes 2064392 | tf_op jit(solution)/shard_map/ppermute | solution.py:378
  5.3 1.3 %collective-permute-start.2 = (bf16[2,96,1792]{2,1,0:T(8,128)(2,1)}, bf16[2,96,1792]{2,1,0:T(8,128)(2,1)}, u32[]{:S(2)}, u32[]{:S(2)}) collective-permute-start(bf16[2,96,1792]{2,1,0:T(8,128)(2,1)} %get-tuple-element.49), channel_id=1, source_target_pairs={{4,0},{5,1},{8,4},{9,5},{2,6},{3,7},{12,8},{13,9},{6,10},{7,11},{1... | collective-permute-start | bytes 2064392 | tf_op jit(solution)/shard_map/ppermute | solution.py:378
  6.5 1.4 %facts.1.refs_1_.refs_3_.refs_5_ = bf16[16,128]{1,0:T(8,128)(2,1)} custom-call(s32[1,96]{1,0:T(1,128)} %bitcast.1, s32[1,2]{1,0:T(1,128)} %pairs.1), custom_call_target="tpu_custom_call" | custom-call | flops 1000 | bytes 1000 | tf_op jit(solution)/shard_map/facts/pallas_call | solution.py:265
  7.9 2.9 %rest.1 = (bf16[2,96,2176]{2,1,0:T(8,128)(2,1)}, bf16[2,96,2176]{2,1,0:T(8,128)(2,1)}, bf16[2,96,2304]{2,1,0:T(8,128)(2,1)}, bf16[2,96,2304]{2,1,0:T(8,128)(2,1)}) custom-call(bf16[2,96,12544]{2,1,0:T(8,128)(2,1)} %refs_1_.3), custom_call_target="tpu_custom_call" | custom-call | flops 1000 | bytes 1000 | tf_op jit(solution)/shard_map/rest/pallas_call | solution.py:301
  10.9 3.6 %collective-permute-start.5 = (bf16[2,96,2176]{2,1,0:T(8,128)(2,1)}, bf16[2,96,2176]{2,1,0:T(8,128)(2,1)}, u32[]{:S(2)}, u32[]{:S(2)}) collective-permute-start(bf16[2,96,2176]{2,1,0:T(8,128)(2,1)} %get-tuple-element.54), channel_id=1, source_target_pairs={{0,2},{1,3},{2,0},{3,1},{4,6},{5,7},{6,4},{7,5},{8,10},{9,11},{10,... | collective-permute-start | bytes 2506760 | tf_op jit(solution)/shard_map/ppermute | solution.py:378
  14.5 1.3 %collective-permute-start.6 = (bf16[2,96,2176]{2,1,0:T(8,128)(2,1)}, bf16[2,96,2176]{2,1,0:T(8,128)(2,1)}, u32[]{:S(2)}, u32[]{:S(2)}) collective-permute-start(bf16[2,96,2176]{2,1,0:T(8,128)(2,1)} %get-tuple-element.55), channel_id=1, source_target_pairs={{4,0},{5,1},{8,4},{9,5},{2,6},{3,7},{12,8},{13,9},{6,10},{7,11},{1... | collective-permute-start | bytes 2506760 | tf_op jit(solution)/shard_map/ppermute | solution.py:378
  15.8 0.0 collective-permute-done.refs_0_
  15.8 0.1 collective-permute-start.3
  15.9 7.2 %diag.1 = f32[288,192]{1,0:T(8,128)} custom-call(f32[3,12544]{1,0:T(4,128)} %k_hbm.9, bf16[2,96,12544]{2,1,0:T(8,128)(2,1)} %refs_1_.3, bf16[16,128]{1,0:T(8,128)(2,1)} %facts.1.refs_1_.refs_3_.refs_5_), custom_call_target="tpu_custom_call" | custom-call | flops 1000 | bytes 1000 | tf_op jit(solution)/shard_map/diag/pallas_call | solution.py:214
  23.1 0.0 collective-permute-done.3.refs_2_
  23.1 5.4 %near.1 = (f32[288,192]{1,0:T(8,128)}, bf16[432,128]{1,0:T(8,128)(2,1)}) custom-call(f32[3,12544]{1,0:T(4,128)} %k_hbm.9, bf16[2,96,12544]{2,1,0:T(8,128)(2,1)} %collective-permute-done.refs_0_, bf16[2,96,12544]{2,1,0:T(8,128)(2,1)} %refs_1_.3, bf16[16,128]{1,0:T(8,128)(2,1)} %collective-permute-done.3.refs_2_, bf16[16,128]{1,0:T(8,128)(2,1)} %facts.1.refs_1_.refs_3_.refs_5_), custom_call_target="tpu_custom_call" | custom-call | flops 1000 | bytes 1000 | tf_op jit(solution)/shard_map/near/pallas_call | solution.py:214
  28.5 0.0 collective-permute-done.1.refs_0_
  28.5 0.0 collective-permute-done.2.refs_2_
  28.5 0.6 collective-permute-start.7
  29.1 2.5 %collective-permute-start.4 = (bf16[2,96,2304]{2,1,0:T(8,128)(2,1)}, bf16[2,96,2304]{2,1,0:T(8,128)(2,1)}, u32[]{:S(2)}, u32[]{:S(2)}) collective-permute-start(bf16[2,96,2304]{2,1,0:T(8,128)(2,1)} %get-tuple-element.43), channel_id=1, source_target_pairs={{0,2},{1,3},{2,0},{3,1},{4,6},{5,7},{6,4},{7,5},{8,10},{9,11},{10,... | collective-permute-start | bytes 2654216 | tf_op jit(solution)/shard_map/ppermute | solution.py:378
  31.6 1.3 %collective-permute-start.10 = (bf16[2,96,2304]{2,1,0:T(8,128)(2,1)}, bf16[2,96,2304]{2,1,0:T(8,128)(2,1)}, u32[]{:S(2)}, u32[]{:S(2)}) collective-permute-start(bf16[2,96,2304]{2,1,0:T(8,128)(2,1)} %get-tuple-element.44), channel_id=1, source_target_pairs={{4,0},{5,1},{8,4},{9,5},{2,6},{3,7},{12,8},{13,9},{6,10},{7,11},{1... | collective-permute-start | bytes 2654216 | tf_op jit(solution)/shard_map/ppermute | solution.py:378
  32.9 0.0 collective-permute-done.7.refs_3_
  32.9 5.0 %far.3.refs_4_ = f32[3,288,192]{2,1,0:T(8,128)} custom-call(f32[3,12544]{1,0:T(4,128)} %k_hbm.9, bf16[2,96,1792]{2,1,0:T(8,128)(2,1)} %collective-permute-done.1.refs_0_, bf16[2,96,12544]{2,1,0:T(8,128)(2,1)} %refs_1_.3, bf16[2,96,1792]{2,1,0:T(8,128)(2,1)} %collective-permute-done.2.refs_2_, bf16[2,96,1792]{2,1,0:T(8,128)(2,1)} %collective-permute-done.7.refs_3_), custom_call_target="tpu_custom_call" | custom-call | flops 1000 | bytes 1000 | tf_op jit(solution)/shard_map/far/pallas_call | solution.py:214
  38.0 1.8 %collective-permute-done.5.refs_0_ = bf16[2,96,2176]{2,1,0:T(8,128)(2,1)} collective-permute-done((bf16[2,96,2176]{2,1,0:T(8,128)(2,1)}, bf16[2,96,2176]{2,1,0:T(8,128)(2,1)}, u32[]{:S(2)}, u32[]{:S(2)}) %collective-permute-start.5) | collective-permute-done | bytes 835616 | tf_op jit(solution)/shard_map/ppermute | solution.py:378
  39.8 3.9 %collective-permute-done.6.refs_2_ = bf16[2,96,2176]{2,1,0:T(8,128)(2,1)} collective-permute-done((bf16[2,96,2176]{2,1,0:T(8,128)(2,1)}, bf16[2,96,2176]{2,1,0:T(8,128)(2,1)}, u32[]{:S(2)}, u32[]{:S(2)}) %collective-permute-start.6) | collective-permute-done | bytes 835616 | tf_op jit(solution)/shard_map/ppermute | solution.py:378
  43.6 0.0 collective-permute-start.8
  43.6 0.5 collective-permute-start.9
  44.2 1.3 %pad_maximum_fusion = bf16[32,128]{1,0:T(8,128)(2,1)} fusion(bf16[16,128]{1,0:T(8,128)(2,1)} %collective-permute-done.3.refs_2_, bf16[16,128]{1,0:T(8,128)(2,1)} %facts.1.refs_1_.refs_3_.refs_5_), kind=kLoop, calls=%fused_computation | loop fusion | flops 16384 | bytes 16384 | tf_op jit(solution)/shard_map/concatenate | solution.py:389
  45.4 0.0 collective-permute-start.12
  45.4 0.9 %collective-permute-done.8.refs_3_ = bf16[2,96,2176]{2,1,0:T(8,128)(2,1)} collective-permute-done((bf16[2,96,2176]{2,1,0:T(8,128)(2,1)}, bf16[2,96,2176]{2,1,0:T(8,128)(2,1)}, u32[]{:S(2)}, u32[]{:S(2)}) %collective-permute-start.8) | collective-permute-done | bytes 835616 | tf_op jit(solution)/shard_map/ppermute | solution.py:378
  46.3 1.3 %collective-permute-start.13 = (bf16[16,128]{1,0:T(8,128)(2,1)}, bf16[16,128]{1,0:T(8,128)(2,1)}, u32[]{:S(2)}, u32[]{:S(2)}) collective-permute-start(bf16[16,128]{1,0:T(8,128)(2,1)} %facts.1.refs_1_.refs_3_.refs_5_), channel_id=1, source_target_pairs={{4,0},{5,1},{8,4},{9,5},{2,6},{3,7},{12,8},{13,9},{6,10},{7,11},{1... | collective-permute-start | bytes 12296 | tf_op jit(solution)/shard_map/ppermute | solution.py:378
  47.6 5.8 %far.4.refs_8_ = f32[3,288,192]{2,1,0:T(8,128)} custom-call(f32[3,12544]{1,0:T(4,128)} %k_hbm.9, bf16[2,96,2176]{2,1,0:T(8,128)(2,1)} %collective-permute-done.5.refs_0_, bf16[2,96,12544]{2,1,0:T(8,128)(2,1)} %refs_1_.3, bf16[2,96,2176]{2,1,0:T(8,128)(2,1)} %collective-permute-done.6.refs_2_, bf16[2,96,2176]{2,1,0:T(8,128)(2,1)} %collective-permute-done.8.refs_3_, ...), custom_call_target="tpu_custom_call" | custom-call | flops 1000 | bytes 1000 | tf_op jit(solution)/shard_map/far/pallas_call | solution.py:214
  53.4 5.1 %collective-permute-done.4.refs_0_ = bf16[2,96,2304]{2,1,0:T(8,128)(2,1)} collective-permute-done((bf16[2,96,2304]{2,1,0:T(8,128)(2,1)}, bf16[2,96,2304]{2,1,0:T(8,128)(2,1)}, u32[]{:S(2)}, u32[]{:S(2)}) %collective-permute-start.4) | collective-permute-done | bytes 884768 | tf_op jit(solution)/shard_map/ppermute | solution.py:378
  58.5 0.0 collective-permute-done.9.core
  58.6 0.0 collective-permute-start.11
  58.6 3.4 %collective-permute-done.13.refs_2_.refs_6_ = bf16[16,128]{1,0:T(8,128)(2,1)} collective-permute-done((bf16[16,128]{1,0:T(8,128)(2,1)}, bf16[16,128]{1,0:T(8,128)(2,1)}, u32[]{:S(2)}, u32[]{:S(2)}) %collective-permute-start.13) | collective-permute-done | bytes 4128 | tf_op jit(solution)/shard_map/ppermute | solution.py:378
  61.9 0.0 collective-permute-done.12.refs_1_.refs_4_.refs_7_
  61.9 0.0 collective-permute-done.10.refs_0_.refs_2_
  61.9 0.6 mark.1.marked
  62.5 0.0 collective-permute-done.11.refs_3_
  62.5 6.0 %far.5 = (f32[2,288,192]{2,1,0:T(8,128)}, bf16[2,432,128]{2,1,0:T(8,128)(2,1)}, bf16[2,432,128]{2,1,0:T(8,128)(2,1)}, bf16[432,128]{1,0:T(8,128)(2,1)}) custom-call(f32[3,12544]{1,0:T(4,128)} %k_hbm.9, bf16[2,96,2304]{2,1,0:T(8,128)(2,1)} %collective-permute-done.4.refs_0_, bf16[2,96,12544]{2,1,0:T(8,128)(2,1)} %refs_1_.3, ...), custom_call_target="tpu_custom_call" | custom-call | flops 1000 | bytes 1000 | tf_op jit(solution)/shard_map/far/pallas_call | solution.py:214
  68.5 0.6 collective-permute-start.14
  69.1 4.2 %collective-permute-start.16 = (bf16[2,432,128]{2,1,0:T(8,128)(2,1)}, bf16[2,432,128]{2,1,0:T(8,128)(2,1)}, u32[]{:S(2)}, u32[]{:S(2)}) collective-permute-start(bf16[2,432,128]{2,1,0:T(8,128)(2,1)} %get-tuple-element.69), channel_id=1, source_target_pairs={{0,4},{1,5},{4,8},{5,9},{6,2},{7,3},{8,12},{9,13},{10,6},{11,7},{1... | collective-permute-start | bytes 663560 | tf_op jit(solution)/shard_map/ppermute | solution.py:378
  73.3 0.0 collective-permute-start.15
  73.3 5.4 %collective-permute-done.15.across = bf16[432,128]{1,0:T(8,128)(2,1)} collective-permute-done((bf16[432,128]{1,0:T(8,128)(2,1)}, bf16[432,128]{1,0:T(8,128)(2,1)}, u32[]{:S(2)}, u32[]{:S(2)}) %collective-permute-start.15) | collective-permute-done | bytes 110624 | tf_op jit(solution)/shard_map/ppermute | solution.py:378
  78.7 0.0 collective-permute-done.14.up_y
  78.7 0.0 collective-permute-done.16.up_z
  78.7 2.9 %final.1 = f32[3,2,96,480]{3,2,1,0:T(8,128)} custom-call(f32[288,192]{1,0:T(8,128)} %diag.1, f32[288,192]{1,0:T(8,128)} %get-tuple-element.53.own, bf16[432,128]{1,0:T(8,128)(2,1)} %collective-permute-done.9.core, f32[2,288,192]{2,1,0:T(8,128)} %get-tuple-element.66.far, bf16[2,432,128]{2,1,0:T(8,128)(2,1)} %collective-permute-done.14.up_y, ...), custom_call_target="tpu_custom_call" | custom-call | tf_op jit(solution)/shard_map/final/pallas_call | solution.py:347
Async XLA Ops:
  2.1 13.6 %collective-permute-start = (bf16[2,96,12544]{2,1,0:T(8,128)(2,1)}, bf16[2,96,12544]{2,1,0:T(8,128)(2,1)}, u32[]{:S(2)}, u32[]{:S(2)}) collective-permute-start(bf16[2,96,12544]{2,1,0:T(8,128)(2,1)} %refs_1_.3), channel_id=1, source_target_pairs={{0,1},{1,0},{2,3},{3,2},{4,5},{5,4},{6,7},{7,6},{8,9},{9,8},{10,11... | collective-permute-start | bytes 14450696 | tf_op jit(solution)/shard_map/ppermute | solution.py:378
  2.7 25.9 %collective-permute-start.1 = (bf16[2,96,1792]{2,1,0:T(8,128)(2,1)}, bf16[2,96,1792]{2,1,0:T(8,128)(2,1)}, u32[]{:S(2)}, u32[]{:S(2)}) collective-permute-start(bf16[2,96,1792]{2,1,0:T(8,128)(2,1)} %get-tuple-element.48), channel_id=1, source_target_pairs={{0,2},{1,3},{2,0},{3,1},{4,6},{5,7},{6,4},{7,5},{8,10},{9,11},{10,... | collective-permute-start | bytes 2064392 | tf_op jit(solution)/shard_map/ppermute | solution.py:378
  5.3 23.3 %collective-permute-start.2 = (bf16[2,96,1792]{2,1,0:T(8,128)(2,1)}, bf16[2,96,1792]{2,1,0:T(8,128)(2,1)}, u32[]{:S(2)}, u32[]{:S(2)}) collective-permute-start(bf16[2,96,1792]{2,1,0:T(8,128)(2,1)} %get-tuple-element.49), channel_id=1, source_target_pairs={{4,0},{5,1},{8,4},{9,5},{2,6},{3,7},{12,8},{13,9},{6,10},{7,11},{1... | collective-permute-start | bytes 2064392 | tf_op jit(solution)/shard_map/ppermute | solution.py:378
  10.9 28.9 %collective-permute-start.5 = (bf16[2,96,2176]{2,1,0:T(8,128)(2,1)}, bf16[2,96,2176]{2,1,0:T(8,128)(2,1)}, u32[]{:S(2)}, u32[]{:S(2)}) collective-permute-start(bf16[2,96,2176]{2,1,0:T(8,128)(2,1)} %get-tuple-element.54), channel_id=1, source_target_pairs={{0,2},{1,3},{2,0},{3,1},{4,6},{5,7},{6,4},{7,5},{8,10},{9,11},{10,... | collective-permute-start | bytes 2506760 | tf_op jit(solution)/shard_map/ppermute | solution.py:378
  14.5 29.2 %collective-permute-start.6 = (bf16[2,96,2176]{2,1,0:T(8,128)(2,1)}, bf16[2,96,2176]{2,1,0:T(8,128)(2,1)}, u32[]{:S(2)}, u32[]{:S(2)}) collective-permute-start(bf16[2,96,2176]{2,1,0:T(8,128)(2,1)} %get-tuple-element.55), channel_id=1, source_target_pairs={{4,0},{5,1},{8,4},{9,5},{2,6},{3,7},{12,8},{13,9},{6,10},{7,11},{1... | collective-permute-start | bytes 2506760 | tf_op jit(solution)/shard_map/ppermute | solution.py:378
  15.8 7.3 %collective-permute-start.3 = (bf16[16,128]{1,0:T(8,128)(2,1)}, bf16[16,128]{1,0:T(8,128)(2,1)}, u32[]{:S(2)}, u32[]{:S(2)}) collective-permute-start(bf16[16,128]{1,0:T(8,128)(2,1)} %facts.1.refs_1_.refs_3_.refs_5_), channel_id=1, source_target_pairs={{0,1},{1,0},{2,3},{3,2},{4,5},{5,4},{6,7},{7,6},{8,9},{9,8},{10,11... | collective-permute-start | bytes 12296 | tf_op jit(solution)/shard_map/ppermute | solution.py:378
  28.5 4.4 %collective-permute-start.7 = (bf16[2,96,1792]{2,1,0:T(8,128)(2,1)}, bf16[2,96,1792]{2,1,0:T(8,128)(2,1)}, u32[]{:S(2)}, u32[]{:S(2)}) collective-permute-start(bf16[2,96,1792]{2,1,0:T(8,128)(2,1)} %collective-permute-done.1.refs_0_), channel_id=1, source_target_pairs={{0,1},{1,0},{2,3},{3,2},{4,5},{5,4},{6,7},{7,6},{8,9},{9,8},{10,11... | collective-permute-start | bytes 2064392 | tf_op jit(solution)/shard_map/ppermute | solution.py:378
  29.1 29.5 %collective-permute-start.4 = (bf16[2,96,2304]{2,1,0:T(8,128)(2,1)}, bf16[2,96,2304]{2,1,0:T(8,128)(2,1)}, u32[]{:S(2)}, u32[]{:S(2)}) collective-permute-start(bf16[2,96,2304]{2,1,0:T(8,128)(2,1)} %get-tuple-element.43), channel_id=1, source_target_pairs={{0,2},{1,3},{2,0},{3,1},{4,6},{5,7},{6,4},{7,5},{8,10},{9,11},{10,... | collective-permute-start | bytes 2654216 | tf_op jit(solution)/shard_map/ppermute | solution.py:378
  31.6 30.3 %collective-permute-start.10 = (bf16[2,96,2304]{2,1,0:T(8,128)(2,1)}, bf16[2,96,2304]{2,1,0:T(8,128)(2,1)}, u32[]{:S(2)}, u32[]{:S(2)}) collective-permute-start(bf16[2,96,2304]{2,1,0:T(8,128)(2,1)} %get-tuple-element.44), channel_id=1, source_target_pairs={{4,0},{5,1},{8,4},{9,5},{2,6},{3,7},{12,8},{13,9},{6,10},{7,11},{1... | collective-permute-start | bytes 2654216 | tf_op jit(solution)/shard_map/ppermute | solution.py:378
  43.6 2.7 %collective-permute-start.8 = (bf16[2,96,2176]{2,1,0:T(8,128)(2,1)}, bf16[2,96,2176]{2,1,0:T(8,128)(2,1)}, u32[]{:S(2)}, u32[]{:S(2)}) collective-permute-start(bf16[2,96,2176]{2,1,0:T(8,128)(2,1)} %collective-permute-done.5.refs_0_), channel_id=1, source_target_pairs={{0,1},{1,0},{2,3},{3,2},{4,5},{5,4},{6,7},{7,6},{8,9},{9,8},{10,11... | collective-permute-start | bytes 2506760 | tf_op jit(solution)/shard_map/ppermute | solution.py:378
  43.6 14.9 %collective-permute-start.9 = (bf16[432,128]{1,0:T(8,128)(2,1)}, bf16[432,128]{1,0:T(8,128)(2,1)}, u32[]{:S(2)}, u32[]{:S(2)}) collective-permute-start(bf16[432,128]{1,0:T(8,128)(2,1)} %get-tuple-element.61), channel_id=1, source_target_pairs={{0,1},{1,0},{2,3},{3,2},{4,5},{5,4},{6,7},{7,6},{8,9},{9,8},{10,11... | collective-permute-start | bytes 331784 | tf_op jit(solution)/shard_map/ppermute | solution.py:378
  45.4 16.5 %collective-permute-start.12 = (bf16[32,128]{1,0:T(8,128)(2,1)}, bf16[32,128]{1,0:T(8,128)(2,1)}, u32[]{:S(2)}, u32[]{:S(2)}) collective-permute-start(bf16[32,128]{1,0:T(8,128)(2,1)} %pad_maximum_fusion), channel_id=1, source_target_pairs={{0,2},{1,3},{2,0},{3,1},{4,6},{5,7},{6,4},{7,5},{8,10},{9,11},{10,... | collective-permute-start | bytes 24584 | tf_op jit(solution)/shard_map/ppermute | solution.py:378
  46.3 15.6 %collective-permute-start.13 = (bf16[16,128]{1,0:T(8,128)(2,1)}, bf16[16,128]{1,0:T(8,128)(2,1)}, u32[]{:S(2)}, u32[]{:S(2)}) collective-permute-start(bf16[16,128]{1,0:T(8,128)(2,1)} %facts.1.refs_1_.refs_3_.refs_5_), channel_id=1, source_target_pairs={{4,0},{5,1},{8,4},{9,5},{2,6},{3,7},{12,8},{13,9},{6,10},{7,11},{1... | collective-permute-start | bytes 12296 | tf_op jit(solution)/shard_map/ppermute | solution.py:378
  58.6 4.0 %collective-permute-start.11 = (bf16[2,96,2304]{2,1,0:T(8,128)(2,1)}, bf16[2,96,2304]{2,1,0:T(8,128)(2,1)}, u32[]{:S(2)}, u32[]{:S(2)}) collective-permute-start(bf16[2,96,2304]{2,1,0:T(8,128)(2,1)} %collective-permute-done.4.refs_0_), channel_id=1, source_target_pairs={{0,1},{1,0},{2,3},{3,2},{4,5},{5,4},{6,7},{7,6},{8,9},{9,8},{10,11... | collective-permute-start | bytes 2654216 | tf_op jit(solution)/shard_map/ppermute | solution.py:378
  68.5 10.2 %collective-permute-start.14 = (bf16[2,432,128]{2,1,0:T(8,128)(2,1)}, bf16[2,432,128]{2,1,0:T(8,128)(2,1)}, u32[]{:S(2)}, u32[]{:S(2)}) collective-permute-start(bf16[2,432,128]{2,1,0:T(8,128)(2,1)} %get-tuple-element.67), channel_id=1, source_target_pairs={{0,2},{1,3},{2,0},{3,1},{4,6},{5,7},{6,4},{7,5},{8,10},{9,11},{10,... | collective-permute-start | bytes 663560 | tf_op jit(solution)/shard_map/ppermute | solution.py:378
  69.1 9.6 %collective-permute-start.16 = (bf16[2,432,128]{2,1,0:T(8,128)(2,1)}, bf16[2,432,128]{2,1,0:T(8,128)(2,1)}, u32[]{:S(2)}, u32[]{:S(2)}) collective-permute-start(bf16[2,432,128]{2,1,0:T(8,128)(2,1)} %get-tuple-element.69), channel_id=1, source_target_pairs={{0,4},{1,5},{4,8},{5,9},{6,2},{7,3},{8,12},{9,13},{10,6},{11,7},{1... | collective-permute-start | bytes 663560 | tf_op jit(solution)/shard_map/ppermute | solution.py:378
  73.3 5.4 %collective-permute-start.15 = (bf16[432,128]{1,0:T(8,128)(2,1)}, bf16[432,128]{1,0:T(8,128)(2,1)}, u32[]{:S(2)}, u32[]{:S(2)}) collective-permute-start(bf16[432,128]{1,0:T(8,128)(2,1)} %get-tuple-element.68), channel_id=1, source_target_pairs={{0,3},{1,2},{2,1},{3,0},{4,7},{5,6},{6,5},{7,4},{8,11},{9,10},{10,... | collective-permute-start | bytes 331784 | tf_op jit(solution)/shard_map/ppermute | solution.py:378

commit v9 on v8

--- a/solution.py
+++ b/solution.py
@@ -171,11 +171,6 @@
         tile = tile * jnp.concatenate([weights[i]] * 3, axis=0)
         if count == 1:
             outs[0][...] = tile
-        else:
-            @pl.when(i < 2)
-            def _():
-                outs[0][i] = tile
-
         if kind == "near":
             outs[1][...] = pack(tile).astype(BF16)
         if kind == "far":
@@ -183,15 +178,15 @@
 
             @pl.when(i != 1)
             def _():
-                outs[1][i // 2] = packed
+                outs[0][i // 2] = packed
 
             @pl.when(i > 0)
             def _():
-                outs[2][i - 1] = packed
+                outs[1][i - 1] = packed
 
             @pl.when(i == 1)
             def _():
-                outs[3][...] = packed
+                outs[2][...] = packed
 
 
 def pair_sums(kind, k, blocks, begin, tiles, facts=None, start=None):
@@ -207,7 +202,7 @@
     if not ends:
         out_shape = [jax.ShapeDtypeStruct(shape, F32)]
     elif kind == "far":
-        out_shape = [jax.ShapeDtypeStruct((2, *tile), F32)] + [jax.ShapeDtypeStruct((2, *packed), BF16)] * 2
+        out_shape = [jax.ShapeDtypeStruct((2, *packed), BF16)] * 2
         out_shape.append(jax.ShapeDtypeStruct(packed, BF16))
     else:
         out_shape = [jax.ShapeDtypeStruct(tile, F32)] + [jax.ShapeDtypeStruct(packed, BF16)] * (kind == "near")
@@ -314,15 +309,15 @@
     )
 
 
-def final_body(diag, own, core, far, up_y, across, up_z, marked, result, out, sems):
+def final_body(diag, own, far, far_1, core, up_y, across, up_z, marked, result, out, sems):
     bands = out.shape[2]
     first, side, _ = position()
     first, low = first == 1, side == 0
     wide = lambda tile: unpack(tile.astype(F32))
     mine = own[...] + wide(core[...])
     middle = wide(across[...])
-    near1 = jnp.where(first, mine, far[1] + middle)
-    near2 = far[0] + wide(up_y[0])
+    near1 = jnp.where(first, mine, wide(far_1[...]) + middle)
+    near2 = wide(far[0]) + wide(up_y[0])
     away1 = jnp.where(first, middle + wide(up_z[0]), mine)
     away2 = wide(up_y[1]) + wide(up_z[1])
     above = [jnp.where(low, near1, away1), jnp.where(low, near2, away2)]
@@ -418,14 +413,14 @@
             got_y[i], sums, tile_own = tie(got_y[i], sums, tile_own)
             marked = mark(got_z[i], facts_y, facts_z)
             other, marked = tie(send(got_y[i], "core"), marked)
-            far, pairs_02, pairs_12, pair_1 = pair_sums(
+            pairs_02, pairs_12, pair_1 = pair_sums(
                 "far", k_plus_g, blocks(other), begin, size,
                 [[(facts_y, None, 0)], here, [(facts_z, None, 0)], [(facts_y, None, 1)]], sums,
             )
     tile_y = send(pairs_02, "y")
     tile_across = send(pair_1, "across")
     tile_z = send(pairs_12, "back")
-    return final(bands, diag, own, tile_own, far, tile_y, tile_across, tile_z, marked)
+    return final(bands, diag, own, pairs_02, pair_1, tile_own, tile_y, tile_across, tile_z, marked)
 
 
 def solution(mesh):

time: 82.2 us -> 82 us (level)
  no operation moved by 1% of the time
where the time goes in v9:
time: 82 us; the launch traced here: 81.5 us
  Pallas kernels  39.3 us (48%)
  waiting for transfers between devices  20.5 us (25%)
  starting transfers between devices  20.3 us (25%)
  other arithmetic  1.28 us (2%)
    pallas_call x5, Pallas kernels, pair_sums(): pl.pallas_call(functools.partial(pair_body, kind, begin, tiles, plans(blo...  29.3 us
    ppermute x17, waiting for transfers between devices, shards(): send = lambda value, name: lax.ppermute(value, 'blk', way[name])  20.5 us
    ppermute x17, starting transfers between devices, shards(): send = lambda value, name: lax.ppermute(value, 'blk', way[name])  20.3 us
    pallas_call x2, Pallas kernels, pieces(): pl.pallas_call(functools.partial(pieces_body, cuts), in_specs=[anywhere],...  5.04 us
    pallas_call x1, Pallas kernels, final(): pl.pallas_call(final_body, in_specs=[vmem] * len(operands), out_specs=pl....  2.93 us
  transfers between devices with their start and end apart: 17, of which 6 were waited for; matrix products, arithmetic and copies ran while one was open for 2% of the time, Pallas kernels for 35%

profile of v9, /device:TPU:0, one launch (start us, length us, event | category | flops | bytes accessed | tf_op | source)
XLA Modules:
  0.0 81.5 jit_solution(14809894838542007989)
XLA Ops:
  0.0 2.1 %one.1 = (bf16[2,96,1792]{2,1,0:T(8,128)(2,1)}, bf16[2,96,1792]{2,1,0:T(8,128)(2,1)}) custom-call(bf16[2,96,12544]{2,1,0:T(8,128)(2,1)} %refs_1_.3), custom_call_target="tpu_custom_call" | custom-call | flops 1000 | bytes 1000 | tf_op jit(solution)/shard_map/one/pallas_call | solution.py:296
  2.1 0.5 collective-permute-start
  2.7 2.6 %collective-permute-start.1 = (bf16[2,96,1792]{2,1,0:T(8,128)(2,1)}, bf16[2,96,1792]{2,1,0:T(8,128)(2,1)}, u32[]{:S(2)}, u32[]{:S(2)}) collective-permute-start(bf16[2,96,1792]{2,1,0:T(8,128)(2,1)} %get-tuple-element.47), channel_id=1, source_target_pairs={{0,2},{1,3},{2,0},{3,1},{4,6},{5,7},{6,4},{7,5},{8,10},{9,11},{10,... | collective-permute-start | bytes 2064392 | tf_op jit(solution)/shard_map/ppermute | solution.py:373
  5.3 1.3 %collective-permute-start.2 = (bf16[2,96,1792]{2,1,0:T(8,128)(2,1)}, bf16[2,96,1792]{2,1,0:T(8,128)(2,1)}, u32[]{:S(2)}, u32[]{:S(2)}) collective-permute-start(bf16[2,96,1792]{2,1,0:T(8,128)(2,1)} %get-tuple-element.48), channel_id=1, source_target_pairs={{4,0},{5,1},{8,4},{9,5},{2,6},{3,7},{12,8},{13,9},{6,10},{7,11},{1... | collective-permute-start | bytes 2064392 | tf_op jit(solution)/shard_map/ppermute | solution.py:373
  6.5 1.4 %facts.1.refs_1_.refs_3_.refs_5_ = bf16[16,128]{1,0:T(8,128)(2,1)} custom-call(s32[1,96]{1,0:T(1,128)} %bitcast.1, s32[1,2]{1,0:T(1,128)} %pairs.1), custom_call_target="tpu_custom_call" | custom-call | flops 1000 | bytes 1000 | tf_op jit(solution)/shard_map/facts/pallas_call | solution.py:260
  7.9 2.9 %rest.1 = (bf16[2,96,2176]{2,1,0:T(8,128)(2,1)}, bf16[2,96,2176]{2,1,0:T(8,128)(2,1)}, bf16[2,96,2304]{2,1,0:T(8,128)(2,1)}, bf16[2,96,2304]{2,1,0:T(8,128)(2,1)}) custom-call(bf16[2,96,12544]{2,1,0:T(8,128)(2,1)} %refs_1_.3), custom_call_target="tpu_custom_call" | custom-call | flops 1000 | bytes 1000 | tf_op jit(solution)/shard_map/rest/pallas_call | solution.py:296
  10.9 3.6 %collective-permute-start.5 = (bf16[2,96,2176]{2,1,0:T(8,128)(2,1)}, bf16[2,96,2176]{2,1,0:T(8,128)(2,1)}, u32[]{:S(2)}, u32[]{:S(2)}) collective-permute-start(bf16[2,96,2176]{2,1,0:T(8,128)(2,1)} %get-tuple-element.53), channel_id=1, source_target_pairs={{0,2},{1,3},{2,0},{3,1},{4,6},{5,7},{6,4},{7,5},{8,10},{9,11},{10,... | collective-permute-start | bytes 2506760 | tf_op jit(solution)/shard_map/ppermute | solution.py:373
  14.5 1.3 %collective-permute-start.6 = (bf16[2,96,2176]{2,1,0:T(8,128)(2,1)}, bf16[2,96,2176]{2,1,0:T(8,128)(2,1)}, u32[]{:S(2)}, u32[]{:S(2)}) collective-permute-start(bf16[2,96,2176]{2,1,0:T(8,128)(2,1)} %get-tuple-element.54), channel_id=1, source_target_pairs={{4,0},{5,1},{8,4},{9,5},{2,6},{3,7},{12,8},{13,9},{6,10},{7,11},{1... | collective-permute-start | bytes 2506760 | tf_op jit(solution)/shard_map/ppermute | solution.py:373
  15.8 0.0 collective-permute-done.refs_0_
  15.8 0.1 collective-permute-start.3
  15.9 7.2 %diag.1 = f32[288,192]{1,0:T(8,128)} custom-call(f32[3,12544]{1,0:T(4,128)} %k_hbm.9, bf16[2,96,12544]{2,1,0:T(8,128)(2,1)} %refs_1_.3, bf16[16,128]{1,0:T(8,128)(2,1)} %facts.1.refs_1_.refs_3_.refs_5_), custom_call_target="tpu_custom_call" | custom-call | flops 1000 | bytes 1000 | tf_op jit(solution)/shard_map/diag/pallas_call | solution.py:209
  23.1 0.0 collective-permute-done.3.refs_2_
  23.1 5.4 %near.1 = (f32[288,192]{1,0:T(8,128)}, bf16[432,128]{1,0:T(8,128)(2,1)}) custom-call(f32[3,12544]{1,0:T(4,128)} %k_hbm.9, bf16[2,96,12544]{2,1,0:T(8,128)(2,1)} %collective-permute-done.refs_0_, bf16[2,96,12544]{2,1,0:T(8,128)(2,1)} %refs_1_.3, bf16[16,128]{1,0:T(8,128)(2,1)} %collective-permute-done.3.refs_2_, bf16[16,128]{1,0:T(8,128)(2,1)} %facts.1.refs_1_.refs_3_.refs_5_), custom_call_target="tpu_custom_call" | custom-call | flops 1000 | bytes 1000 | tf_op jit(solution)/shard_map/near/pallas_call | solution.py:209
  28.5 0.0 collective-permute-done.1.refs_0_
  28.5 0.0 collective-permute-done.2.refs_2_
  28.5 0.6 collective-permute-start.7
  29.1 2.5 %collective-permute-start.4 = (bf16[2,96,2304]{2,1,0:T(8,128)(2,1)}, bf16[2,96,2304]{2,1,0:T(8,128)(2,1)}, u32[]{:S(2)}, u32[]{:S(2)}) collective-permute-start(bf16[2,96,2304]{2,1,0:T(8,128)(2,1)} %get-tuple-element.42), channel_id=1, source_target_pairs={{0,2},{1,3},{2,0},{3,1},{4,6},{5,7},{6,4},{7,5},{8,10},{9,11},{10,... | collective-permute-start | bytes 2654216 | tf_op jit(solution)/shard_map/ppermute | solution.py:373
  31.6 1.3 %collective-permute-start.10 = (bf16[2,96,2304]{2,1,0:T(8,128)(2,1)}, bf16[2,96,2304]{2,1,0:T(8,128)(2,1)}, u32[]{:S(2)}, u32[]{:S(2)}) collective-permute-start(bf16[2,96,2304]{2,1,0:T(8,128)(2,1)} %get-tuple-element.43), channel_id=1, source_target_pairs={{4,0},{5,1},{8,4},{9,5},{2,6},{3,7},{12,8},{13,9},{6,10},{7,11},{1... | collective-permute-start | bytes 2654216 | tf_op jit(solution)/shard_map/ppermute | solution.py:373
  32.9 0.0 collective-permute-done.7.refs_3_
  32.9 5.0 %far.3.refs_4_ = f32[3,288,192]{2,1,0:T(8,128)} custom-call(f32[3,12544]{1,0:T(4,128)} %k_hbm.9, bf16[2,96,1792]{2,1,0:T(8,128)(2,1)} %collective-permute-done.1.refs_0_, bf16[2,96,12544]{2,1,0:T(8,128)(2,1)} %refs_1_.3, bf16[2,96,1792]{2,1,0:T(8,128)(2,1)} %collective-permute-done.2.refs_2_, bf16[2,96,1792]{2,1,0:T(8,128)(2,1)} %collective-permute-done.7.refs_3_), custom_call_target="tpu_custom_call" | custom-call | flops 1000 | bytes 1000 | tf_op jit(solution)/shard_map/far/pallas_call | solution.py:209
  38.0 1.8 %collective-permute-done.5.refs_0_ = bf16[2,96,2176]{2,1,0:T(8,128)(2,1)} collective-permute-done((bf16[2,96,2176]{2,1,0:T(8,128)(2,1)}, bf16[2,96,2176]{2,1,0:T(8,128)(2,1)}, u32[]{:S(2)}, u32[]{:S(2)}) %collective-permute-start.5) | collective-permute-done | bytes 835616 | tf_op jit(solution)/shard_map/ppermute | solution.py:373
  39.8 3.9 %collective-permute-done.6.refs_2_ = bf16[2,96,2176]{2,1,0:T(8,128)(2,1)} collective-permute-done((bf16[2,96,2176]{2,1,0:T(8,128)(2,1)}, bf16[2,96,2176]{2,1,0:T(8,128)(2,1)}, u32[]{:S(2)}, u32[]{:S(2)}) %collective-permute-start.6) | collective-permute-done | bytes 835616 | tf_op jit(solution)/shard_map/ppermute | solution.py:373
  43.6 0.0 collective-permute-start.8
  43.6 0.5 collective-permute-start.9
  44.2 1.3 %pad_maximum_fusion = bf16[32,128]{1,0:T(8,128)(2,1)} fusion(bf16[16,128]{1,0:T(8,128)(2,1)} %collective-permute-done.3.refs_2_, bf16[16,128]{1,0:T(8,128)(2,1)} %facts.1.refs_1_.refs_3_.refs_5_), kind=kLoop, calls=%fused_computation | loop fusion | flops 16384 | bytes 16384 | tf_op jit(solution)/shard_map/concatenate | solution.py:384
  45.4 0.0 collective-permute-start.12
  45.4 0.9 %collective-permute-done.8.refs_3_ = bf16[2,96,2176]{2,1,0:T(8,128)(2,1)} collective-permute-done((bf16[2,96,2176]{2,1,0:T(8,128)(2,1)}, bf16[2,96,2176]{2,1,0:T(8,128)(2,1)}, u32[]{:S(2)}, u32[]{:S(2)}) %collective-permute-start.8) | collective-permute-done | bytes 835616 | tf_op jit(solution)/shard_map/ppermute | solution.py:373
  46.3 1.3 %collective-permute-start.13 = (bf16[16,128]{1,0:T(8,128)(2,1)}, bf16[16,128]{1,0:T(8,128)(2,1)}, u32[]{:S(2)}, u32[]{:S(2)}) collective-permute-start(bf16[16,128]{1,0:T(8,128)(2,1)} %facts.1.refs_1_.refs_3_.refs_5_), channel_id=1, source_target_pairs={{4,0},{5,1},{8,4},{9,5},{2,6},{3,7},{12,8},{13,9},{6,10},{7,11},{1... | collective-permute-start | bytes 12296 | tf_op jit(solution)/shard_map/ppermute | solution.py:373
  47.6 5.8 %far.4.refs_8_ = f32[3,288,192]{2,1,0:T(8,128)} custom-call(f32[3,12544]{1,0:T(4,128)} %k_hbm.9, bf16[2,96,2176]{2,1,0:T(8,128)(2,1)} %collective-permute-done.5.refs_0_, bf16[2,96,12544]{2,1,0:T(8,128)(2,1)} %refs_1_.3, bf16[2,96,2176]{2,1,0:T(8,128)(2,1)} %collective-permute-done.6.refs_2_, bf16[2,96,2176]{2,1,0:T(8,128)(2,1)} %collective-permute-done.8.refs_3_, ...), custom_call_target="tpu_custom_call" | custom-call | flops 1000 | bytes 1000 | tf_op jit(solution)/shard_map/far/pallas_call | solution.py:209
  53.4 5.1 %collective-permute-done.4.refs_0_ = bf16[2,96,2304]{2,1,0:T(8,128)(2,1)} collective-permute-done((bf16[2,96,2304]{2,1,0:T(8,128)(2,1)}, bf16[2,96,2304]{2,1,0:T(8,128)(2,1)}, u32[]{:S(2)}, u32[]{:S(2)}) %collective-permute-start.4) | collective-permute-done | bytes 884768 | tf_op jit(solution)/shard_map/ppermute | solution.py:373
  58.5 0.0 collective-permute-done.9.core
  58.6 0.0 collective-permute-start.11
  58.6 3.4 %collective-permute-done.13.refs_2_.refs_6_ = bf16[16,128]{1,0:T(8,128)(2,1)} collective-permute-done((bf16[16,128]{1,0:T(8,128)(2,1)}, bf16[16,128]{1,0:T(8,128)(2,1)}, u32[]{:S(2)}, u32[]{:S(2)}) %collective-permute-start.13) | collective-permute-done | bytes 4128 | tf_op jit(solution)/shard_map/ppermute | solution.py:373
  61.9 0.0 collective-permute-done.12.refs_1_.refs_4_.refs_7_
  61.9 0.0 collective-permute-done.10.refs_0_.refs_2_
  61.9 0.6 mark.1.marked
  62.5 0.0 collective-permute-done.11.refs_3_
  62.5 5.8 %far.5 = (bf16[2,432,128]{2,1,0:T(8,128)(2,1)}, bf16[2,432,128]{2,1,0:T(8,128)(2,1)}, bf16[432,128]{1,0:T(8,128)(2,1)}) custom-call(f32[3,12544]{1,0:T(4,128)} %k_hbm.9, bf16[2,96,2304]{2,1,0:T(8,128)(2,1)} %collective-permute-done.4.refs_0_, bf16[2,96,12544]{2,1,0:T(8,128)(2,1)} %refs_1_.3, bf16[2,96,2304]{2,1,0:T(8,128)(2,1)} %collective-permute-done.10.refs_0_.refs_2_, ...), custom_call_target="tpu_custom_call" | custom-call | flops 1000 | bytes 1000 | tf_op jit(solution)/shard_map/far/pallas_call | solution.py:209
  68.4 0.6 collective-permute-start.14
  69.0 4.2 %collective-permute-start.16 = (bf16[2,432,128]{2,1,0:T(8,128)(2,1)}, bf16[2,432,128]{2,1,0:T(8,128)(2,1)}, u32[]{:S(2)}, u32[]{:S(2)}) collective-permute-start(bf16[2,432,128]{2,1,0:T(8,128)(2,1)} %get-tuple-element.67), channel_id=1, source_target_pairs={{0,4},{1,5},{4,8},{5,9},{6,2},{7,3},{8,12},{9,13},{10,6},{11,7},{1... | collective-permute-start | bytes 663560 | tf_op jit(solution)/shard_map/ppermute | solution.py:373
  73.2 0.0 collective-permute-start.15
  73.2 5.4 %collective-permute-done.15.across = bf16[432,128]{1,0:T(8,128)(2,1)} collective-permute-done((bf16[432,128]{1,0:T(8,128)(2,1)}, bf16[432,128]{1,0:T(8,128)(2,1)}, u32[]{:S(2)}, u32[]{:S(2)}) %collective-permute-start.15) | collective-permute-done | bytes 110624 | tf_op jit(solution)/shard_map/ppermute | solution.py:373
  78.6 0.0 collective-permute-done.14.up_y
  78.6 0.0 collective-permute-done.16.up_z
  78.6 2.9 %final.1 = f32[3,2,96,480]{3,2,1,0:T(8,128)} custom-call(f32[288,192]{1,0:T(8,128)} %diag.1, f32[288,192]{1,0:T(8,128)} %get-tuple-element.52.own, bf16[2,432,128]{2,1,0:T(8,128)(2,1)} %get-tuple-element.64.far, bf16[432,128]{1,0:T(8,128)(2,1)} %get-tuple-element.65.far_1, bf16[432,128]{1,0:T(8,128)(2,1)} %collective-permute-done.9.core, ...), custom_call_target="tpu_custom_call" | custom-call | tf_op jit(solution)/shard_map/final/pallas_call | solution.py:342
Async XLA Ops:
  2.1 13.6 %collective-permute-start = (bf16[2,96,12544]{2,1,0:T(8,128)(2,1)}, bf16[2,96,12544]{2,1,0:T(8,128)(2,1)}, u32[]{:S(2)}, u32[]{:S(2)}) collective-permute-start(bf16[2,96,12544]{2,1,0:T(8,128)(2,1)} %refs_1_.3), channel_id=1, source_target_pairs={{0,1},{1,0},{2,3},{3,2},{4,5},{5,4},{6,7},{7,6},{8,9},{9,8},{10,11... | collective-permute-start | bytes 14450696 | tf_op jit(solution)/shard_map/ppermute | solution.py:373
  2.7 25.9 %collective-permute-start.1 = (bf16[2,96,1792]{2,1,0:T(8,128)(2,1)}, bf16[2,96,1792]{2,1,0:T(8,128)(2,1)}, u32[]{:S(2)}, u32[]{:S(2)}) collective-permute-start(bf16[2,96,1792]{2,1,0:T(8,128)(2,1)} %get-tuple-element.47), channel_id=1, source_target_pairs={{0,2},{1,3},{2,0},{3,1},{4,6},{5,7},{6,4},{7,5},{8,10},{9,11},{10,... | collective-permute-start | bytes 2064392 | tf_op jit(solution)/shard_map/ppermute | solution.py:373
  5.3 23.3 %collective-permute-start.2 = (bf16[2,96,1792]{2,1,0:T(8,128)(2,1)}, bf16[2,96,1792]{2,1,0:T(8,128)(2,1)}, u32[]{:S(2)}, u32[]{:S(2)}) collective-permute-start(bf16[2,96,1792]{2,1,0:T(8,128)(2,1)} %get-tuple-element.48), channel_id=1, source_target_pairs={{4,0},{5,1},{8,4},{9,5},{2,6},{3,7},{12,8},{13,9},{6,10},{7,11},{1... | collective-permute-start | bytes 2064392 | tf_op jit(solution)/shard_map/ppermute | solution.py:373
  10.9 28.9 %collective-permute-start.5 = (bf16[2,96,2176]{2,1,0:T(8,128)(2,1)}, bf16[2,96,2176]{2,1,0:T(8,128)(2,1)}, u32[]{:S(2)}, u32[]{:S(2)}) collective-permute-start(bf16[2,96,2176]{2,1,0:T(8,128)(2,1)} %get-tuple-element.53), channel_id=1, source_target_pairs={{0,2},{1,3},{2,0},{3,1},{4,6},{5,7},{6,4},{7,5},{8,10},{9,11},{10,... | collective-permute-start | bytes 2506760 | tf_op jit(solution)/shard_map/ppermute | solution.py:373
  14.5 29.2 %collective-permute-start.6 = (bf16[2,96,2176]{2,1,0:T(8,128)(2,1)}, bf16[2,96,2176]{2,1,0:T(8,128)(2,1)}, u32[]{:S(2)}, u32[]{:S(2)}) collective-permute-start(bf16[2,96,2176]{2,1,0:T(8,128)(2,1)} %get-tuple-element.54), channel_id=1, source_target_pairs={{4,0},{5,1},{8,4},{9,5},{2,6},{3,7},{12,8},{13,9},{6,10},{7,11},{1... | collective-permute-start | bytes 2506760 | tf_op jit(solution)/shard_map/ppermute | solution.py:373
  15.8 7.3 %collective-permute-start.3 = (bf16[16,128]{1,0:T(8,128)(2,1)}, bf16[16,128]{1,0:T(8,128)(2,1)}, u32[]{:S(2)}, u32[]{:S(2)}) collective-permute-start(bf16[16,128]{1,0:T(8,128)(2,1)} %facts.1.refs_1_.refs_3_.refs_5_), channel_id=1, source_target_pairs={{0,1},{1,0},{2,3},{3,2},{4,5},{5,4},{6,7},{7,6},{8,9},{9,8},{10,11... | collective-permute-start | bytes 12296 | tf_op jit(solution)/shard_map/ppermute | solution.py:373
  28.5 4.4 %collective-permute-start.7 = (bf16[2,96,1792]{2,1,0:T(8,128)(2,1)}, bf16[2,96,1792]{2,1,0:T(8,128)(2,1)}, u32[]{:S(2)}, u32[]{:S(2)}) collective-permute-start(bf16[2,96,1792]{2,1,0:T(8,128)(2,1)} %collective-permute-done.1.refs_0_), channel_id=1, source_target_pairs={{0,1},{1,0},{2,3},{3,2},{4,5},{5,4},{6,7},{7,6},{8,9},{9,8},{10,11... | collective-permute-start | bytes 2064392 | tf_op jit(solution)/shard_map/ppermute | solution.py:373
  29.1 29.5 %collective-permute-start.4 = (bf16[2,96,2304]{2,1,0:T(8,128)(2,1)}, bf16[2,96,2304]{2,1,0:T(8,128)(2,1)}, u32[]{:S(2)}, u32[]{:S(2)}) collective-permute-start(bf16[2,96,2304]{2,1,0:T(8,128)(2,1)} %get-tuple-element.42), channel_id=1, source_target_pairs={{0,2},{1,3},{2,0},{3,1},{4,6},{5,7},{6,4},{7,5},{8,10},{9,11},{10,... | collective-permute-start | bytes 2654216 | tf_op jit(solution)/shard_map/ppermute | solution.py:373
  31.6 30.3 %collective-permute-start.10 = (bf16[2,96,2304]{2,1,0:T(8,128)(2,1)}, bf16[2,96,2304]{2,1,0:T(8,128)(2,1)}, u32[]{:S(2)}, u32[]{:S(2)}) collective-permute-start(bf16[2,96,2304]{2,1,0:T(8,128)(2,1)} %get-tuple-element.43), channel_id=1, source_target_pairs={{4,0},{5,1},{8,4},{9,5},{2,6},{3,7},{12,8},{13,9},{6,10},{7,11},{1... | collective-permute-start | bytes 2654216 | tf_op jit(solution)/shard_map/ppermute | solution.py:373
  43.6 2.7 %collective-permute-start.8 = (bf16[2,96,2176]{2,1,0:T(8,128)(2,1)}, bf16[2,96,2176]{2,1,0:T(8,128)(2,1)}, u32[]{:S(2)}, u32[]{:S(2)}) collective-permute-start(bf16[2,96,2176]{2,1,0:T(8,128)(2,1)} %collective-permute-done.5.refs_0_), channel_id=1, source_target_pairs={{0,1},{1,0},{2,3},{3,2},{4,5},{5,4},{6,7},{7,6},{8,9},{9,8},{10,11... | collective-permute-start | bytes 2506760 | tf_op jit(solution)/shard_map/ppermute | solution.py:373
  43.6 14.9 %collective-permute-start.9 = (bf16[432,128]{1,0:T(8,128)(2,1)}, bf16[432,128]{1,0:T(8,128)(2,1)}, u32[]{:S(2)}, u32[]{:S(2)}) collective-permute-start(bf16[432,128]{1,0:T(8,128)(2,1)} %get-tuple-element.60), channel_id=1, source_target_pairs={{0,1},{1,0},{2,3},{3,2},{4,5},{5,4},{6,7},{7,6},{8,9},{9,8},{10,11... | collective-permute-start | bytes 331784 | tf_op jit(solution)/shard_map/ppermute | solution.py:373
  45.4 16.5 %collective-permute-start.12 = (bf16[32,128]{1,0:T(8,128)(2,1)}, bf16[32,128]{1,0:T(8,128)(2,1)}, u32[]{:S(2)}, u32[]{:S(2)}) collective-permute-start(bf16[32,128]{1,0:T(8,128)(2,1)} %pad_maximum_fusion), channel_id=1, source_target_pairs={{0,2},{1,3},{2,0},{3,1},{4,6},{5,7},{6,4},{7,5},{8,10},{9,11},{10,... | collective-permute-start | bytes 24584 | tf_op jit(solution)/shard_map/ppermute | solution.py:373
  46.3 15.6 %collective-permute-start.13 = (bf16[16,128]{1,0:T(8,128)(2,1)}, bf16[16,128]{1,0:T(8,128)(2,1)}, u32[]{:S(2)}, u32[]{:S(2)}) collective-permute-start(bf16[16,128]{1,0:T(8,128)(2,1)} %facts.1.refs_1_.refs_3_.refs_5_), channel_id=1, source_target_pairs={{4,0},{5,1},{8,4},{9,5},{2,6},{3,7},{12,8},{13,9},{6,10},{7,11},{1... | collective-permute-start | bytes 12296 | tf_op jit(solution)/shard_map/ppermute | solution.py:373
  58.6 4.0 %collective-permute-start.11 = (bf16[2,96,2304]{2,1,0:T(8,128)(2,1)}, bf16[2,96,2304]{2,1,0:T(8,128)(2,1)}, u32[]{:S(2)}, u32[]{:S(2)}) collective-permute-start(bf16[2,96,2304]{2,1,0:T(8,128)(2,1)} %collective-permute-done.4.refs_0_), channel_id=1, source_target_pairs={{0,1},{1,0},{2,3},{3,2},{4,5},{5,4},{6,7},{7,6},{8,9},{9,8},{10,11... | collective-permute-start | bytes 2654216 | tf_op jit(solution)/shard_map/ppermute | solution.py:373
  68.4 10.2 %collective-permute-start.14 = (bf16[2,432,128]{2,1,0:T(8,128)(2,1)}, bf16[2,432,128]{2,1,0:T(8,128)(2,1)}, u32[]{:S(2)}, u32[]{:S(2)}) collective-permute-start(bf16[2,432,128]{2,1,0:T(8,128)(2,1)} %get-tuple-element.64.far), channel_id=1, source_target_pairs={{0,2},{1,3},{2,0},{3,1},{4,6},{5,7},{6,4},{7,5},{8,10},{9,11},{10,... | collective-permute-start | bytes 663560 | tf_op jit(solution)/shard_map/ppermute | solution.py:373
  69.0 9.6 %collective-permute-start.16 = (bf16[2,432,128]{2,1,0:T(8,128)(2,1)}, bf16[2,432,128]{2,1,0:T(8,128)(2,1)}, u32[]{:S(2)}, u32[]{:S(2)}) collective-permute-start(bf16[2,432,128]{2,1,0:T(8,128)(2,1)} %get-tuple-element.67), channel_id=1, source_target_pairs={{0,4},{1,5},{4,8},{5,9},{6,2},{7,3},{8,12},{9,13},{10,6},{11,7},{1... | collective-permute-start | bytes 663560 | tf_op jit(solution)/shard_map/ppermute | solution.py:373
  73.2 5.4 %collective-permute-start.15 = (bf16[432,128]{1,0:T(8,128)(2,1)}, bf16[432,128]{1,0:T(8,128)(2,1)}, u32[]{:S(2)}, u32[]{:S(2)}) collective-permute-start(bf16[432,128]{1,0:T(8,128)(2,1)} %get-tuple-element.65.far_1), channel_id=1, source_target_pairs={{0,3},{1,2},{2,1},{3,0},{4,7},{5,6},{6,5},{7,4},{8,11},{9,10},{10,... | collective-permute-start | bytes 331784 | tf_op jit(solution)/shard_map/ppermute | solution.py:373
